TPU v7x, 32 devices: a whole 2x2x4 slice. The times are simulated.
32 devices in a mesh: shard: 4 (over x, core), heads: 4 (over z), tensor: 2 (over y).
Axes of the slice: x: 2, y: 2, z: 4, core: 2. Of those that a mesh axis runs over, the one named last changes fastest.
Arguments:
- tokens: bfloat16 [64, 197, 768], P(('shard', 'tensor')), may hold values from -6 to 6
- norm_scales: bfloat16 [2, 768], P(None, ('shard', 'tensor')), may hold values from 0.5 to 1.5
- norm_biases: bfloat16 [2, 768], P(None, ('shard', 'tensor')), may hold values from -0.59765625 to 0.59765625
- w_attn: bfloat16 [4, 768, 768], P(None, ('shard', 'tensor'), 'heads'), may hold values from -0.3125 to 0.3125
- phi: bfloat16 [768, 64], P(('shard', 'tensor'), 'heads'), may hold values from -0.109375 to 0.109375
- experts: bfloat16 [768, 2, 64, 3072], P('shard', None, 'heads', 'tensor'), may hold values from -2 to 2
- in_bias: bfloat16 [64, 3072], P('heads', ('shard', 'tensor')), may hold values from -0.59765625 to 0.59765625
- out_bias: bfloat16 [64, 768], P('heads', ('shard', 'tensor')), may hold values from -4.78125 to 4.78125
- cotangent: bfloat16 [64, 197, 768], P(('shard', 'tensor')), may hold values from -6 to 6
Outputs:
- output: bfloat16 [64, 197, 768], P(('shard', 'tensor'))
- input_grad: bfloat16 [64, 197, 768], P(('shard', 'tensor'))
- scales_grad: float32 [2, 768], P(None, ('shard', 'tensor'))
- biases_grad: float32 [2, 768], P(None, ('shard', 'tensor'))
- attn_grad: float32 [4, 768, 768], P(None, ('shard', 'tensor'), 'heads')
- phi_grad: float32 [768, 64], P(('shard', 'tensor'), 'heads')
- experts_grad: float32 [768, 2, 64, 3072], P('shard', None, 'heads', 'tensor')
- in_bias_grad: float32 [64, 3072], P('heads', ('shard', 'tensor'))
- out_bias_grad: float32 [64, 768], P('heads', ('shard', 'tensor'))
All inputs are finite; a program needn't handle non-finite values.
Results may differ from a plain program's by a relative error of at most 0.019.
Values may be sent and summed in bfloat16 or wider, within the bound.
A program may use at most 576 MiB of HBM per device.

v0:
```python
from functools import partial

import jax
import jax.numpy as jnp
from jax import lax
from jax.experimental import pallas as pl
from jax.experimental.pallas import tpu as pltpu
from jax.sharding import PartitionSpec as P

HEAD_DIM = 64
F32 = jnp.float32
BF16 = jnp.bfloat16
ROWS = ("shard", "tensor")
MESH = pl.DeviceIdType.MESH
VMEM_BYTES = 58 * 1024 * 1024
epsilon = 1e-06
einsum = partial(jnp.einsum, preferred_element_type=F32)


def dot(a, b):
    return lax.dot_general(a, b, (((1,), (0,)), ((), ())), preferred_element_type=F32)


def dot_t(a, b):
    return lax.dot_general(a, b, (((1,), (1,)), ((), ())), preferred_element_type=F32)


def swap_matrix(n):
    out = lax.broadcasted_iota(jnp.int32, (n * n, n * n), 0)
    row = lax.broadcasted_iota(jnp.int32, (n * n, n * n), 1)
    return ((out // n == row % n) & (out % n == row // n)).astype(F32).astype(BF16)


class Peers:
    def __init__(self, sizes):
        self.sizes = sizes
        self.at = tuple(lax.axis_index(name) for name in ("shard", "heads", "tensor"))
        self.count = sizes[0] * sizes[1] * sizes[2]

    def flat(self, place):
        return (place[0] * self.sizes[1] + place[1]) * self.sizes[2] + place[2]

    def step(self, k, sign):
        _, n_h, n_t = self.sizes
        steps = (k // (n_h * n_t), (k // n_t) % n_h, k % n_t)
        return tuple(
            lax.rem(at + n + sign * d, n) for at, n, d in zip(self.at, self.sizes, steps)
        )

    def greet_all(self):
        barrier = pltpu.get_barrier_semaphore()

        def signal(k, carry):
            pl.semaphore_signal(barrier, inc=1, device_id=self.step(k, 1), device_id_type=MESH)
            return carry

        lax.fori_loop(1, self.count, signal, 0)
        pl.semaphore_wait(barrier, self.count - 1)


def remote(src, dst, send, recv, place):
    return pltpu.make_async_remote_copy(
        src_ref=src, dst_ref=dst, send_sem=send, recv_sem=recv, device_id=place, device_id_type=MESH
    )


def plane(sizes):
    n_s, n_h, n_t = sizes
    s, h, t = (lax.axis_index(name) for name in ("shard", "heads", "tensor"))
    core, chip = lax.rem(s, 2), s // 2
    sibling = (s + 1 - 2 * core, h, t)
    across_x = (lax.rem(s + 2, n_s), h, t)
    across_y = (s, h, 1 - t)
    line = [(s, lax.rem(h + d, n_h), t) for d in range(n_h)]
    barrier = pltpu.get_barrier_semaphore()
    others = [sibling, across_x, across_y] + line[1:]
    for place in others:
        pl.semaphore_signal(barrier, inc=1, device_id=place, device_id_type=MESH)
    pl.semaphore_wait(barrier, len(others))
    return (s, h, t), core, chip, sibling, across_x, across_y, line


def pair_matrix(block, wide, transposed):
    shape = (2 * block, 2 * wide) if transposed else (2 * wide, 2 * block)
    tight = lax.broadcasted_iota(jnp.int32, shape, 0 if transposed else 1)
    padded = lax.broadcasted_iota(jnp.int32, shape, 1 if transposed else 0)
    second = padded >= wide
    lane = jnp.where(second, padded - wide, padded)
    same = (lane < block) & (tight == jnp.where(second, lane + block, lane))
    return same.astype(F32).astype(BF16)


def gather_kernel(
    sizes, packet, extra, experts, w_out, small_out, turned,
    w, small, lined, tile_in, tile_out,
    z_send, z_recv, x_sems, y_sems, d_sems, c_sems, t_sems, o_sems,
):
    (s, h, t), core, chip, sibling, across_x, across_y, line = plane(sizes)
    n_k, rows, wide = packet.shape
    n_h, n_t = sizes[1], sizes[2]
    width = w.shape[2]
    block = width // n_h
    side = 16
    n_tiles = experts.shape[0] // side
    halves = ((0, rows // 2), (rows // 2, rows // 2))

    def z_hop(k, origin, up):
        place = line[1] if up else line[n_h - 1]
        return remote(
            lined.at[origin, k], lined.at[origin, k],
            z_send.at[k, origin, up], z_recv.at[k, origin], place,
        )

    def relay(k, d):
        @pl.when(h >= d)
        def _():
            z_hop(k, h - d, 1).wait_recv()

            @pl.when(h < n_h - 1)
            def _():
                z_hop(k, h - d, 1).start()

        @pl.when(h + d < n_h)
        def _():
            z_hop(k, h + d, 0).wait_recv()

            @pl.when(h > 0)
            def _():
                z_hop(k, h + d, 0).start()

    chunks = (0, 2, 1, 3)
    lined[h] = packet[...]
    for k in chunks:
        @pl.when(h < n_h - 1)
        def _():
            z_hop(k, h, 1).start()

        @pl.when(h > 0)
        def _():
            z_hop(k, h, 0).start()

    def load(i):
        return pltpu.make_async_copy(
            experts.at[pl.ds((i % n_tiles) * side, side), i // n_tiles],
            tile_in.at[i % 2],
            t_sems.at[0, i % 2],
        )

    def store(i):
        return pltpu.make_async_copy(
            tile_out.at[i % 2],
            turned.at[i // n_tiles, :, pl.ds((i % n_tiles) * side, side)],
            t_sems.at[1, i % 2],
        )

    load(0).start()
    swap = swap_matrix(side)
    done = [0]

    def turn(count):
        def step(i, carry):
            load(i).wait()

            @pl.when(i + 1 < 2 * n_tiles)
            def _():
                load(i + 1).start()

            @pl.when(i >= 2)
            def _():
                store(i - 2).wait()

            rows_in = tile_in[i % 2].reshape(side * side, tile_in.shape[3])
            tile_out[i % 2] = dot(swap, rows_in).astype(BF16).reshape(tile_out.shape[1:])
            store(i).start()
            return carry

        last = min(done[0] + count, 2 * n_tiles)
        lax.fori_loop(done[0], last, step, 0)
        done[0] = last

    pair = pair_matrix(block, wide, False)
    shape = (n_h * wide, small.shape[1])
    row = lax.broadcasted_iota(jnp.int32, shape, 0)
    column = lax.broadcasted_iota(jnp.int32, shape, 1)
    lane, of = row % wide - block, row // wide
    beside = (lane >= 0) & (lane < 16) & (column == of * 16 + lane)
    beside |= (lane >= 16) & (lane < 32) & (column == n_h * 16 + of * 16 + lane - 16)
    beside = beside.astype(F32).astype(BF16)

    def at(k, place):
        first = pl.multiple_of((place[0] * n_t + place[2]) * rows, 16)
        lines = pl.ds(first, rows)
        return small.at[lines] if k == n_k else w.at[k, lines]

    def hop(q, origin, place, sems, j):
        return remote(at(q, origin), at(q, origin), sems.at[0, j], sems.at[1, j], place)

    def half_hop(q, origin, place, half):
        part = at(q, origin).at[pl.ds(*halves[half])]
        j = 2 * q + half
        return remote(part, part, d_sems.at[0, j], d_sems.at[1, j], place)

    me = (s, h, t)
    from_d = (across_x[0], h, across_y[2])
    sent = []

    def send(copy):
        copy.start()
        sent.append(copy)

    def assemble(k):
        for i in range(0, n_h, 2):
            lines = jnp.concatenate([lined[i, k], lined[i + 1, k]], axis=1)
            at(k, me)[:, i * block : (i + 2) * block] = dot(lines, pair).astype(BF16)
        if k == 0:
            lines = jnp.concatenate([lined[i, k] for i in range(n_h)], axis=1)
            at(n_k, me)[...] = (dot(lines, beside) + extra[...].astype(F32)).astype(BF16)
        for q in members(k):
            send(hop(q, me, across_x, x_sems, q))
            send(hop(q, me, across_y, y_sems, q))
            send(hop(q, me, sibling, c_sems, 4 * q))

    def members(k):
        return (0, n_k) if k == 0 else (k,)

    def relay_xy(k):
        for q in members(k):
            hop(q, across_x, across_x, x_sems, q).wait_recv()
            send(half_hop(q, across_x, across_y, 0))
            send(hop(q, across_x, sibling, c_sems, 4 * q + 1))
            hop(q, across_y, across_y, y_sems, q).wait_recv()
            send(half_hop(q, across_y, across_x, 1))
            send(hop(q, across_y, sibling, c_sems, 4 * q + 2))

    def relay_d(k):
        for q in members(k):
            half_hop(q, from_d, across_y, 0).wait_recv()
            half_hop(q, from_d, across_x, 1).wait_recv()
            send(hop(q, from_d, sibling, c_sems, 4 * q + 3))

    for wave in range(n_k + n_h - 2):
        for d in range(1, n_h):
            if 0 <= wave - d + 1 < n_k:
                relay(chunks[wave - d + 1], d)
        turn(2)
        i = wave - n_h + 2
        if i >= 0:
            assemble(chunks[i])
            if i >= 1:
                relay_xy(chunks[i - 1])
            if i >= 2:
                relay_d(chunks[i - 2])
            turn(2)
    relay_xy(chunks[-1])
    relay_d(chunks[-2])
    turn(2 * n_tiles)
    relay_d(chunks[-1])
    stores = []
    for k in chunks:
        for q in members(k):
            for j in range(4):
                hop(q, me, sibling, c_sems, 4 * q + j).wait_recv()
            if q == n_k:
                stores.append(pltpu.make_async_copy(small, small_out, o_sems.at[q]))
            else:
                stores.append(pltpu.make_async_copy(w.at[q], w_out.at[q], o_sems.at[q]))
            stores[-1].start()
    for copy in sent:
        copy.wait_send()
    for origin in range(n_h):
        @pl.when((origin <= h) & (h < n_h - 1))
        def _():
            for k in range(n_k):
                z_hop(k, origin, 1).wait_send()

        @pl.when((origin >= h) & (h > 0))
        def _():
            for k in range(n_k):
                z_hop(k, origin, 0).wait_send()

    store(2 * n_tiles - 2).wait()
    store(2 * n_tiles - 1).wait()
    for copy in stores:
        copy.wait()


def gather_weights(sizes, packet, extra, experts):
    n_k, rows, wide = packet.shape
    n_s, n_h, n_t = sizes
    width = n_s * n_t * rows
    vmem = pl.BlockSpec(memory_space=pltpu.VMEM)
    hbm = pl.BlockSpec(memory_space=pl.ANY)
    dma = pltpu.SemaphoreType.DMA
    hidden = experts.shape[3]
    small = (width, extra.shape[1])
    return pl.pallas_call(
        partial(gather_kernel, sizes),
        out_shape=(
            jax.ShapeDtypeStruct((n_k, width, width), BF16),
            jax.ShapeDtypeStruct(small, BF16),
            jax.ShapeDtypeStruct((2, experts.shape[2], experts.shape[0], hidden), BF16),
        ),
        in_specs=[vmem, vmem, hbm],
        out_specs=(hbm, hbm, hbm),
        scratch_shapes=[
            pltpu.VMEM((n_k, width, width), BF16),
            pltpu.VMEM(small, BF16),
            pltpu.VMEM((n_h, n_k, rows, wide), BF16),
            pltpu.VMEM((2, 16, 16, hidden), BF16),
            pltpu.VMEM((2, 16, 16, hidden), BF16),
            dma((n_k, n_h, 2)), dma((n_k, n_h)), dma((2, n_k + 1)), dma((2, n_k + 1)),
            dma((2, 2 * (n_k + 1))), dma((2, 4 * (n_k + 1))), dma((2, 2)), dma((n_k + 1,)),
        ],
        compiler_params=pltpu.CompilerParams(
            collective_id=3, has_side_effects=True, vmem_limit_bytes=VMEM_BYTES
        ),
        name="gather_weights",
    )(packet, extra, experts)


def reduce_kernel(
    sizes, grads, small, out, core_in, core_small, met, met_small,
    d_in, d_small, x_in, x_small, y_in, y_small, pieces, z_in,
    c_sems, d_sems, x_sems, y_sems, z_sems,
):
    (s, h, t), core, chip, sibling, across_x, across_y, line = plane(sizes)
    n_k, width, _ = grads.shape
    n_s, n_h, n_t = sizes
    rows = width // (n_s * n_t)
    wide = pieces.shape[3]
    pair = n_t * rows
    half = rows // 2
    halves = (pl.ds(0, half), pl.ds(half, half))
    chunks = (0, 2, 1, 3)

    def members(k):
        return (0, n_k) if k == 0 else (k,)

    def pick(q, large, little):
        return little if q == n_k else large.at[q]

    def core_copy(q, x):
        first = pl.multiple_of((2 * x + 1 - core) * pair, 16)
        return remote(
            pick(q, grads, small).at[pl.ds(first, pair)],
            pick(q, core_in, core_small).at[x],
            c_sems.at[0, 2 * q + x], c_sems.at[1, 2 * q + x], sibling,
        )

    for k in chunks:
        for q in members(k):
            for x in range(2):
                core_copy(q, x).start()
    joined = pair_matrix(width // n_h, wide, True)
    shape = (small.shape[1], n_h * wide)
    row = lax.broadcasted_iota(jnp.int32, shape, 0)
    column = lax.broadcasted_iota(jnp.int32, shape, 1)
    lane, of = column % wide - width // n_h, column // wide
    beside = (lane >= 0) & (lane < 16) & (row == of * 16 + lane)
    beside |= (lane >= 16) & (lane < 20) & (row == n_h * 16 + lane - 16)
    beside = beside.astype(F32).astype(BF16)
    to_d, to_x, to_y = (d_in, d_small), (x_in, x_small), (y_in, y_small)
    sent = []

    def hop(q, kind, part, source, place):
        sems = {id(to_d): d_sems, id(to_x): x_sems, id(to_y): y_sems}[id(kind)]
        target = pick(q, *kind)
        target = target.at[part] if kind is to_d else target.at[halves[part]]
        j = 2 * q + part
        return remote(source, target, sems.at[0, j], sems.at[1, j], place)

    def send(copy):
        copy.start()
        sent.append(copy)

    def part_of(q, x, y, part):
        return pick(q, met, met_small).at[x, y].at[halves[part]]

    def arrived(q, kind, part):
        hop(q, kind, part, part_of(q, 0, 0, part), sibling).wait_recv()

    def open_up(q):
        part = pick(q, met, met_small)
        for x in range(2):
            core_copy(q, x).wait_recv()
            first = pl.multiple_of((2 * x + core) * pair, 16)
            own = pick(q, grads, small)[pl.ds(first, pair)].astype(F32)
            total = own + pick(q, core_in, core_small)[x].astype(F32)
            part[x] = total.astype(BF16).reshape(n_t, rows, total.shape[1])
        send(hop(q, to_d, 0, part_of(q, 1 - chip, 1 - t, 0), across_x))
        send(hop(q, to_d, 1, part_of(q, 1 - chip, 1 - t, 1), across_y))
        send(hop(q, to_x, 0, part_of(q, 1 - chip, t, 0), across_x))
        send(hop(q, to_y, 1, part_of(q, chip, 1 - t, 1), across_y))

    def pass_on(q):
        for part, kind, x, y, place in (
            (0, to_y, chip, 1 - t, across_y),
            (1, to_x, 1 - chip, t, across_x),
        ):
            arrived(q, to_d, part)
            block = part_of(q, x, y, part)
            total = block[...].astype(F32) + pick(q, *to_d)[part].astype(F32)
            block[...] = total.astype(BF16)
            send(hop(q, kind, part, block, place))

    def whole(q):
        for kind in (to_x, to_y):
            for part in range(2):
                arrived(q, kind, part)
        total = pick(q, met, met_small)[chip, t].astype(F32) + pick(q, *to_x)[...].astype(F32)
        return (total + pick(q, *to_y)[...].astype(F32)).astype(BF16)

    def z_copy(k, d):
        return remote(
            pieces.at[line[d][1], k], z_in.at[h, k], z_sems.at[0, k, d], z_sems.at[1, k, d], line[d]
        )

    def share_out(k):
        value = whole(k)
        columns = width // n_h
        if k == 0:
            little = dot(whole(n_k), beside)
        for i in range(0, n_h, 2):
            lanes = dot(value[:, i * columns : (i + 2) * columns], joined)
            if k == 0:
                lanes = lanes + little[:, i * wide : (i + 2) * wide]
            pieces[i, k] = lanes[:, :wide].astype(BF16)
            pieces[i + 1, k] = lanes[:, wide:].astype(BF16)
        for d in range(n_h - 1, 0, -1):
            z_copy(k, d).start()

    for i in range(n_k + 2):
        if i < n_k:
            for q in members(chunks[i]):
                open_up(q)
        if 0 <= i - 1 < n_k:
            for q in members(chunks[i - 1]):
                pass_on(q)
        if i >= 2:
            share_out(chunks[i - 2])
    for k in chunks:
        total = pieces[h, k].astype(F32)
        for d in range(1, n_h):
            z_copy(k, d).wait_recv()
        for d in range(1, n_h):
            total = total + z_in[line[d][1], k].astype(F32)
        out[k] = total
    for k in chunks:
        for q in members(k):
            for x in range(2):
                core_copy(q, x).wait_send()
    for copy in sent:
        copy.wait_send()
    for k in range(n_k):
        for d in range(1, n_h):
            z_copy(k, d).wait_send()


def reduce_grads(sizes, grads, small):
    n_k, width, _ = grads.shape
    n_s, n_h, n_t = sizes
    rows, wide, thin = width // (n_s * n_t), 256, small.shape[1]
    vmem = pl.BlockSpec(memory_space=pltpu.VMEM)
    dma = pltpu.SemaphoreType.DMA

    def buffers(*lead):
        return [
            pltpu.VMEM((n_k, *lead, width), BF16),
            pltpu.VMEM((*lead, thin), BF16),
        ]

    return pl.pallas_call(
        partial(reduce_kernel, sizes),
        out_shape=jax.ShapeDtypeStruct((n_k, rows, wide), F32),
        in_specs=[vmem, vmem],
        out_specs=vmem,
        scratch_shapes=[
            *buffers(2, n_t * rows), *buffers(2, n_t, rows),
            *buffers(2, rows // 2), *buffers(rows), *buffers(rows),
            pltpu.VMEM((n_h, n_k, rows, wide), BF16),
            pltpu.VMEM((n_h, n_k, rows, wide), BF16),
            dma((2, 2 * (n_k + 1))), dma((2, 2 * (n_k + 1))), dma((2, 2 * (n_k + 1))),
            dma((2, 2 * (n_k + 1))), dma((2, n_k, n_h)),
        ],
        compiler_params=pltpu.CompilerParams(
            collective_id=4, has_side_effects=True, vmem_limit_bytes=VMEM_BYTES
        ),
        name="reduce_grads",
    )(grads, small)


def expert_kernel(sizes, backward, *refs):
    if backward:
        (blocks, weights, gate, slots_out, act_out, back_out, bias_out,
         w_a, w_b, gate_v, sums, slots, act, core_out, core_in, x_out, x_in, land, leave, back, land_back,
         w_sem, o_sem, in_sems, back_sems, core_sems, x_sems, act_sems, b_sems,
         bias_all, bias_send, bias_land) = refs
    else:
        (blocks, weights, gate, slots_out, act_out, gate_out, back_out,
         w_a, w_b, sums, slots, act, core_out, core_in, x_out, x_in, land, leave, back, land_back,
         w_sem, o_sem, in_sems, back_sems, core_sems, x_sems, act_sems) = refs
    peers = Peers(sizes)
    s, h, t = peers.at
    n_s, n_h, n_t = sizes
    me = peers.flat(peers.at)
    core, chip = lax.rem(s, 2), s // 2
    sibling = (s + 1 - 2 * core, h, t)
    across = (lax.rem(s + 2, n_s), h, t)
    half = act.shape[0] // 2
    own, other = core * half, (1 - core) * half
    n_blocks = peers.count
    first = 1 if backward else 0
    loads = [
        pltpu.make_async_copy(weights.at[first], w_a, w_sem.at[0]),
        pltpu.make_async_copy(weights.at[1 - first], w_b, w_sem.at[1]),
    ]
    for load in loads:
        load.start()
    if backward:
        gate_load = pltpu.make_async_copy(gate, gate_v, o_sem.at[0])
        gate_load.start()
    peers.greet_all()

    def block_out(p, k):
        place = peers.step(k, 1)
        return remote(
            blocks.at[place[1], place[0], p], land.at[p, me],
            in_sems.at[0, p, k], in_sems.at[1, p, k], place,
        )

    def block_in(p, k):
        source = peers.flat(peers.step(k, -1))
        return remote(
            blocks.at[0, 0, p], land.at[p, source], in_sems.at[0, p, k], in_sems.at[1, p, k], sibling
        )

    def each(function, count=n_blocks, start=1):
        lax.fori_loop(start, count, lambda k, carry: (function(k), carry)[1], 0)

    for p in range(2):
        each(lambda k: block_out(p, k).start())
        land[p, me] = blocks[h, s, p]
    few = half // 2
    group = 16
    many = 2 * group
    out_row = lax.broadcasted_iota(jnp.int32, (16 * group, 16 * group), 0)
    in_row = lax.broadcasted_iota(jnp.int32, (16 * group, 16 * group), 1)
    there = (out_row // many == in_row % (2 * few)) & (out_row % many == in_row // (2 * few))
    there = there.astype(F32).astype(BF16)
    again = (in_row // many == out_row % (2 * few)) & (in_row % many == out_row // (2 * few))
    again = again.astype(F32).astype(BF16)

    def receive(p):
        each(lambda k: block_in(p, k).wait_recv())
        for b in range(n_blocks // group):
            rows = land[p, b * group : (b + 1) * group].reshape(group * 16, land.shape[3])
            turned = dot(there, rows).astype(BF16).reshape(2 * few, many, land.shape[3])
            for c in range(2):
                first = c * half + p * few
                slots[first : first + few, b * many : (b + 1) * many, :] = turned[
                    c * few : (c + 1) * few
                ]

    receive(0)
    loads[0].wait()

    def core_copy(j):
        return remote(
            core_out.at[j], core_in.at[j], core_sems.at[0, j], core_sems.at[1, j], sibling
        )

    def x_copy(j):
        return remote(x_out.at[j], x_in.at[j], x_sems.at[0, j], x_sems.at[1, j], across)

    def act_copy(j):
        return remote(
            act.at[own + j], act.at[own + j], act_sems.at[0, j], act_sems.at[1, j], sibling
        )

    def act_in(j):
        return remote(
            act.at[other + j], act.at[other + j], act_sems.at[0, j], act_sems.at[1, j], sibling
        )

    def meet(j):
        core_copy(j).wait_recv()
        sums[j] = sums[j] + core_in[j].astype(F32)
        x_out[j] = sums[j].astype(BF16)
        x_copy(j).start()

    def first_sums(j):
        core_out[j] = dot(slots[other + j], w_a[other + j]).astype(BF16)
        core_copy(j).start()
        sums[j] = dot(slots[own + j], w_a[own + j])

        @pl.when(j > 0)
        def _():
            meet(j - 1)

    each(first_sums, few, 0)
    receive(1)
    each(first_sums, half, few)
    meet(half - 1)
    loads[1].wait()
    if backward:
        gate_load.wait()

    def second(e):
        leave[e] = dot_t(act[e], w_b[e]).astype(BF16)

    def finish(j):
        x_copy(j).wait_recv()
        value = sums[j] + x_in[j].astype(F32)
        if backward:
            act[own + j] = (value * gate_v[j]).astype(BF16)
        else:
            value = value + gate[own + j]
            cumulative = 0.5 + 0.5 * lax.erf(value * 0.7071067811865476)
            act[own + j] = (value * cumulative).astype(BF16)
            sums[j] = cumulative + value * (
                jnp.exp(value * value * -0.5) * 0.3989422804014327
            )
        act_copy(j).start()
        second(own + j)

        @pl.when(j > 0)
        def _():
            act_in(j - 1).wait_recv()
            second(other + j - 1)

    def back_copy(p, k):
        place = peers.step(k, 1)
        return remote(
            back.at[p, peers.flat(place)], land_back.at[p, me],
            back_sems.at[0, p, k], back_sems.at[1, p, k], place,
        )

    def back_in(p, k):
        source = peers.flat(peers.step(k, -1))
        return remote(
            back.at[p, 0], land_back.at[p, source],
            back_sems.at[0, p, k], back_sems.at[1, p, k], sibling,
        )

    def give_back(p):
        for b in range(n_blocks // group):
            rows = jnp.concatenate(
                [
                    leave[c * half + p * few : c * half + (p + 1) * few, b * many : (b + 1) * many, :]
                    for c in range(2)
                ],
                axis=0,
            ).reshape(group * 16, leave.shape[2])
            turned = dot(again, rows).astype(BF16)
            back[p, b * group : (b + 1) * group] = turned.reshape(group, 16, leave.shape[2])
        each(lambda k: back_copy(p, k).start())
        land_back[p, me] = back[p, me]

    each(finish, few + 1, 0)
    give_back(0)
    each(finish, half, few + 1)
    act_in(half - 1).wait_recv()
    second(other + half - 1)
    give_back(1)
    stores = [pltpu.make_async_copy(act, act_out, o_sem.at[1])]
    if not backward:
        stores.append(pltpu.make_async_copy(sums, gate_out, o_sem.at[0]))
    for store in stores:
        store.start()
    slots_out[...] = slots[...]
    if backward:
        across_t = (s, h, 1 - t)
        width = bias_out.shape[1]

        def bias_row(e):
            bias_all[pl.ds(e, 1), :] = jnp.sum(act[e].astype(F32), axis=0, keepdims=True)

        each(bias_row, 2 * half, 0)

        def piece(for_t):
            return bias_all[:, pl.ds(pl.multiple_of((core * n_t + for_t) * width, 128), width)]

        bias_send[...] = piece(1 - t)
        bias_copy = remote(bias_send, bias_land, b_sems.at[0], b_sems.at[1], across_t)
        bias_copy.start()
        bias_copy.wait()
        bias_out[...] = jnp.where(t == chip, piece(t), bias_land[...])
    for p in range(2):
        each(lambda k: back_in(p, k).wait_recv())
    back_out[...] = land_back[...]
    for store in stores:
        store.wait()
    for p in range(2):
        each(lambda k: block_out(p, k).wait_send())
        each(lambda k: back_copy(p, k).wait_send())
    for copy in (core_copy, x_copy, act_copy):
        each(lambda j: copy(j).wait_send(), half, 0)


def expert_pass(sizes, backward, blocks, weights, gate, bias_width=0):
    _, experts, rows, hidden = weights.shape
    devices = sizes[0] * sizes[1] * sizes[2]
    images = 2 * devices
    half = experts // 2
    vmem = pl.BlockSpec(memory_space=pltpu.VMEM)
    hbm = pl.BlockSpec(memory_space=pl.ANY)
    slots = jax.ShapeDtypeStruct((experts, images, rows), BF16)
    act = jax.ShapeDtypeStruct((experts, images, hidden), BF16)
    gate_shape = (half, images, hidden)
    returned = jax.ShapeDtypeStruct((2, devices, experts, rows), BF16)
    if backward:
        operands, in_specs = (blocks, weights, gate), [vmem, hbm, hbm]
        outs = (slots, act, returned, jax.ShapeDtypeStruct((experts, bias_width), F32))
        out_specs = (vmem, hbm, vmem, vmem)
    else:
        operands, in_specs = (blocks, weights, gate), [vmem, hbm, vmem]
        outs = (slots, act, jax.ShapeDtypeStruct(gate_shape, F32), returned)
        out_specs = (vmem, hbm, hbm, vmem)
    weight = pltpu.VMEM((experts, rows, hidden), BF16)
    chunk = pltpu.VMEM((half, images, hidden), BF16)
    block = pltpu.VMEM((2, devices, experts, rows), BF16)
    dma = pltpu.SemaphoreType.DMA
    scratch = [weight, weight]
    if backward:
        scratch.append(pltpu.VMEM(gate_shape, F32))
    scratch += [
        pltpu.VMEM(gate_shape, F32),
        pltpu.VMEM(slots.shape, BF16),
        pltpu.VMEM(act.shape, BF16),
        chunk, chunk, chunk, chunk, block,
        pltpu.VMEM(slots.shape, BF16),
        block, block,
        dma((2,)), dma((2,)), dma((2, 2, devices)), dma((2, 2, devices)),
        dma((2, half)), dma((2, half)), dma((2, half)),
    ]
    if backward:
        scratch += [
            dma((2,)),
            pltpu.VMEM((experts, hidden), F32),
            pltpu.VMEM((experts, bias_width), F32),
            pltpu.VMEM((experts, bias_width), F32),
        ]
    return pl.pallas_call(
        partial(expert_kernel, sizes, backward),
        out_shape=outs,
        in_specs=in_specs,
        out_specs=out_specs,
        scratch_shapes=scratch,
        compiler_params=pltpu.CompilerParams(
            collective_id=2 if backward else 1, has_side_effects=True, vmem_limit_bytes=VMEM_BYTES
        ),
        cost_estimate=pl.CostEstimate(
            flops=8 * images * experts * rows * hidden,
            bytes_accessed=weights.size * 2,
            transcendentals=0,
        ),
        name="experts_back" if backward else "experts_ahead",
    )(*operands)


def weight_grad_kernel(slots_0, act_0, slots_1, act_1, out, lines, pick, same):
    group, images, rows = slots_0.shape
    d_block = out.shape[0]
    n = group * d_block
    m, d = pl.program_id(0), pl.program_id(2)

    @pl.when((m == 0) & (pl.program_id(1) == 0) & (d == 0))
    def _():
        row = lax.broadcasted_iota(jnp.int32, pick.shape, 0)
        column = lax.broadcasted_iota(jnp.int32, pick.shape, 1)
        pick[...] = (column == row // group).astype(F32).astype(BF16)
        row = lax.broadcasted_iota(jnp.int32, same.shape, 0)
        column = lax.broadcasted_iota(jnp.int32, same.shape, 1)
        same[...] = (row % group == column // images).astype(F32)

    def prepare(slots):
        @pl.when(d == 0)
        def _():
            turned = slots[...].reshape(group * images, rows).astype(F32)
            lines[...] = jnp.swapaxes(turned, 0, 1).astype(BF16)

    def term(act):
        mine = lines[pl.ds(pl.multiple_of(d * d_block, d_block), d_block)]
        spread = (dot(pick[...], mine) * same[...]).astype(BF16)
        values = act[...].reshape(group * images, act.shape[2])
        out[...] = dot(spread, values).reshape(out.shape)

    @pl.when(m == 0)
    def _():
        prepare(slots_0)
        term(act_0)

    @pl.when(m == 1)
    def _():
        prepare(slots_1)
        term(act_1)


def weight_grads(slots_0, act_0, slots_1, act_1):
    experts, images, rows = slots_0.shape
    hidden = act_0.shape[2]
    group, d_block = 8, 32
    last = experts // group - 1

    def early(m, g, d):
        return jnp.where(m == 0, g, last), 0, 0

    def late(m, g, d):
        return jnp.where(m == 0, 0, g), 0, 0

    slots, act = (group, images, rows), (group, images, hidden)
    return pl.pallas_call(
        weight_grad_kernel,
        grid=(2, experts // group, rows // d_block),
        out_shape=jax.ShapeDtypeStruct((rows, 2, experts, hidden), F32),
        in_specs=[
            pl.BlockSpec(slots, early), pl.BlockSpec(act, early),
            pl.BlockSpec(slots, late), pl.BlockSpec(act, late),
        ],
        out_specs=pl.BlockSpec((d_block, 1, group, hidden), lambda m, g, d: (d, m, g, 0)),
        scratch_shapes=[
            pltpu.VMEM((rows, group * images), BF16),
            pltpu.VMEM((group * d_block, d_block), BF16),
            pltpu.VMEM((group * d_block, group * images), F32),
        ],
        compiler_params=pltpu.CompilerParams(vmem_limit_bytes=VMEM_BYTES),
        cost_estimate=pl.CostEstimate(
            flops=4 * images * experts * rows * hidden,
            bytes_accessed=8 * rows * experts * hidden,
            transcendentals=0,
        ),
        name="weight_grads",
    )(slots_0, act_0, slots_1, act_1)


def normalize(values, scale, shift):
    centered = values - jnp.mean(values, axis=-1, keepdims=True)
    variance = jnp.mean(centered * centered, axis=-1, keepdims=True)
    inverse = lax.rsqrt(variance + epsilon)
    unit_part = centered * inverse
    return (unit_part * scale + shift, unit_part, inverse)


def normalize_back(grad_output, unit_part, inverse, scale):
    scaled = grad_output * scale
    average = jnp.mean(scaled, axis=-1, keepdims=True)
    projection = jnp.mean(scaled * unit_part, axis=-1, keepdims=True)
    grad_input = inverse * (scaled - average - unit_part * projection)
    return (
        grad_input,
        jnp.sum(grad_output * unit_part, axis=(0, 1)),
        jnp.sum(grad_output, axis=(0, 1)),
    )


def to_experts(slots):
    slots = lax.all_to_all(slots, "heads", split_axis=1, concat_axis=0, tiled=True)
    slots = lax.all_to_all(slots, "shard", split_axis=2, concat_axis=0, tiled=True)
    return lax.all_gather(slots, "tensor", axis=0, tiled=True)


def to_blocks(slots, sizes):
    own, experts, width = slots.shape
    n_s, n_h, _ = sizes
    few = experts // n_h // 4
    slots = slots.reshape(own, n_h, 2, 2, few, n_s, width // n_s)
    return slots.transpose(1, 5, 3, 0, 2, 4, 6).reshape(n_h, n_s, 2, own * 2 * few, width // n_s)


def from_blocks(blocks, sizes):
    n_s, n_h, n_t = sizes
    rows = blocks.shape[3]
    blocks = jnp.sum(blocks.reshape(2, n_s, n_h, n_t, 2, 2, -1, rows).astype(F32), axis=3)
    return blocks.transpose(3, 2, 4, 0, 5, 1, 6).reshape(2, -1, n_s * rows)


def to_images(slots):
    slots = lax.psum_scatter(slots, "tensor", scatter_dimension=0, tiled=True)
    slots = lax.all_to_all(slots, "shard", split_axis=0, concat_axis=2, tiled=True)
    return lax.all_to_all(slots, "heads", split_axis=0, concat_axis=1, tiled=True)


def shards(tokens, norm_scales, norm_biases, w_attn, phi, experts, in_bias, out_bias, cotangent):
    heads_n = lax.axis_size("heads")
    sizes = tuple(lax.axis_size(name) for name in ("shard", "heads", "tensor"))
    if sizes != (4, 4, 2) or tokens.shape[0] != 8 or experts.shape[2] != 16:
        sizes = None
    group, seq_len, width = tokens.shape
    own = group // heads_n
    heads_index = lax.axis_index("heads")
    tensor_index = lax.axis_index("tensor")
    shard_index = lax.axis_index("shard")
    hidden = experts.shape[3]
    rows = experts.shape[0]
    if sizes is not None:
        n_s, n_h, n_t = sizes
        block, slot = w_attn.shape[2], phi.shape[1]
        beside = jnp.concatenate((phi, out_bias.T), axis=1)
        beside = jnp.pad(beside, ((0, 0), (0, 256 - block - 2 * slot)))
        beside = jnp.concatenate((beside[None], jnp.zeros((3, *beside.shape), BF16)), axis=0)
        packet = jnp.concatenate((w_attn, beside), axis=2)
        extra = jnp.concatenate(
            (
                in_bias.reshape(-1, 64),
                norm_scales.T,
                norm_biases.T,
            ),
            axis=1,
        )
        extra = jnp.pad(extra, ((0, 0), (128, 60)))
        attn, small, turned = gather_weights(sizes, packet, extra, experts)
        phi_full = small[:, :64]
        out_all = small[:, 64:128].T.astype(F32)
        in_full = small[:, 128:192].reshape(n_s * n_t, -1, in_bias.shape[1])
        in_full = in_full.transpose(1, 0, 2).reshape(in_bias.shape[0], -1).astype(F32)
        scales = small[:, 192:194].T.astype(F32)
        biases = small[:, 194:196].T.astype(F32)
    else:
        scales, biases, in_full = (
            lax.all_gather(norm_scales, ROWS, axis=1, tiled=True).astype(F32),
            lax.all_gather(norm_biases, ROWS, axis=1, tiled=True).astype(F32),
            lax.all_gather(in_bias, ROWS, axis=1, tiled=True).astype(F32),
        )
        attn = lax.all_gather(
            lax.all_gather(w_attn, "heads", axis=2, tiled=True), ROWS, axis=1, tiled=True
        )
        phi_full = lax.all_gather(
            lax.all_gather(phi, "heads", axis=1, tiled=True), ROWS, axis=0, tiled=True
        )
        out_rows = lax.all_gather(out_bias, "tensor", axis=1, tiled=True).astype(F32)
    e_own = experts.shape[2] // lax.axis_size("shard")
    in_local = lax.dynamic_slice_in_dim(in_full, tensor_index * hidden, hidden, 1)
    factor = HEAD_DIM ** (-0.5)
    tokens = lax.dynamic_slice_in_dim(tokens, heads_index * own, own, 0)
    cotangent = lax.dynamic_slice_in_dim(cotangent, heads_index * own, own, 0)
    n_heads = width // HEAD_DIM
    inputs = tokens.astype(F32)
    normed_one, unit_one, inverse_one = normalize(inputs, scales[0], biases[0])
    normed_one_b = normed_one.astype(BF16)
    projected = einsum("nsd,kdc->knsc", normed_one_b, attn[:3]).astype(BF16)
    query, keyed, valued = projected.reshape(3, own, seq_len, n_heads, HEAD_DIM)
    scores = einsum("nqhe,nkhe->nhqk", query, keyed) * factor
    score_peak = jnp.max(scores, axis=-1, keepdims=True)
    exponent = jnp.exp(scores - score_peak)
    probs = exponent / jnp.sum(exponent, axis=-1, keepdims=True)
    probs_b = probs.astype(BF16)
    context_b = (
        einsum("nhqk,nkhe->nqhe", probs_b, valued).astype(BF16).reshape(own, seq_len, width)
    )
    hidden_one = inputs + einsum("nsc,dc->nsd", context_b, attn[3])
    normed_two, unit_two, inverse_two = normalize(hidden_one, scales[1], biases[1])
    normed_two_b = normed_two.astype(BF16)
    logits = einsum("nsd,de->nse", normed_two_b, phi_full)
    dispatch = jax.nn.softmax(logits, axis=1)
    dispatch_b = dispatch.astype(BF16)
    combine = jax.nn.softmax(logits, axis=2)
    combine_b = combine.astype(BF16)
    slot_in = einsum("nse,nsd->ned", dispatch_b, normed_two_b).astype(BF16)
    if sizes is not None:
        slot_in, activated, gate, back = expert_pass(
            sizes, False, to_blocks(slot_in, sizes), turned, in_local[:, None, :]
        )
        slot_out = (from_blocks(back, sizes) + out_all).astype(BF16)
    else:
        slot_in = to_experts(slot_in)
        share = 1 if e_own else 0

        def meet(partial_sum):
            return lax.psum_scatter(partial_sum, "shard", scatter_dimension=share, tiled=True)

        def spread(values):
            return lax.all_gather(values, "shard", axis=share, tiled=True)

        pre = meet(einsum("ned,def->nef", slot_in, experts[:, 0]))
        if e_own:
            pre = pre + lax.dynamic_slice_in_dim(in_local, shard_index * e_own, e_own, 0)
        else:
            pre = pre + in_local
        gelu_value, gelu_back = jax.vjp(partial(jax.nn.gelu, approximate=False), pre)
        activated = spread(gelu_value.astype(BF16))
        slot_out_part = einsum("nef,def->ned", activated, experts[:, 1])
        slot_out_part = slot_out_part + jnp.where(tensor_index == 0, out_rows, 0.0)
        slot_out = to_images(slot_out_part).astype(BF16)
    output = (hidden_one + einsum("nse,ned->nsd", combine_b, slot_out)).astype(BF16)
    grad_combine = einsum("nsd,ned->nse", cotangent, slot_out)
    grad_slot = einsum("nse,nsd->ned", combine_b, cotangent).astype(BF16)
    if sizes is not None:
        grad_slot, grad_pre, back, in_bias_grad = expert_pass(
            sizes, True, to_blocks(grad_slot, sizes), turned, gate, in_bias.shape[1]
        )
        back, output = lax.optimization_barrier((back, output))
        output = lax.all_gather(output, "heads", axis=0, tiled=True)
        grad_slot_in = from_blocks(back, sizes).astype(BF16)
        experts_grad = weight_grads(slot_in, grad_pre, grad_slot, activated)
        grad_slot_sum = jnp.sum(grad_slot.astype(F32), axis=1)
    else:
        output = lax.all_gather(output, "heads", axis=0, tiled=True)
        grad_slot = to_experts(grad_slot)
        grad_act = meet(einsum("ned,def->nef", grad_slot, experts[:, 1]))
        grad_pre = spread(gelu_back(grad_act)[0].astype(BF16))
        grad_slot_in = einsum("nef,def->ned", grad_pre, experts[:, 0]).astype(BF16)
        input_term = einsum("ned,nef->def", slot_in, grad_pre)
        output_term = einsum("ned,nef->def", grad_slot, activated)
        experts_grad = jnp.stack((input_term, output_term), axis=1)
        grad_slot_in = to_images(grad_slot_in.astype(F32)).astype(BF16)
        in_bias_grad = lax.dynamic_slice_in_dim(
            lax.all_gather(jnp.sum(grad_pre.astype(F32), axis=0), "tensor", axis=1, tiled=True),
            (shard_index * lax.axis_size("tensor") + tensor_index) * in_bias.shape[1],
            in_bias.shape[1],
            1,
        )
        grad_slot_sum = jnp.sum(grad_slot.astype(F32), axis=0)
    out_bias_grad = lax.dynamic_slice_in_dim(
        grad_slot_sum,
        tensor_index * out_bias.shape[1],
        out_bias.shape[1],
        1,
    )
    grad_dispatch = einsum("nsd,ned->nse", normed_two_b, grad_slot_in)
    grad_logits = (
        dispatch * (grad_dispatch - jnp.sum(dispatch * grad_dispatch, axis=1, keepdims=True))
        + combine * (grad_combine - jnp.sum(combine * grad_combine, axis=2, keepdims=True))
    ).astype(BF16)
    phi_grad = einsum("nsd,nse->de", normed_two_b, grad_logits)
    grad_normed_two = einsum("nse,ned->nsd", dispatch_b, grad_slot_in) + einsum(
        "nse,de->nsd", grad_logits, phi_full
    )
    grad_hidden_norm, scale_two_grad, bias_two_grad = normalize_back(
        grad_normed_two, unit_two, inverse_two, scales[1]
    )
    grad_hidden = cotangent.astype(F32) + grad_hidden_norm
    grad_hidden_b = grad_hidden.astype(BF16)
    out_weight_grad = einsum("nsd,nsc->dc", grad_hidden_b, context_b)
    grad_context = einsum("nsd,dc->nsc", grad_hidden_b, attn[3]).astype(BF16)
    grad_context = grad_context.reshape(own, seq_len, n_heads, HEAD_DIM)
    grad_value = einsum("nhqk,nqhe->nkhe", probs_b, grad_context).astype(BF16)
    grad_probs = einsum("nqhe,nkhe->nhqk", grad_context, valued)
    grad_scores = (
        probs * (grad_probs - jnp.sum(probs * grad_probs, axis=-1, keepdims=True))
    ).astype(BF16)
    grad_query = (einsum("nhqk,nkhe->nqhe", grad_scores, keyed) * factor).astype(BF16)
    grad_key = (einsum("nhqk,nqhe->nkhe", grad_scores, query) * factor).astype(BF16)
    grad_proj = jnp.stack((grad_query, grad_key, grad_value)).reshape(3, own, seq_len, width)
    proj_grad = einsum("nsd,knsc->kdc", normed_one_b, grad_proj)
    grad_normed_one = einsum("knsc,kdc->nsd", grad_proj, attn[:3])
    grad_input_norm, scale_one_grad, bias_one_grad = normalize_back(
        grad_normed_one, unit_one, inverse_one, scales[0]
    )
    input_grad = (grad_hidden + grad_input_norm).astype(BF16)
    input_grad = lax.all_gather(input_grad, "heads", axis=0, tiled=True)
    attn_grad = jnp.concatenate((proj_grad, out_weight_grad[None]), axis=0)
    norms = jnp.stack((scale_one_grad, scale_two_grad, bias_one_grad, bias_two_grad))
    if sizes is not None:
        small = jnp.concatenate((phi_grad, norms.T), axis=1)
        small = jnp.pad(small, ((0, 0), (0, 128 - small.shape[1]))).astype(BF16)
        summed = reduce_grads(sizes, attn_grad.astype(BF16), small)
        attn_grad = summed[:, :, :block]
        phi_grad = summed[0, :, block : block + slot]
        norms = summed[0, :, block + slot : block + slot + 4].T
    else:
        attn_grad = lax.psum_scatter(attn_grad, ROWS, scatter_dimension=1, tiled=True)
        attn_grad = lax.psum_scatter(attn_grad, "heads", scatter_dimension=2, tiled=True)
        phi_grad = lax.psum_scatter(phi_grad, ROWS, scatter_dimension=0, tiled=True)
        phi_grad = lax.psum_scatter(phi_grad, "heads", scatter_dimension=1, tiled=True)
        norms = lax.psum(lax.psum_scatter(norms, ROWS, scatter_dimension=1, tiled=True), "heads")
    return (
        output,
        input_grad,
        norms[:2],
        norms[2:],
        attn_grad,
        phi_grad,
        experts_grad,
        in_bias_grad,
        out_bias_grad,
    )


def solution(mesh):
    images = P(ROWS, None, None)
    return jax.shard_map(
        shards,
        mesh=mesh,
        in_specs=(
            images,
            P(None, ROWS),
            P(None, ROWS),
            P(None, ROWS, "heads"),
            P(ROWS, "heads"),
            P("shard", None, "heads", "tensor"),
            P("heads", ROWS),
            P("heads", ROWS),
            images,
        ),
        out_specs=(
            images,
            images,
            P(None, ROWS),
            P(None, ROWS),
            P(None, ROWS, "heads"),
            P(ROWS, "heads"),
            P("shard", None, "heads", "tensor"),
            P("heads", ROWS),
            P("heads", ROWS),
        ),
        check_vma=False,
    )
```

profile of v0, /device:TPU:0, one launch (start us, length us, event | category | flops | bytes accessed | tf_op | source)
XLA Modules:
  0.0 403.9 jit_solution(13910305038792557704)
XLA Ops:
  7.2 0.7 pad_maximum_fusion.4
  8.1 0.8 copy.196
  8.8 0.8 copy.195
  9.6 0.8 reshape.124
  10.4 1.7 fusion.73.packet
  12.1 0.7 fusion.88.extra
  12.8 47.2 %gather_weights.1 = (bf16[4,768,768]{2,1,0:T(8,128)(2,1)}, bf16[768,256]{1,0:T(8,128)(2,1)}, bf16[2,16,192,1536]{3,2,1,0:T(8,128)(2,1)}) custom-call(bf16[4,96,256]{2,1,0:T(8,128)(2,1)} %fusion.73.packet, bf16[96,256]{1,0:T(8,128)(2,1)} %fusion.88.extra, bf16[192,2,16,1536]{3,2,1,0:T(8,128)(2,1)} %experts.1), custom_call_target="tpu_custom_call" | custom-call | tf_op jit(solution)/shard_map/gather_weights/pallas_call | solution.py:296
  60.0 1.2 convert_bitcast_fusion.3
  61.2 3.8 constant_dynamic-slice_fusion.2
  65.6 0.7 slice_reduce_fusion
  66.9 1.8 convert_bitcast_fusion
  68.8 1.2 copy.197
  70.5 4.2 %fusion.101 = (f32[2,12,197]{2,1,0:T(8,128)S(1)}, f32[2,12,197,197]{2,3,1,0:T(8,128)}) fusion(bf16[2,197,12,64]{1,3,2,0:T(8,128)(2,1)S(1)} %bitcast.137, bf16[2,197,12,64]{1,3,2,0:T(8,128)(2,1)S(1)} %bitcast.135), kind=kOutput, calls=%fused_computation.158 | convolution fusion | flops 122015688 | bytes 4954944 | tf_op jit(solution)/shard_map/sub | solution.py:944
  74.7 3.3 convolution_convert_fusion.1
  78.0 2.5 fusion.102
  82.8 0.8 fusion.104
  83.6 0.9 convert_bitcast_fusion.1
  84.5 1.9 convolution_convert_fusion.4
  86.4 1.9 reshape.126
  88.3 1.8 copy.267
  90.0 1.8 reshape.127.refs_0_
  91.9 2.0 convolution_convert_fusion.3
  93.9 1.2 reshape.128
  95.1 0.9 reshape.129.refs_0_
  96.2 0.7 broadcast_in_dim.8.refs_2_
  96.9 68.2 %experts_ahead.1 = (bf16[16,64,192]{2,1,0:T(8,128)(2,1)}, bf16[16,64,1536]{2,1,0:T(8,128)(2,1)}, f32[8,64,1536]{2,1,0:T(8,128)}, bf16[2,32,16,192]{3,2,1,0:T(8,128)(2,1)}) custom-call(bf16[4,4,2,16,192]{4,3,2,1,0:T(8,128)(2,1)} %reshape.129.refs_0_, bf16[2,16,192,1536]{3,2,1,0:T(8,128)(2,1)} %get-tuple-element.24.refs_1_, f32[16,1,1536]{2,1,0:T(1,128)} %broadcast_in_dim.8.refs_2_), custom_call_target="tpu_custom_call" | custom-call | flops 2415919104 | bytes 18874368 | tf_op jit(solution)/shard_map/experts_ahead/pallas_call | solution.py:743
  165.1 1.3 reshape.133
  166.4 1.3 reduce_sum.196
  167.7 1.4 copy.207
  169.4 1.1 copy.208
  170.6 69.0 %experts_back.1 = (bf16[16,64,192]{2,1,0:T(8,128)(2,1)}, bf16[16,64,1536]{2,1,0:T(8,128)(2,1)}, bf16[2,32,16,192]{3,2,1,0:T(8,128)(2,1)}, f32[16,384]{1,0:T(8,128)}) custom-call(bf16[4,4,2,16,192]{4,3,2,1,0:T(8,128)(2,1)} %reshape.127.refs_0_, bf16[2,16,192,1536]{3,2,1,0:T(8,128)(2,1)} %get-tuple-element.24.refs_1_, f32[8,64,1536]{2,1,0:T(8,128)} %get-tuple-element.25.refs_2_), custom_call_target="tpu_custom_call" | custom-call | flops 2415919104 | bytes 18874368 | tf_op jit(solution)/shard_map/experts_back/pallas_call | solution.py:743
  239.5 2.2 fusion.28
  242.0 1.0 fusion.57
  243.2 1.2 reduce
  244.4 1.2 copy.209
  245.6 0.9 convert_element_type.171
  246.5 2.6 fusion.89
  249.2 2.4 fusion.51
  251.6 3.3 multiply_reduce_fusion.2
  254.9 1.7 multiply_add_fusion
  256.7 1.0 copy-done
  257.7 1.9 convolution_convert_fusion.2
  260.4 3.3 convolution_convert_fusion
  263.7 1.1 copy.217
  264.8 3.4 multiply_reduce_fusion
  268.3 3.3 multiply_convert_fusion
  271.6 1.8 multiply_convert_fusion.1
  273.4 2.2 copy.216
  275.6 2.6 multiply_convert_fusion.2
  278.2 2.3 copy.215
  280.6 4.3 %fusion.36 = (bf16[768]{0:T(1024)(128)(2,1)S(1)}, f32[2,197]{1,0:T(2,128)S(1)}, f32[2,197]{1,0:T(2,128)S(1)}, bf16[768]{0:T(1024)(128)(2,1)S(1)}, f32[2,197,768]{2,1,0:T(8,128)S(1)}) fusion(f32[2,197]{1,0:T(2,128)S(1)} %copy-done.37, f32[2,197]{1,0:T(2,128)S(1)} %copy-done.33, bf16[2,197,768]{2,0,1:T(2,128)(2,1)S(1)} %get-tuple-element.123, ...), kind=kOutput, calls=%fused_computation.50 | convolution fusion | flops 1399183104 | bytes 7191712 | tf_op jit(solution)/shard_map/knsc,kdc->nsd/dot_general | solution.py:1045
  284.9 1.3 fusion.35
  286.5 1.4 fusion.44
  288.1 0.8 fusion.74.small
  288.9 2.1 fusion.27
  291.0 2.4 fusion.8
  293.4 2.6 pad_maximum_fusion.grads
  296.0 59.4 %reduce_grads.1 = f32[4,96,256]{2,1,0:T(8,128)} custom-call(bf16[4,768,768]{2,1,0:T(8,128)(2,1)} %pad_maximum_fusion.grads, bf16[768,128]{1,0:T(8,128)(2,1)} %fusion.74.small), custom_call_target="tpu_custom_call" | custom-call | tf_op jit(solution)/shard_map/reduce_grads/pallas_call | solution.py:472
  355.4 0.9 slice_bitcast_fusion.1
  357.7 0.9 slice_bitcast_fusion
  360.0 28.2 %weight_grads.1 = f32[192,2,16,1536]{3,2,1,0:T(8,128)} custom-call(bf16[16,64,192]{2,1,0:T(8,128)(2,1)} %get-tuple-element.30.slots_0, bf16[16,64,1536]{2,1,0:T(8,128)(2,1)} %get-tuple-element.31.act_0, bf16[16,64,192]{2,1,0:T(8,128)(2,1)} %get-tuple-element.32.slots_1, bf16[16,64,1536]{2,1,0:T(8,128)(2,1)} %get-tuple-element.33.act_1), custom_call_target="tpu_custom_call" | custom-call | flops 1207959552 | bytes 37748736 | tf_op jit(solution)/shard_map/weight_grads/pallas_call | solution.py:812
  388.2 3.6 copy.222
  391.8 3.6 copy.223
  395.5 0.7 copy.270
  (131 shorter events, 9.9 us)
Async XLA Ops:
  7.2 381.1 %all-gather.3.cloned.1.call-start = ((), (), s32[]{:S(2)}) async-start(), calls=%async_computation | async-start | bytes 3072000 | tf_op jit(solution)/shard_map/all_gather | solution.py:992
  61.2 5.7 %copy-start.19 = (bf16[4,768,768]{2,1,0:T(8,128)(2,1)S(1)}, bf16[4,768,768]{2,1,0:T(8,128)(2,1)}, u32[]{:S(2)}) copy-start(bf16[4,768,768]{2,1,0:T(8,128)(2,1)} %get-tuple-element.22) | copy-start | bytes 14155780
  65.2 1.1 copy-start.32
  65.6 0.8 copy-start.36
  66.3 0.6 copy-start.34
  66.3 0.6 copy-start.38
  66.3 14.5 %copy-start.21 = (f32[768]{0:T(1024)}, f32[768]{0:T(1024)S(1)}, u32[]{:S(2)}) copy-start(f32[768]{0:T(1024)S(1)} %get-tuple-element.125) | copy-start | bytes 9220
  70.2 4.4 %copy-start.5 = (bf16[1,2,197,768]{2,3,1,0:T(8,128)(2,1)}, bf16[1,2,197,768]{2,3,1,0:T(8,128)(2,1)S(1)}, u32[]{:S(2)}) copy-start(bf16[1,2,197,768]{2,3,1,0:T(8,128)(2,1)S(1)} %copy.198) | copy-start | bytes 1815556
  70.5 4.2 %copy-start.4 = (bf16[1,2,197,768]{2,3,1,0:T(8,128)(2,1)}, bf16[1,2,197,768]{2,3,1,0:T(8,128)(2,1)S(1)}, u32[]{:S(2)}) copy-start(bf16[1,2,197,768]{2,3,1,0:T(8,128)(2,1)S(1)} %copy.199) | copy-start | bytes 1815556
  74.7 3.3 copy-start.27
  78.0 2.5 copy-start.42
  80.5 0.6 copy-start.23
  80.8 1.0 copy-start.2
  80.8 1.3 copy-start.25
  81.8 10.1 %copy-start.7 = (bf16[2,197,768]{2,1,0:T(8,128)(2,1)}, bf16[2,197,768]{2,1,0:T(8,128)(2,1)S(1)}, u32[]{:S(2)}) copy-start(bf16[2,197,768]{2,1,0:T(8,128)(2,1)S(1)} %add_convert_fusion) | copy-start | bytes 1815556
  82.1 0.7 copy-start.12
  82.8 156.7 %copy-start.30 = (f32[2,197]{1,0:T(2,128)}, f32[2,197]{1,0:T(2,128)S(1)}, u32[]{:S(2)}) copy-start(f32[2,197]{1,0:T(2,128)S(1)} %get-tuple-element.114) | copy-start | bytes 4732
  83.6 8.3 %copy-start.40 = (f32[2,64]{1,0:T(2,128)}, f32[2,64]{1,0:T(2,128)S(1)}, u32[]{:S(2)}) copy-start(f32[2,64]{1,0:T(2,128)S(1)} %get-tuple-element.116) | copy-start | bytes 1540
  241.8 1.2 copy-start.18
  241.8 150.0 %all-gather.5.cloned.1.call-start = ((), (), s32[]{:S(2)}) async-start(), calls=%async_computation.1 | async-start | bytes 3072000 | tf_op jit(solution)/shard_map/all_gather | solution.py:1050
  243.2 3.3 copy-start.41
  244.4 4.8 %copy-start.8 = (bf16[2,197,768]{2,1,0:T(8,128)(2,1)S(1)}, bf16[2,197,768]{2,1,0:T(8,128)(2,1)}, u32[]{:S(2)}) copy-start(bf16[2,197,768]{2,1,0:T(8,128)(2,1)} %copy-done.7) | copy-start | bytes 1815556
  249.1 2.5 copy-start.3
  249.1 2.5 copy-start.22
  249.1 2.5 copy-start.24
  249.1 2.5 copy-start.26
  249.1 2.5 copy-start.31
  256.6 1.0 copy-start
  259.6 0.8 copy-start.28
  263.7 1.1 copy-start.13
  268.3 3.3 copy-start.6
  278.2 2.3 copy-start.14
  278.2 2.3 copy-start.15
  278.2 2.3 copy-start.33
  278.2 2.3 copy-start.35
  278.2 2.3 copy-start.37
  280.6 4.3 %copy-start.1 = (f32[2,197,768]{2,1,0:T(8,128)S(1)}, f32[2,197,768]{2,1,0:T(8,128)}, u32[]{:S(2)}) copy-start(f32[2,197,768]{2,1,0:T(8,128)} %copy-done) | copy-start | bytes 3631108
  284.9 1.6 copy-start.9
  284.9 1.6 copy-start.20
  288.9 2.1 copy-start.16
  288.9 2.1 copy-start.17
  288.9 2.1 copy-start.39
  296.0 63.2 %copy-start.10 = (bf16[16,64,192]{2,1,0:T(8,128)(2,1)S(1)}, bf16[16,64,192]{2,1,0:T(8,128)(2,1)}, u32[]{:S(2)}) copy-start(bf16[16,64,192]{2,1,0:T(8,128)(2,1)} %get-tuple-element.32.slots_1) | copy-start | bytes 1179652
  391.8 3.6 copy-start.11
  391.8 4.4 %copy-start.29 = (f32[16,384]{1,0:T(8,128)S(1)}, f32[16,384]{1,0:T(8,128)}, u32[]{:S(2)}) copy-start(f32[16,384]{1,0:T(8,128)} %get-tuple-element.142) | copy-start | bytes 73732
Sparse Core Ops, SparseCore 0:
  241.9 52.2 all-gather.2
  296.3 67.3 all-gather.4
where the time goes:
time: 411 us; the launch traced here: 404 us
  Pallas kernels  272 us (66%)
  matrix products  50.8 us (12%)
  local copies, waits for them, and re-layouts  46 us (11%)
  other arithmetic  20 us (5%)
  between operations  15 us (4%)
    pallas_call x2, Pallas kernels, expert_pass(): pl.pallas_call(partial(expert_kernel, sizes, backward), out_shape=outs, i...  137 us
    pallas_call x1, Pallas kernels, reduce_grads(): pl.pallas_call(partial(reduce_kernel, sizes), out_shape=jax.ShapeDtypeStr...  59.4 us
    pallas_call x1, Pallas kernels, gather_weights(): pl.pallas_call(partial(gather_kernel, sizes), out_shape=(jax.ShapeDtypeSt...  47.2 us
    pallas_call x1, Pallas kernels, weight_grads(): pl.pallas_call(weight_grad_kernel, grid=(2, experts // group, rows // d_b...  28.2 us
    unnamed x95, local copies, waits for them, and re-layouts  15 us
  transfers between devices with their start and end apart: 2, of which 0 were waited for; matrix products, arithmetic and copies ran while one was open for 15% of the time, Pallas kernels for 22%

commit v1 on v0

--- a/solution.py
+++ b/solution.py
@@ -102,6 +102,7 @@
     block = width // n_h
     side = 16
     n_tiles = experts.shape[0] // side
+    depth = tile_in.shape[0]
     halves = ((0, rows // 2), (rows // 2, rows // 2))
 
     def z_hop(k, origin, up):
@@ -142,18 +143,19 @@
     def load(i):
         return pltpu.make_async_copy(
             experts.at[pl.ds((i % n_tiles) * side, side), i // n_tiles],
-            tile_in.at[i % 2],
-            t_sems.at[0, i % 2],
+            tile_in.at[i % depth],
+            t_sems.at[0, i % depth],
         )
 
     def store(i):
         return pltpu.make_async_copy(
-            tile_out.at[i % 2],
+            tile_out.at[i % depth],
             turned.at[i // n_tiles, :, pl.ds((i % n_tiles) * side, side)],
-            t_sems.at[1, i % 2],
-        )
-
-    load(0).start()
+            t_sems.at[1, i % depth],
+        )
+
+    for i in range(depth - 1):
+        load(i).start()
     swap = swap_matrix(side)
     done = [0]
 
@@ -161,16 +163,16 @@
         def step(i, carry):
             load(i).wait()
 
-            @pl.when(i + 1 < 2 * n_tiles)
+            @pl.when(i + depth - 1 < 2 * n_tiles)
             def _():
-                load(i + 1).start()
-
-            @pl.when(i >= 2)
+                load(i + depth - 1).start()
+
+            @pl.when(i >= depth)
             def _():
-                store(i - 2).wait()
-
-            rows_in = tile_in[i % 2].reshape(side * side, tile_in.shape[3])
-            tile_out[i % 2] = dot(swap, rows_in).astype(BF16).reshape(tile_out.shape[1:])
+                store(i - depth).wait()
+
+            rows_in = tile_in[i % depth].reshape(side * side, tile_in.shape[3])
+            tile_out[i % depth] = dot(swap, rows_in).astype(BF16).reshape(tile_out.shape[1:])
             store(i).start()
             return carry
 
@@ -278,8 +280,8 @@
             for k in range(n_k):
                 z_hop(k, origin, 0).wait_send()
 
-    store(2 * n_tiles - 2).wait()
-    store(2 * n_tiles - 1).wait()
+    for i in range(depth):
+        store(2 * n_tiles - depth + i).wait()
     for copy in stores:
         copy.wait()
 
@@ -306,10 +308,10 @@
             pltpu.VMEM((n_k, width, width), BF16),
             pltpu.VMEM(small, BF16),
             pltpu.VMEM((n_h, n_k, rows, wide), BF16),
-            pltpu.VMEM((2, 16, 16, hidden), BF16),
-            pltpu.VMEM((2, 16, 16, hidden), BF16),
+            pltpu.VMEM((4, 16, 16, hidden), BF16),
+            pltpu.VMEM((4, 16, 16, hidden), BF16),
             dma((n_k, n_h, 2)), dma((n_k, n_h)), dma((2, n_k + 1)), dma((2, n_k + 1)),
-            dma((2, 2 * (n_k + 1))), dma((2, 4 * (n_k + 1))), dma((2, 2)), dma((n_k + 1,)),
+            dma((2, 2 * (n_k + 1))), dma((2, 4 * (n_k + 1))), dma((2, 4)), dma((n_k + 1,)),
         ],
         compiler_params=pltpu.CompilerParams(
             collective_id=3, has_side_effects=True, vmem_limit_bytes=VMEM_BYTES
@@ -799,7 +801,7 @@
 def weight_grads(slots_0, act_0, slots_1, act_1):
     experts, images, rows = slots_0.shape
     hidden = act_0.shape[2]
-    group, d_block = 8, 32
+    group, d_block = 8, 96
     last = experts // group - 1
 
     def early(m, g, d):
@@ -991,7 +993,6 @@
         back, output = lax.optimization_barrier((back, output))
         output = lax.all_gather(output, "heads", axis=0, tiled=True)
         grad_slot_in = from_blocks(back, sizes).astype(BF16)
-        experts_grad = weight_grads(slot_in, grad_pre, grad_slot, activated)
         grad_slot_sum = jnp.sum(grad_slot.astype(F32), axis=1)
     else:
         output = lax.all_gather(output, "heads", axis=0, tiled=True)
@@ -1047,13 +1048,18 @@
         grad_normed_one, unit_one, inverse_one, scales[0]
     )
     input_grad = (grad_hidden + grad_input_norm).astype(BF16)
+    if sizes is not None:
+        input_grad, output = lax.optimization_barrier((input_grad, output))
     input_grad = lax.all_gather(input_grad, "heads", axis=0, tiled=True)
     attn_grad = jnp.concatenate((proj_grad, out_weight_grad[None]), axis=0)
     norms = jnp.stack((scale_one_grad, scale_two_grad, bias_one_grad, bias_two_grad))
     if sizes is not None:
         small = jnp.concatenate((phi_grad, norms.T), axis=1)
         small = jnp.pad(small, ((0, 0), (0, 128 - small.shape[1]))).astype(BF16)
-        summed = reduce_grads(sizes, attn_grad.astype(BF16), small)
+        attn_grad, grad_pre = lax.optimization_barrier((attn_grad.astype(BF16), grad_pre))
+        experts_grad = weight_grads(slot_in, grad_pre, grad_slot, activated)
+        attn_grad, experts_grad = lax.optimization_barrier((attn_grad, experts_grad))
+        summed = reduce_grads(sizes, attn_grad, small)
         attn_grad = summed[:, :, :block]
         phi_grad = summed[0, :, block : block + slot]
         norms = summed[0, :, block + slot : block + slot + 4].T

time: 411 us -> 387 us (0.942)
  Pallas kernels: 272 us -> 242 us
  waiting for transfers between devices: 0.04 us -> 9.06 us
    pallas_call x1, Pallas kernels: 59.4 us -> 40.5 us  [reduce_grads(): pl.pallas_call(partial(reduce_kernel, sizes), out_shape=jax.ShapeDtypeStr...]
    all_gather x1, waiting for transfers between devices: 0.01 us -> 9.02 us  [shards(): output = lax.all_gather(output, 'heads', axis=0, tiled=True)]
    pallas_call x1, Pallas kernels: 28.2 us -> 21.1 us  [weight_grads(): pl.pallas_call(weight_grad_kernel, grid=(2, experts // group, rows // d_b...]
    another operation x4, local copies, waits for them, and re-layouts: 1.82 us -> 6.17 us  [shards(): query, keyed, valued = projected.reshape(3, own, seq_len, n_heads, HEAD_DIM)]
    unnamed x95 -> x103, local copies, waits for them, and re-layouts: 15 us -> 12.7 us
  transfers between devices with their start and end apart: 2 -> 2, of which waited for: 0 -> 1; matrix products, arithmetic and copies ran while one was open for 15% -> 15% of each run, Pallas kernels for 22% -> 16%
where the time goes in v1:
time: 387 us; the launch traced here: 381 us
  Pallas kernels  242 us (63%)
  matrix products  52.1 us (13%)
  local copies, waits for them, and re-layouts  45.4 us (12%)
  other arithmetic  17.5 us (5%)
  between operations  15.1 us (4%)
  waiting for transfers between devices  9.06 us (2%)
    pallas_call x2, Pallas kernels, expert_pass(): pl.pallas_call(partial(expert_kernel, sizes, backward), out_shape=outs, i...  137 us
    pallas_call x1, Pallas kernels, gather_weights(): pl.pallas_call(partial(gather_kernel, sizes), out_shape=(jax.ShapeDtypeSt...  43.4 us
    pallas_call x1, Pallas kernels, reduce_grads(): pl.pallas_call(partial(reduce_kernel, sizes), out_shape=jax.ShapeDtypeStr...  40.5 us
    pallas_call x1, Pallas kernels, weight_grads(): pl.pallas_call(weight_grad_kernel, grid=(2, experts // group, rows // d_b...  21.1 us
    unnamed x103, local copies, waits for them, and re-layouts  12.7 us
    all_gather x1, waiting for transfers between devices, shards(): output = lax.all_gather(output, 'heads', axis=0, tiled=True)  9.02 us
  transfers between devices with their start and end apart: 2, of which 1 were waited for; matrix products, arithmetic and copies ran while one was open for 15% of the time, Pallas kernels for 16%

profile of v1, /device:TPU:0, one launch (start us, length us, event | category | flops | bytes accessed | tf_op | source)
XLA Modules:
  0.0 381.3 jit_solution(12841397380109735464)
XLA Ops:
  8.1 0.8 copy.196
  8.8 0.8 copy.197
  9.6 0.8 reshape.124
  10.4 1.7 fusion.73.packet
  12.8 43.4 %gather_weights.1 = (bf16[4,768,768]{2,1,0:T(8,128)(2,1)}, bf16[768,256]{1,0:T(8,128)(2,1)}, bf16[2,16,192,1536]{3,2,1,0:T(8,128)(2,1)}) custom-call(bf16[4,96,256]{2,1,0:T(8,128)(2,1)} %fusion.73.packet, bf16[96,256]{1,0:T(8,128)(2,1)} %fusion.88.extra, bf16[192,2,16,1536]{3,2,1,0:T(8,128)(2,1)} %experts.1), custom_call_target="tpu_custom_call" | custom-call | tf_op jit(solution)/shard_map/gather_weights/pallas_call | solution.py:298
  56.3 1.2 convert_bitcast_fusion.3
  57.5 0.9 convert_bitcast_fusion.1
  58.4 3.8 constant_dynamic-slice_fusion.2
  63.5 1.8 convert_bitcast_fusion
  65.4 1.1 fusion.99
  66.5 1.3 copy.199
  67.9 2.5 copy.200
  70.4 1.2 copy.198
  71.6 5.3 %fusion.101 = (f32[2,12,197]{2,1,0:T(8,128)S(1)}, f32[2,12,197,197]{2,3,1,0:T(8,128)}) fusion(bf16[2,197,12,64]{1,3,2,0:T(8,128)(2,1)S(1)} %bitcast.137, bf16[2,197,12,64]{1,3,2,0:T(8,128)(2,1)} %bitcast.139), kind=kOutput, calls=%fused_computation.158 | convolution fusion | flops 122015688 | bytes 4954944 | tf_op jit(solution)/shard_map/sub | solution.py:946
  76.8 3.3 convolution_convert_fusion.1
  80.1 2.5 fusion.102
  83.6 0.7 fusion.104
  85.1 2.0 convolution_convert_fusion.3
  87.1 1.9 reshape.128
  89.0 1.1 copy.266
  90.0 0.9 reshape.129.refs_0_
  91.8 68.1 %experts_ahead.1 = (bf16[16,64,192]{2,1,0:T(8,128)(2,1)}, bf16[16,64,1536]{2,1,0:T(8,128)(2,1)}, f32[8,64,1536]{2,1,0:T(8,128)}, bf16[2,32,16,192]{3,2,1,0:T(8,128)(2,1)}) custom-call(bf16[4,4,2,16,192]{4,3,2,1,0:T(8,128)(2,1)} %reshape.129.refs_0_, bf16[2,16,192,1536]{3,2,1,0:T(8,128)(2,1)} %get-tuple-element.30.refs_1_, f32[16,1,1536]{2,1,0:T(1,128)} %broadcast_in_dim.8.refs_2_), custom_call_target="tpu_custom_call" | custom-call | flops 2415919104 | bytes 18874368 | tf_op jit(solution)/shard_map/experts_ahead/pallas_call | solution.py:745
  159.9 1.3 reshape.133
  161.3 1.3 reduce_sum.196
  162.5 1.4 copy.207
  164.2 1.1 copy.208
  165.4 1.2 convolution_convert_fusion.4
  167.0 0.9 reshape.127.refs_0_
  167.9 2.2 fusion.28
  170.1 68.9 %experts_back.1 = (bf16[16,64,192]{2,1,0:T(8,128)(2,1)}, bf16[16,64,1536]{2,1,0:T(8,128)(2,1)}, bf16[2,32,16,192]{3,2,1,0:T(8,128)(2,1)}, f32[16,384]{1,0:T(8,128)}) custom-call(bf16[4,4,2,16,192]{4,3,2,1,0:T(8,128)(2,1)} %reshape.127.refs_0_, bf16[2,16,192,1536]{3,2,1,0:T(8,128)(2,1)} %get-tuple-element.30.refs_1_, f32[8,64,1536]{2,1,0:T(8,128)} %get-tuple-element.31.refs_2_), custom_call_target="tpu_custom_call" | custom-call | flops 2415919104 | bytes 18874368 | tf_op jit(solution)/shard_map/experts_back/pallas_call | solution.py:745
  239.2 1.0 fusion.57
  240.4 1.2 reduce
  241.5 1.2 copy.209
  242.8 0.9 convert_element_type.171
  243.7 2.6 fusion.91
  246.3 2.4 fusion.51
  248.8 3.3 multiply_reduce_fusion.2
  252.1 1.7 multiply_add_fusion
  253.9 1.0 copy-done
  254.9 1.9 convolution_convert_fusion.2
  257.1 0.8 copy-done.14
  258.0 4.2 %multiply_reduce_fusion = (f32[2,12,197]{2,1,0:T(8,128)S(1)}, f32[2,12,197,197]{2,3,1,0:T(8,128)S(1)}) fusion(f32[2,12,197,197]{2,3,1,0:T(8,128)} %get-tuple-element.123, f32[2,12,197]{2,1,0:T(8,128)S(1)} %copy-done.30, bf16[2,197,12,64]{1,3,2,0:T(8,128)(2,1)S(1)} %bitcast.152, bf16[2,197,12,64]{1,3,2,0:T(8,128)(2,1)S(1)} %bitcast.151), kind=kOutput, calls=%fused_computation.7 | convolution fusion | flops 122010768 | bytes 8699520 | tf_op jit(solution)/shard_map/nqhe,nkhe->nhqk/dot_general | solution.py:1038
  262.2 0.8 multiply_convert_fusion
  263.3 1.4 multiply_convert_fusion.2
  264.7 2.2 copy.215
  267.0 2.9 multiply_convert_fusion.1
  269.9 2.3 copy.216
  272.2 3.3 convolution_convert_fusion
  275.5 1.1 copy.217
  276.6 4.4 %fusion.36 = (bf16[768]{0:T(1024)(128)(2,1)S(1)}, f32[2,197]{1,0:T(2,128)S(1)}, f32[2,197]{1,0:T(2,128)S(1)}, bf16[768]{0:T(1024)(128)(2,1)S(1)}, f32[2,197,768]{2,1,0:T(8,128)S(1)}) fusion(f32[2,197]{1,0:T(2,128)S(1)} %copy-done.39, f32[2,197]{1,0:T(2,128)S(1)} %copy-done.35, bf16[2,197,768]{2,0,1:T(2,128)(2,1)S(1)} %get-tuple-element.136, ...), kind=kOutput, calls=%fused_computation.50 | convolution fusion | flops 1399183104 | bytes 7200928 | tf_op jit(solution)/shard_map/knsc,kdc->nsd/dot_general | solution.py:1046
  281.1 1.3 fusion.35
  282.4 9.0 %all-gather.3.cloned.1.call-done = bf16[8,197,768]{2,1,0:T(8,128)(2,1)} async-done(((bf16[2,197,768]{2,1,0:T(8,128)(2,1)}), bf16[8,197,768]{2,1,0:T(8,128)(2,1)}) %all-gather.3.cloned.1.call-update) | async-done | bytes 2420752 | tf_op jit(solution)/shard_map/all_gather | solution.py:994
  291.5 1.4 fusion.44
  293.3 2.1 fusion.27
  295.4 2.5 fusion.8
  297.9 2.5 pad_maximum_fusion.grads
  300.4 21.1 %weight_grads.1 = f32[192,2,16,1536]{3,2,1,0:T(8,128)} custom-call(bf16[16,64,192]{2,1,0:T(8,128)(2,1)} %get-tuple-element.40.slots_0, bf16[16,64,1536]{2,1,0:T(8,128)(2,1)} %get-tuple-element.41.act_0, bf16[16,64,192]{2,1,0:T(8,128)(2,1)} %get-tuple-element.42.slots_1, bf16[16,64,1536]{2,1,0:T(8,128)(2,1)} %get-tuple-element.43.act_1), custom_call_target="tpu_custom_call" | custom-call | flops 1207959552 | bytes 37748736 | tf_op jit(solution)/shard_map/weight_grads/pallas_call | solution.py:814
  321.5 0.8 fusion.74.small
  322.3 40.5 %reduce_grads.1 = f32[4,96,256]{2,1,0:T(8,128)} custom-call(bf16[4,768,768]{2,1,0:T(8,128)(2,1)} %pad_maximum_fusion.grads, bf16[768,128]{1,0:T(8,128)(2,1)} %fusion.74.small), custom_call_target="tpu_custom_call" | custom-call | tf_op jit(solution)/shard_map/reduce_grads/pallas_call | solution.py:474
  362.8 0.9 slice_bitcast_fusion.1
  365.0 0.9 slice_bitcast_fusion
  367.4 1.9 copy.222
  369.3 3.6 copy.223
  372.9 0.7 copy.270
  (140 shorter events, 10.9 us)
Async XLA Ops:
  7.2 284.2 %all-gather.3.cloned.1.call-start = ((), (), s32[]{:S(2)}) async-start(), calls=%async_computation | async-start | bytes 3072000 | tf_op jit(solution)/shard_map/all_gather | solution.py:994
  56.2 1.3 copy-start.2
  58.4 5.1 %copy-start.21 = (bf16[4,768,768]{2,1,0:T(8,128)(2,1)S(1)}, bf16[4,768,768]{2,1,0:T(8,128)(2,1)}, u32[]{:S(2)}) copy-start(bf16[4,768,768]{2,1,0:T(8,128)(2,1)} %get-tuple-element.28) | copy-start | bytes 14155780
  62.4 2.9 copy-start.34
  62.8 2.6 copy-start.38
  63.5 1.9 copy-start.36
  63.5 1.9 copy-start.40
  63.5 19.4 %copy-start.23 = (f32[768]{0:T(1024)}, f32[768]{0:T(1024)S(1)}, u32[]{:S(2)}) copy-start(f32[768]{0:T(1024)S(1)} %get-tuple-element.135) | copy-start | bytes 9220
  67.9 3.7 copy-start.4
  76.8 3.3 copy-start.29
  80.1 2.5 copy-start.44
  82.7 0.6 copy-start.25
  83.0 0.6 copy-start.27
  83.2 3.8 %copy-start.6 = (bf16[2,197,768]{2,1,0:T(8,128)(2,1)}, bf16[2,197,768]{2,1,0:T(8,128)(2,1)S(1)}, u32[]{:S(2)}) copy-start(bf16[2,197,768]{2,1,0:T(8,128)(2,1)S(1)} %add_convert_fusion) | copy-start | bytes 1815556
  83.6 1.5 copy-start.13
  84.4 6.6 %copy-start.42 = (f32[2,64]{1,0:T(2,128)}, f32[2,64]{1,0:T(2,128)S(1)}, u32[]{:S(2)}) copy-start(f32[2,64]{1,0:T(2,128)S(1)} %get-tuple-element.128) | copy-start | bytes 1540
  85.1 80.3 %copy-start.32 = (f32[2,197]{1,0:T(2,128)}, f32[2,197]{1,0:T(2,128)S(1)}, u32[]{:S(2)}) copy-start(f32[2,197]{1,0:T(2,128)S(1)} %get-tuple-element.126) | copy-start | bytes 4732
  85.1 5.9 %copy-start.12 = (f32[768,64]{1,0:T(8,128)S(1)}, f32[768,64]{1,0:T(8,128)}, u32[]{:S(2)}) copy-start(f32[768,64]{1,0:T(8,128)} %get-tuple-element.117) | copy-start | bytes 589828
  239.0 1.2 copy-start.20
  239.0 130.3 %all-gather.5.cloned.1.call-start = ((), (), s32[]{:S(2)}) async-start(), calls=%async_computation.1 | async-start | bytes 3072000 | tf_op jit(solution)/shard_map/all_gather | solution.py:1053
  240.3 3.3 copy-start.43
  241.5 4.8 %copy-start.7 = (bf16[2,197,768]{2,1,0:T(8,128)(2,1)S(1)}, bf16[2,197,768]{2,1,0:T(8,128)(2,1)}, u32[]{:S(2)}) copy-start(bf16[2,197,768]{2,1,0:T(8,128)(2,1)} %copy-done.6) | copy-start | bytes 1815556
  246.3 2.5 copy-start.3
  246.3 2.5 copy-start.24
  246.3 2.5 copy-start.26
  246.3 2.5 copy-start.28
  246.3 2.5 copy-start.33
  253.9 1.0 copy-start
  256.8 1.1 copy-start.14
  256.8 1.1 copy-start.30
  257.1 5.0 %copy-start.15 = (bf16[2,197,768]{1,2,0:T(8,128)(2,1)}, bf16[2,197,768]{1,2,0:T(8,128)(2,1)S(1)}, u32[]{:S(2)}) copy-start(bf16[2,197,768]{1,2,0:T(8,128)(2,1)S(1)} %copy.211) | copy-start | bytes 1815556
  257.1 5.0 %slice-start = ((s8[4915200]{0:T(1024)(128)(4,1)}), s8[4194304]{0:T(1024)(128)(4,1)S(1)}, s32[]{:S(2)}) async-start(s8[4915200]{0:T(1024)(128)(4,1)} %bitcast.135), calls=%async_computation.2 | async-start | bytes 8388608
  258.0 4.2 %slice-start.1 = ((s8[4915200]{0:T(1024)(128)(4,1)}), s8[720896]{0:T(1024)(128)(4,1)S(1)}, s32[]{:S(2)}) async-start(s8[4915200]{0:T(1024)(128)(4,1)} %bitcast.135), calls=%async_computation.3 | async-start | bytes 1441792
  262.2 1.1 copy-start.5
  269.9 2.3 copy-start.16
  275.5 1.1 copy-start.17
  275.5 1.1 copy-start.35
  275.5 1.1 copy-start.37
  275.5 1.1 copy-start.39
  276.6 4.5 %copy-start.1 = (f32[2,197,768]{2,1,0:T(8,128)S(1)}, f32[2,197,768]{2,1,0:T(8,128)}, u32[]{:S(2)}) copy-start(f32[2,197,768]{2,1,0:T(8,128)} %copy-done) | copy-start | bytes 3631108
  281.1 10.3 %copy-start.8 = (bf16[2,197,768]{2,1,0:T(8,128)(2,1)S(1)}, bf16[2,197,768]{2,1,0:T(8,128)(2,1)}, u32[]{:S(2)}) copy-start(bf16[2,197,768]{2,1,0:T(8,128)(2,1)} %copy-done.6) | copy-start | bytes 1815556
  281.1 10.3 %copy-start.22 = (f32[2,197,64]{1,2,0:T(8,128)S(1)}, f32[2,197,64]{1,2,0:T(8,128)}, u32[]{:S(2)}) copy-start(f32[2,197,64]{1,2,0:T(8,128)} %fusion.51) | copy-start | bytes 302596
  293.3 2.1 copy-start.18
  293.3 2.1 copy-start.19
  293.3 2.1 copy-start.41
  322.3 44.3 %copy-start.10 = (bf16[16,64,192]{2,1,0:T(8,128)(2,1)S(1)}, bf16[16,64,192]{2,1,0:T(8,128)(2,1)}, u32[]{:S(2)}) copy-start(bf16[16,64,192]{2,1,0:T(8,128)(2,1)} %get-tuple-element.42.slots_1) | copy-start | bytes 1179652
  322.3 45.1 %copy-start.9 = (bf16[8,197,768]{2,1,0:T(8,128)(2,1)S(1)}, bf16[8,197,768]{2,1,0:T(8,128)(2,1)}, u32[]{:S(2)}) copy-start(bf16[8,197,768]{2,1,0:T(8,128)(2,1)} %all-gather.3.cloned.1.call-done) | copy-start | bytes 7262212
  369.3 3.6 copy-start.11
  369.3 4.4 %copy-start.31 = (f32[16,384]{1,0:T(8,128)S(1)}, f32[16,384]{1,0:T(8,128)}, u32[]{:S(2)}) copy-start(f32[16,384]{1,0:T(8,128)} %get-tuple-element.154) | copy-start | bytes 73732
Sparse Core Ops, SparseCore 0:
  239.1 52.2 all-gather.2
  293.6 52.2 all-gather.4

commit v2 on v1

--- a/solution.py
+++ b/solution.py
@@ -493,14 +493,15 @@
 
 def expert_kernel(sizes, backward, *refs):
     if backward:
-        (blocks, weights, gate, slots_out, act_out, back_out, bias_out,
+        (blocks, weights, gate, output, slots_out, act_out, back_out, bias_out, sum_out, gathered,
          w_a, w_b, gate_v, sums, slots, act, core_out, core_in, x_out, x_in, land, leave, back, land_back,
          w_sem, o_sem, in_sems, back_sems, core_sems, x_sems, act_sems, b_sems,
+         g_send, g_recv, g_sem,
          bias_all, bias_send, bias_land) = refs
     else:
         (blocks, weights, gate, slots_out, act_out, gate_out, back_out,
          w_a, w_b, sums, slots, act, core_out, core_in, x_out, x_in, land, leave, back, land_back,
-         w_sem, o_sem, in_sems, back_sems, core_sems, x_sems, act_sems) = refs
+         w_sem, o_sem, in_sems, back_sems, core_sems, x_sems, act_sems, bias) = refs
     peers = Peers(sizes)
     s, h, t = peers.at
     n_s, n_h, n_t = sizes
@@ -563,6 +564,62 @@
                     c * few : (c + 1) * few
                 ]
 
+    if backward:
+        own_images = output.shape[0]
+        line = [(s, lax.rem(h + d, n_h), t) for d in range(n_h)]
+        g_own = pltpu.make_async_copy(output, gathered.at[pl.ds(h * own_images, own_images)], g_sem)
+        g_own.start()
+
+        def z_hop(i, origin, up, source=None):
+            there = gathered.at[origin * own_images + i]
+            return remote(
+                there if source is None else source, there,
+                g_send.at[i, origin, up], g_recv.at[i, origin], line[1] if up else line[n_h - 1],
+            )
+
+        def relay(wave):
+            for d in range(1, n_h):
+                i = wave - d + 1
+                if 0 <= i < own_images:
+                    @pl.when(h >= d)
+                    def _():
+                        z_hop(i, h - d, 1).wait_recv()
+
+                        @pl.when(h < n_h - 1)
+                        def _():
+                            z_hop(i, h - d, 1).start()
+
+                    @pl.when(h + d < n_h)
+                    def _():
+                        z_hop(i, h + d, 0).wait_recv()
+
+                        @pl.when(h > 0)
+                        def _():
+                            z_hop(i, h + d, 0).start()
+
+        def gather_output():
+            for i in range(own_images):
+                @pl.when(h < n_h - 1)
+                def _():
+                    z_hop(i, h, 1, output.at[i]).start()
+
+                @pl.when(h > 0)
+                def _():
+                    z_hop(i, h, 0, output.at[i]).start()
+    else:
+        piece, count = 6 * 64, act.shape[2] // (6 * 64)
+        row = lax.broadcasted_iota(jnp.int32, (6 * 128, piece), 0)
+        column = lax.broadcasted_iota(jnp.int32, (6 * 128, piece), 1)
+        lane = row % 128
+        place = (lane < 64) & (column == (row // 128) * 64 + lane)
+        place = place.astype(F32).astype(BF16)
+        for m in range(count):
+            first = (t * count + m) * 96
+            lines = [
+                gate[pl.ds(pl.multiple_of(first + j * 16, 16), 16), 128:256] for j in range(6)
+            ]
+            bias[:, m * piece : (m + 1) * piece] = dot(jnp.concatenate(lines, axis=1), place)
+
     receive(0)
     loads[0].wait()
 
@@ -601,6 +658,8 @@
 
     each(first_sums, few, 0)
     receive(1)
+    if backward:
+        gather_output()
     each(first_sums, half, few)
     meet(half - 1)
     loads[1].wait()
@@ -616,7 +675,7 @@
         if backward:
             act[own + j] = (value * gate_v[j]).astype(BF16)
         else:
-            value = value + gate[own + j]
+            value = value + bias[pl.ds(own + j, 1), :]
             cumulative = 0.5 + 0.5 * lax.erf(value * 0.7071067811865476)
             act[own + j] = (value * cumulative).astype(BF16)
             sums[j] = cumulative + value * (
@@ -629,6 +688,12 @@
         def _():
             act_in(j - 1).wait_recv()
             second(other + j - 1)
+
+        if backward:
+            for wave in range(3):
+                @pl.when(j == 3 + 2 * wave)
+                def _():
+                    relay(wave)
 
     def back_copy(p, k):
         place = peers.step(k, 1)
@@ -679,6 +744,11 @@
 
         each(bias_row, 2 * half, 0)
 
+        def slot_row(e):
+            sum_out[pl.ds(e, 1), :] = jnp.sum(slots[e].astype(F32), axis=0, keepdims=True)
+
+        each(slot_row, 2 * half, 0)
+
         def piece(for_t):
             return bias_all[:, pl.ds(pl.multiple_of((core * n_t + for_t) * width, 128), width)]
 
@@ -692,6 +762,30 @@
     back_out[...] = land_back[...]
     for store in stores:
         store.wait()
+    if backward:
+        relay(3)
+        g_own.wait()
+        for origin in range(n_h):
+            @pl.when((origin < h) & (h < n_h - 1))
+            def _():
+                for i in range(own_images):
+                    z_hop(i, origin, 1).wait_send()
+
+            @pl.when((origin > h) & (h > 0))
+            def _():
+                for i in range(own_images):
+                    z_hop(i, origin, 0).wait_send()
+
+        @pl.when(h < n_h - 1)
+        def _():
+            for i in range(own_images):
+                z_hop(i, h, 1, output.at[i]).wait_send()
+
+        @pl.when(h > 0)
+        def _():
+            for i in range(own_images):
+                z_hop(i, h, 0, output.at[i]).wait_send()
+
     for p in range(2):
         each(lambda k: block_out(p, k).wait_send())
         each(lambda k: back_copy(p, k).wait_send())
@@ -699,7 +793,7 @@
         each(lambda j: copy(j).wait_send(), half, 0)
 
 
-def expert_pass(sizes, backward, blocks, weights, gate, bias_width=0):
+def expert_pass(sizes, backward, blocks, weights, gate, output=None, bias_width=0):
     _, experts, rows, hidden = weights.shape
     devices = sizes[0] * sizes[1] * sizes[2]
     images = 2 * devices
@@ -711,9 +805,14 @@
     gate_shape = (half, images, hidden)
     returned = jax.ShapeDtypeStruct((2, devices, experts, rows), BF16)
     if backward:
-        operands, in_specs = (blocks, weights, gate), [vmem, hbm, hbm]
-        outs = (slots, act, returned, jax.ShapeDtypeStruct((experts, bias_width), F32))
-        out_specs = (vmem, hbm, vmem, vmem)
+        operands, in_specs = (blocks, weights, gate, output), [vmem, hbm, hbm, hbm]
+        outs = (
+            slots, act, returned,
+            jax.ShapeDtypeStruct((experts, bias_width), F32),
+            jax.ShapeDtypeStruct((experts, rows), F32),
+            jax.ShapeDtypeStruct((sizes[1] * output.shape[0], *output.shape[1:]), BF16),
+        )
+        out_specs = (vmem, hbm, vmem, vmem, vmem, hbm)
     else:
         operands, in_specs = (blocks, weights, gate), [vmem, hbm, vmem]
         outs = (slots, act, jax.ShapeDtypeStruct(gate_shape, F32), returned)
@@ -737,11 +836,13 @@
     ]
     if backward:
         scratch += [
-            dma((2,)),
+            dma((2,)), dma((output.shape[0], sizes[1], 2)), dma((output.shape[0], sizes[1])), dma,
             pltpu.VMEM((experts, hidden), F32),
             pltpu.VMEM((experts, bias_width), F32),
             pltpu.VMEM((experts, bias_width), F32),
         ]
+    else:
+        scratch.append(pltpu.VMEM((experts, hidden), F32))
     return pl.pallas_call(
         partial(expert_kernel, sizes, backward),
         out_shape=outs,
@@ -835,6 +936,357 @@
     )(slots_0, act_0, slots_1, act_1)
 
 
+def dot_r(a, b):
+    return lax.dot_general(a, b, (((0,), (0,)), ((), ())), preferred_element_type=F32)
+
+
+def row_of(shape, axis):
+    return lax.broadcasted_iota(jnp.int32, shape, axis)
+
+
+def one_hot(mask):
+    return mask.astype(F32).astype(BF16)
+
+
+def order_matrix(n_h, few, back):
+    n = n_h * 8 * few
+    shape = (n, n)
+    blocked, natural = row_of(shape, 1 if back else 0), row_of(shape, 0 if back else 1)
+    f, half, image = blocked % few, (blocked // few) % 2, (blocked // (2 * few)) % 2
+    group = blocked // (4 * few)
+    if back:
+        part, h = group // n_h, group % n_h
+    else:
+        h, part = group // 2, group % 2
+    expert = ((h * 2 + half) * 2 + part) * few + f
+    return one_hot(natural == image * (4 * n_h * few) + expert)
+
+
+def norm_parts(x, scale, shift, live):
+    centered = x - jnp.mean(x, axis=-1, keepdims=True)
+    inverse = lax.rsqrt(jnp.mean(centered * centered, axis=-1, keepdims=True) + epsilon)
+    unit = centered * inverse
+    return unit * scale + shift, unit, inverse
+
+
+def norm_back(grad, unit, inverse, scale):
+    scaled = grad * scale
+    average = jnp.mean(scaled, axis=-1, keepdims=True)
+    projection = jnp.mean(scaled * unit, axis=-1, keepdims=True)
+    return (
+        inverse * (scaled - average - unit * projection),
+        jnp.sum(grad * unit, axis=0, keepdims=True),
+        jnp.sum(grad, axis=0, keepdims=True),
+    )
+
+
+def norm_rows(small):
+    return jnp.swapaxes(small[:, 128:].astype(F32), 0, 1)[64:68]
+
+
+def slots_to_blocks(slots, blocks, columns, joined, order):
+    n_h, n_s = blocks.shape[:2]
+    turned = dot(order, slots).astype(BF16)
+    wide = joined.shape[1] // 2
+    for s in range(0, n_s, 2):
+        lanes = dot(turned[:, s * columns : (s + 2) * columns], joined).astype(BF16)
+        for h in range(n_h):
+            for p in range(2):
+                rows = (h * 2 + p) * 16
+                for e in range(2):
+                    blocks[h, s + e, p] = lanes[rows : rows + 16, e * wide : e * wide + columns]
+
+
+def blocks_to_slots(back, sizes, order, pair, padded):
+    n_s, n_h, n_t = sizes
+    columns = back.shape[3]
+    both = jnp.concatenate([order] * n_t, axis=1)
+    results = []
+    for s in range(n_s):
+        rows = jnp.concatenate(
+            [
+                back[p, (s * n_h + h) * n_t + t]
+                for t in range(n_t)
+                for p in range(2)
+                for h in range(n_h)
+            ],
+            axis=0,
+        )
+        padded[s % 2, :, :columns] = dot(both, rows)
+        if s % 2:
+            value = jnp.concatenate([padded[0], padded[1]], axis=1)
+            high = value.astype(BF16)
+            rest = (value - high.astype(F32)).astype(BF16)
+            results.append(dot(high, pair) + dot(rest, pair))
+    return jnp.concatenate(results, axis=1)
+
+
+def live_rows(shape, length):
+    return row_of(shape, 0) < length
+
+
+def ahead_kernel(
+    length, tokens, small, w_hbm, blocks, normed_1, query, keyed, valued, context, hidden, normed_2,
+    dispatch_out, combine_out, w, joined, order, w_sem,
+):
+    n, rows, width = tokens.shape
+    keys = keyed.shape[1]
+    loads = [pltpu.make_async_copy(w_hbm.at[k], w.at[k], w_sem.at[k]) for k in range(4)]
+    for load in loads:
+        load.start()
+    norms = norm_rows(small)
+    live = live_rows((rows, 1), length)
+    for i in range(n):
+        value, _, _ = norm_parts(tokens[i].astype(F32), norms[0:1], norms[2:3], live)
+        normed_1[i] = jnp.where(live, value, 0.0).astype(BF16)
+    joined[...] = pair_matrix(blocks.shape[4], joined.shape[1] // 2, True)
+    order[...] = order_matrix(blocks.shape[0], 4, False)
+    flat = (n * rows, width)
+    for k, target in enumerate((query, keyed, valued)):
+        loads[k].wait()
+        value = dot(normed_1[...].reshape(flat), w[k]).astype(BF16).reshape(n, rows, width)
+        if k == 0:
+            target[...] = value
+        else:
+            target[:, :rows] = value
+            target[:, rows:] = jnp.zeros((n, keys - rows, width), BF16)
+    factor = HEAD_DIM ** (-0.5)
+    pairs = width // 128
+    lane = row_of((rows, 128), 1)
+    shown = row_of((rows, keys), 1) < length
+
+    def attend(step, carry):
+        i = step // pairs
+        lanes = pl.ds(pl.multiple_of((step % pairs) * 128, 128), 128)
+        q, k, v = query[i, :, lanes], keyed[i, :, lanes], valued[i, :, lanes]
+        parts = []
+        for a in range(2):
+            mine = (lane < 64) if a == 0 else (lane >= 64)
+            scores = dot_t(jnp.where(mine, q, jnp.zeros_like(q)), k) * factor
+            scores = jnp.where(shown, scores, -1e30)
+            exponent = jnp.exp(scores - jnp.max(scores, axis=-1, keepdims=True))
+            probs = exponent / jnp.sum(exponent, axis=-1, keepdims=True)
+            parts.append(dot(probs.astype(BF16), v))
+        context[i, :, lanes] = jnp.where(lane < 64, parts[0], parts[1]).astype(BF16)
+        return carry
+
+    lax.fori_loop(0, n * pairs, attend, 0, unroll=2)
+    loads[3].wait()
+    attended = dot_t(context[...].reshape(flat), w[3]).reshape(n, rows, width)
+    for i in range(n):
+        value = tokens[i].astype(F32) + attended[i]
+        hidden[i] = value
+        value, _, _ = norm_parts(value, norms[1:2], norms[3:4], live)
+        normed_2[i] = jnp.where(live, value, 0.0).astype(BF16)
+    logits = dot(normed_2[...].reshape(flat), small[:, :128]).reshape(n, rows, 128)
+    experts = row_of((rows, 128), 1) < 64
+    slots = []
+    for i in range(n):
+        here = logits[i]
+        down = jnp.where(live, here, -1e30)
+        exponent = jnp.exp(down - jnp.max(down, axis=0, keepdims=True))
+        dispatch = exponent / jnp.sum(exponent, axis=0, keepdims=True)
+        dispatch = jnp.where(experts, dispatch, 0.0)
+        across = jnp.where(experts, here, -1e30)
+        exponent = jnp.exp(across - jnp.max(across, axis=1, keepdims=True))
+        combine = exponent / jnp.sum(exponent, axis=1, keepdims=True)
+        dispatch_out[i] = dispatch
+        combine_out[i] = combine
+        slots.append(dot_r(dispatch.astype(BF16), normed_2[i])[:64].astype(BF16))
+    slots_to_blocks(
+        jnp.concatenate(slots, axis=0), blocks, blocks.shape[4], joined[...], order[...]
+    )
+
+
+def tokens_ahead(sizes, length, tokens, small, weights):
+    n, rows, width = tokens.shape
+    keys = 256
+    vmem = pl.BlockSpec(memory_space=pltpu.VMEM)
+    shape = jax.ShapeDtypeStruct
+    wide = (n, keys, width)
+    thin = shape((n, rows, 128), F32)
+    return pl.pallas_call(
+        partial(ahead_kernel, length),
+        out_shape=(
+            shape((sizes[1], sizes[0], 2, 16, width // sizes[0]), BF16),
+            shape(tokens.shape, BF16), shape(tokens.shape, BF16), shape(wide, BF16),
+            shape(wide, BF16), shape(tokens.shape, BF16), shape(tokens.shape, F32),
+            shape(tokens.shape, BF16), thin, thin,
+        ),
+        in_specs=[vmem, vmem, pl.BlockSpec(memory_space=pl.ANY)],
+        out_specs=(vmem,) * 10,
+        scratch_shapes=[
+            pltpu.VMEM(weights.shape, BF16),
+            pltpu.VMEM((2 * width // sizes[0], 512), BF16),
+            pltpu.VMEM((128, 128), BF16),
+            pltpu.SemaphoreType.DMA((4,)),
+        ],
+        compiler_params=pltpu.CompilerParams(vmem_limit_bytes=VMEM_BYTES),
+        name="tokens_ahead",
+    )(tokens, small, weights)
+
+
+def middle_kernel(
+    sizes, back, small, combine, hidden, cotangent, output, blocks, grad_logits, padded
+):
+    n, rows, _ = hidden.shape
+    columns = back.shape[3]
+    padded[...] = jnp.zeros_like(padded)
+    pair = pair_matrix(columns, padded.shape[2], False)
+    joined = pair_matrix(columns, padded.shape[2], True)
+    total = blocks_to_slots(back, sizes, order_matrix(sizes[1], 4, True), pair, padded)
+    bias = jnp.swapaxes(small[:, :128].astype(F32), 0, 1)[64:]
+    slots = []
+    for i in range(n):
+        slot_out = (total[i * 64 : (i + 1) * 64] + bias).astype(BF16)
+        combine_b = combine[i].astype(BF16)[:, :64]
+        output[i] = (hidden[i] + dot(combine_b, slot_out)).astype(BF16)
+        grad_combine = dot_t(cotangent[i], slot_out)
+        weight = combine[i][:, :64]
+        weighted = jnp.sum(weight * grad_combine, axis=1, keepdims=True)
+        grad_logits[i] = weight * (grad_combine - weighted)
+        slots.append(dot_r(combine_b, cotangent[i]).astype(BF16))
+    slots_to_blocks(
+        jnp.concatenate(slots, axis=0), blocks, columns, joined, order_matrix(sizes[1], 4, False)
+    )
+
+
+def tokens_middle(sizes, back, small, combine, hidden, cotangent):
+    n, rows, width = hidden.shape
+    vmem = pl.BlockSpec(memory_space=pltpu.VMEM)
+    shape = jax.ShapeDtypeStruct
+    return pl.pallas_call(
+        partial(middle_kernel, sizes),
+        out_shape=(
+            shape(hidden.shape, BF16),
+            shape((sizes[1], sizes[0], 2, 16, width // sizes[0]), BF16),
+            shape((n, rows, 64), F32),
+        ),
+        in_specs=[vmem] * 5,
+        out_specs=(vmem,) * 3,
+        scratch_shapes=[pltpu.VMEM((2, 128, 256), F32)],
+        compiler_params=pltpu.CompilerParams(vmem_limit_bytes=VMEM_BYTES),
+        name="tokens_middle",
+    )(back, small, combine, hidden, cotangent)
+
+
+def behind_kernel(
+    sizes, length, back, small, w_hbm, tokens, normed_1, query, keyed, valued, context, hidden,
+    normed_2, dispatch, grad_logits, cotangent, grads, small_grads, input_grad,
+    w, padded, grad_hidden, rounded, grad_context, grad_q, grad_k, grad_v, w_sem,
+):
+    n, rows, width = tokens.shape
+    keys = keyed.shape[1]
+    loads = [pltpu.make_async_copy(w_hbm.at[k], w.at[k], w_sem.at[k]) for k in range(4)]
+    for load in loads:
+        load.start()
+    norms = norm_rows(small)
+    padded[...] = jnp.zeros_like(padded)
+    pair = pair_matrix(back.shape[3], padded.shape[2], False)
+    grad_slots = blocks_to_slots(
+        back, sizes, order_matrix(sizes[1], 4, True), pair, padded
+    ).astype(BF16)
+    phi = small[:, :64]
+    phi_grad = jnp.zeros((width, 64), F32)
+    sums = []
+    flat = (n * rows, width)
+    for i in range(n):
+        slots = grad_slots[i * 64 : (i + 1) * 64]
+        weight = dispatch[i][:, :64]
+        grad_dispatch = dot_t(normed_2[i], slots)
+        weighted = jnp.sum(weight * grad_dispatch, axis=0, keepdims=True)
+        logits = (weight * (grad_dispatch - weighted) + grad_logits[i]).astype(BF16)
+        phi_grad = phi_grad + dot_r(normed_2[i], logits)
+        grad = dot(weight.astype(BF16), slots) + dot_t(logits, phi)
+        _, unit, inverse = norm_parts(hidden[i], norms[1:2], norms[3:4], None)
+        grad_in, scale_grad, bias_grad = norm_back(grad, unit, inverse, norms[1:2])
+        value = cotangent[i].astype(F32) + grad_in
+        grad_hidden[i] = value
+        rounded[i] = value.astype(BF16)
+        sums.append((scale_grad, bias_grad))
+    scale_2, bias_2 = sums[0][0] + sums[1][0], sums[0][1] + sums[1][1]
+    flat_rounded = rounded[...].reshape(flat)
+    loads[3].wait()
+    grad_context[...] = dot(flat_rounded, w[3]).astype(BF16).reshape(n, rows, width)
+    grads[3] = dot_r(flat_rounded, context[...].reshape(flat)).astype(BF16)
+    factor = HEAD_DIM ** (-0.5)
+    pairs = width // 128
+    lane = row_of((rows, 128), 1)
+    key_lane = row_of((keys, 128), 1)
+    shown = row_of((rows, keys), 1) < length
+
+    def attend(step, carry):
+        i = step // pairs
+        lanes = pl.ds(pl.multiple_of((step % pairs) * 128, 128), 128)
+        q, k, v = query[i, :, lanes], keyed[i, :, lanes], valued[i, :, lanes]
+        g = grad_context[i, :, lanes]
+        to_q, to_k, to_v = [], [], []
+        for a in range(2):
+            mine = (lane < 64) if a == 0 else (lane >= 64)
+            scores = dot_t(jnp.where(mine, q, jnp.zeros_like(q)), k) * factor
+            grad_probs = dot_t(jnp.where(mine, g, jnp.zeros_like(g)), v)
+            scores = jnp.where(shown, scores, -1e30)
+            exponent = jnp.exp(scores - jnp.max(scores, axis=-1, keepdims=True))
+            probs = exponent / jnp.sum(exponent, axis=-1, keepdims=True)
+            weighted = jnp.sum(probs * grad_probs, axis=-1, keepdims=True)
+            grad_scores = (probs * (grad_probs - weighted)).astype(BF16)
+            to_v.append(dot_r(probs.astype(BF16), g))
+            to_q.append(dot(grad_scores, k))
+            to_k.append(dot_r(grad_scores, q))
+        grad_q[i, :, lanes] = (jnp.where(lane < 64, to_q[0], to_q[1]) * factor).astype(BF16)
+        kept = key_lane < 64
+        grad_k[i, :, lanes] = (jnp.where(kept, to_k[0], to_k[1]) * factor)[:rows].astype(BF16)
+        grad_v[i, :, lanes] = jnp.where(kept, to_v[0], to_v[1])[:rows].astype(BF16)
+        return carry
+
+    lax.fori_loop(0, n * pairs, attend, 0, unroll=2)
+    total = jnp.zeros(flat, F32)
+    turned = jnp.swapaxes(normed_1[...].reshape(flat).astype(F32), 0, 1).astype(BF16)
+    for k, source in enumerate((grad_q, grad_k, grad_v)):
+        loads[k].wait()
+        value = source[...].reshape(flat)
+        total = total + dot_t(value, w[k])
+        grads[k] = dot(turned, value).astype(BF16)
+    total = total.reshape(n, rows, width)
+    sums = []
+    for i in range(n):
+        _, unit, inverse = norm_parts(tokens[i].astype(F32), norms[0:1], norms[2:3], None)
+        grad_in, scale_grad, bias_grad = norm_back(total[i], unit, inverse, norms[0:1])
+        input_grad[i] = (grad_hidden[i] + grad_in).astype(BF16)
+        sums.append((scale_grad, bias_grad))
+    scale_1, bias_1 = sums[0][0] + sums[1][0], sums[0][1] + sums[1][1]
+    line = row_of((128, width), 0)
+    spread = jnp.zeros((128, width), F32)
+    for j, value in enumerate((scale_1, scale_2, bias_1, bias_2)):
+        spread = jnp.where(line == 64 + j, value, spread)
+    small_grads[...] = jnp.swapaxes(spread, 0, 1).astype(BF16)
+    small_grads[:, :64] = phi_grad.astype(BF16)
+
+
+def tokens_behind(sizes, length, back, small, weights, tokens, kept, grad_logits, cotangent):
+    n, rows, width = tokens.shape
+    vmem = pl.BlockSpec(memory_space=pltpu.VMEM)
+    shape = jax.ShapeDtypeStruct
+    low = pltpu.VMEM(tokens.shape, BF16)
+    return pl.pallas_call(
+        partial(behind_kernel, sizes, length),
+        out_shape=(
+            shape((4, width, width), BF16), shape((width, 128), BF16), shape(tokens.shape, BF16)
+        ),
+        in_specs=[vmem, vmem, pl.BlockSpec(memory_space=pl.ANY)] + [vmem] * 11,
+        out_specs=(vmem,) * 3,
+        scratch_shapes=[
+            pltpu.VMEM(weights.shape, BF16),
+            pltpu.VMEM((2, 128, 256), F32),
+            pltpu.VMEM(tokens.shape, F32),
+            low, low, low, low, low,
+            pltpu.SemaphoreType.DMA((4,)),
+        ],
+        compiler_params=pltpu.CompilerParams(vmem_limit_bytes=VMEM_BYTES),
+        name="tokens_behind",
+    )(back, small, weights, tokens, *kept, grad_logits, cotangent)
+
+
 def normalize(values, scale, shift):
     centered = values - jnp.mean(values, axis=-1, keepdims=True)
     variance = jnp.mean(centered * centered, axis=-1, keepdims=True)
@@ -861,32 +1313,14 @@
     return lax.all_gather(slots, "tensor", axis=0, tiled=True)
 
 
-def to_blocks(slots, sizes):
-    own, experts, width = slots.shape
-    n_s, n_h, _ = sizes
-    few = experts // n_h // 4
-    slots = slots.reshape(own, n_h, 2, 2, few, n_s, width // n_s)
-    return slots.transpose(1, 5, 3, 0, 2, 4, 6).reshape(n_h, n_s, 2, own * 2 * few, width // n_s)
-
-
-def from_blocks(blocks, sizes):
-    n_s, n_h, n_t = sizes
-    rows = blocks.shape[3]
-    blocks = jnp.sum(blocks.reshape(2, n_s, n_h, n_t, 2, 2, -1, rows).astype(F32), axis=3)
-    return blocks.transpose(3, 2, 4, 0, 5, 1, 6).reshape(2, -1, n_s * rows)
-
-
 def to_images(slots):
     slots = lax.psum_scatter(slots, "tensor", scatter_dimension=0, tiled=True)
     slots = lax.all_to_all(slots, "shard", split_axis=0, concat_axis=2, tiled=True)
     return lax.all_to_all(slots, "heads", split_axis=0, concat_axis=1, tiled=True)
 
 
-def shards(tokens, norm_scales, norm_biases, w_attn, phi, experts, in_bias, out_bias, cotangent):
+def general_shards(tokens, norm_scales, norm_biases, w_attn, phi, experts, in_bias, out_bias, cotangent):
     heads_n = lax.axis_size("heads")
-    sizes = tuple(lax.axis_size(name) for name in ("shard", "heads", "tensor"))
-    if sizes != (4, 4, 2) or tokens.shape[0] != 8 or experts.shape[2] != 16:
-        sizes = None
     group, seq_len, width = tokens.shape
     own = group // heads_n
     heads_index = lax.axis_index("heads")
@@ -894,42 +1328,18 @@
     shard_index = lax.axis_index("shard")
     hidden = experts.shape[3]
     rows = experts.shape[0]
-    if sizes is not None:
-        n_s, n_h, n_t = sizes
-        block, slot = w_attn.shape[2], phi.shape[1]
-        beside = jnp.concatenate((phi, out_bias.T), axis=1)
-        beside = jnp.pad(beside, ((0, 0), (0, 256 - block - 2 * slot)))
-        beside = jnp.concatenate((beside[None], jnp.zeros((3, *beside.shape), BF16)), axis=0)
-        packet = jnp.concatenate((w_attn, beside), axis=2)
-        extra = jnp.concatenate(
-            (
-                in_bias.reshape(-1, 64),
-                norm_scales.T,
-                norm_biases.T,
-            ),
-            axis=1,
-        )
-        extra = jnp.pad(extra, ((0, 0), (128, 60)))
-        attn, small, turned = gather_weights(sizes, packet, extra, experts)
-        phi_full = small[:, :64]
-        out_all = small[:, 64:128].T.astype(F32)
-        in_full = small[:, 128:192].reshape(n_s * n_t, -1, in_bias.shape[1])
-        in_full = in_full.transpose(1, 0, 2).reshape(in_bias.shape[0], -1).astype(F32)
-        scales = small[:, 192:194].T.astype(F32)
-        biases = small[:, 194:196].T.astype(F32)
-    else:
-        scales, biases, in_full = (
-            lax.all_gather(norm_scales, ROWS, axis=1, tiled=True).astype(F32),
-            lax.all_gather(norm_biases, ROWS, axis=1, tiled=True).astype(F32),
-            lax.all_gather(in_bias, ROWS, axis=1, tiled=True).astype(F32),
-        )
-        attn = lax.all_gather(
-            lax.all_gather(w_attn, "heads", axis=2, tiled=True), ROWS, axis=1, tiled=True
-        )
-        phi_full = lax.all_gather(
-            lax.all_gather(phi, "heads", axis=1, tiled=True), ROWS, axis=0, tiled=True
-        )
-        out_rows = lax.all_gather(out_bias, "tensor", axis=1, tiled=True).astype(F32)
+    scales, biases, in_full = (
+        lax.all_gather(norm_scales, ROWS, axis=1, tiled=True).astype(F32),
+        lax.all_gather(norm_biases, ROWS, axis=1, tiled=True).astype(F32),
+        lax.all_gather(in_bias, ROWS, axis=1, tiled=True).astype(F32),
+    )
+    attn = lax.all_gather(
+        lax.all_gather(w_attn, "heads", axis=2, tiled=True), ROWS, axis=1, tiled=True
+    )
+    phi_full = lax.all_gather(
+        lax.all_gather(phi, "heads", axis=1, tiled=True), ROWS, axis=0, tiled=True
+    )
+    out_rows = lax.all_gather(out_bias, "tensor", axis=1, tiled=True).astype(F32)
     e_own = experts.shape[2] // lax.axis_size("shard")
     in_local = lax.dynamic_slice_in_dim(in_full, tensor_index * hidden, hidden, 1)
     factor = HEAD_DIM ** (-0.5)
@@ -957,62 +1367,44 @@
     dispatch_b = dispatch.astype(BF16)
     combine = jax.nn.softmax(logits, axis=2)
     combine_b = combine.astype(BF16)
-    slot_in = einsum("nse,nsd->ned", dispatch_b, normed_two_b).astype(BF16)
-    if sizes is not None:
-        slot_in, activated, gate, back = expert_pass(
-            sizes, False, to_blocks(slot_in, sizes), turned, in_local[:, None, :]
-        )
-        slot_out = (from_blocks(back, sizes) + out_all).astype(BF16)
+    slot_in = to_experts(einsum("nse,nsd->ned", dispatch_b, normed_two_b).astype(BF16))
+    share = 1 if e_own else 0
+
+    def meet(partial_sum):
+        return lax.psum_scatter(partial_sum, "shard", scatter_dimension=share, tiled=True)
+
+    def spread(values):
+        return lax.all_gather(values, "shard", axis=share, tiled=True)
+
+    pre = meet(einsum("ned,def->nef", slot_in, experts[:, 0]))
+    if e_own:
+        pre = pre + lax.dynamic_slice_in_dim(in_local, shard_index * e_own, e_own, 0)
     else:
-        slot_in = to_experts(slot_in)
-        share = 1 if e_own else 0
-
-        def meet(partial_sum):
-            return lax.psum_scatter(partial_sum, "shard", scatter_dimension=share, tiled=True)
-
-        def spread(values):
-            return lax.all_gather(values, "shard", axis=share, tiled=True)
-
-        pre = meet(einsum("ned,def->nef", slot_in, experts[:, 0]))
-        if e_own:
-            pre = pre + lax.dynamic_slice_in_dim(in_local, shard_index * e_own, e_own, 0)
-        else:
-            pre = pre + in_local
-        gelu_value, gelu_back = jax.vjp(partial(jax.nn.gelu, approximate=False), pre)
-        activated = spread(gelu_value.astype(BF16))
-        slot_out_part = einsum("nef,def->ned", activated, experts[:, 1])
-        slot_out_part = slot_out_part + jnp.where(tensor_index == 0, out_rows, 0.0)
-        slot_out = to_images(slot_out_part).astype(BF16)
+        pre = pre + in_local
+    gelu_value, gelu_back = jax.vjp(partial(jax.nn.gelu, approximate=False), pre)
+    activated = spread(gelu_value.astype(BF16))
+    slot_out_part = einsum("nef,def->ned", activated, experts[:, 1])
+    slot_out_part = slot_out_part + jnp.where(tensor_index == 0, out_rows, 0.0)
+    slot_out = to_images(slot_out_part).astype(BF16)
     output = (hidden_one + einsum("nse,ned->nsd", combine_b, slot_out)).astype(BF16)
+    output = lax.all_gather(output, "heads", axis=0, tiled=True)
     grad_combine = einsum("nsd,ned->nse", cotangent, slot_out)
-    grad_slot = einsum("nse,nsd->ned", combine_b, cotangent).astype(BF16)
-    if sizes is not None:
-        grad_slot, grad_pre, back, in_bias_grad = expert_pass(
-            sizes, True, to_blocks(grad_slot, sizes), turned, gate, in_bias.shape[1]
-        )
-        back, output = lax.optimization_barrier((back, output))
-        output = lax.all_gather(output, "heads", axis=0, tiled=True)
-        grad_slot_in = from_blocks(back, sizes).astype(BF16)
-        grad_slot_sum = jnp.sum(grad_slot.astype(F32), axis=1)
-    else:
-        output = lax.all_gather(output, "heads", axis=0, tiled=True)
-        grad_slot = to_experts(grad_slot)
-        grad_act = meet(einsum("ned,def->nef", grad_slot, experts[:, 1]))
-        grad_pre = spread(gelu_back(grad_act)[0].astype(BF16))
-        grad_slot_in = einsum("nef,def->ned", grad_pre, experts[:, 0]).astype(BF16)
-        input_term = einsum("ned,nef->def", slot_in, grad_pre)
-        output_term = einsum("ned,nef->def", grad_slot, activated)
-        experts_grad = jnp.stack((input_term, output_term), axis=1)
-        grad_slot_in = to_images(grad_slot_in.astype(F32)).astype(BF16)
-        in_bias_grad = lax.dynamic_slice_in_dim(
-            lax.all_gather(jnp.sum(grad_pre.astype(F32), axis=0), "tensor", axis=1, tiled=True),
-            (shard_index * lax.axis_size("tensor") + tensor_index) * in_bias.shape[1],
-            in_bias.shape[1],
-            1,
-        )
-        grad_slot_sum = jnp.sum(grad_slot.astype(F32), axis=0)
+    grad_slot = to_experts(einsum("nse,nsd->ned", combine_b, cotangent).astype(BF16))
+    grad_act = meet(einsum("ned,def->nef", grad_slot, experts[:, 1]))
+    grad_pre = spread(gelu_back(grad_act)[0].astype(BF16))
+    grad_slot_in = einsum("nef,def->ned", grad_pre, experts[:, 0]).astype(BF16)
+    input_term = einsum("ned,nef->def", slot_in, grad_pre)
+    output_term = einsum("ned,nef->def", grad_slot, activated)
+    experts_grad = jnp.stack((input_term, output_term), axis=1)
+    grad_slot_in = to_images(grad_slot_in.astype(F32)).astype(BF16)
+    in_bias_grad = lax.dynamic_slice_in_dim(
+        lax.all_gather(jnp.sum(grad_pre.astype(F32), axis=0), "tensor", axis=1, tiled=True),
+        (shard_index * lax.axis_size("tensor") + tensor_index) * in_bias.shape[1],
+        in_bias.shape[1],
+        1,
+    )
     out_bias_grad = lax.dynamic_slice_in_dim(
-        grad_slot_sum,
+        jnp.sum(grad_slot.astype(F32), axis=0),
         tensor_index * out_bias.shape[1],
         out_bias.shape[1],
         1,
@@ -1048,27 +1440,14 @@
         grad_normed_one, unit_one, inverse_one, scales[0]
     )
     input_grad = (grad_hidden + grad_input_norm).astype(BF16)
-    if sizes is not None:
-        input_grad, output = lax.optimization_barrier((input_grad, output))
     input_grad = lax.all_gather(input_grad, "heads", axis=0, tiled=True)
     attn_grad = jnp.concatenate((proj_grad, out_weight_grad[None]), axis=0)
+    attn_grad = lax.psum_scatter(attn_grad, ROWS, scatter_dimension=1, tiled=True)
+    attn_grad = lax.psum_scatter(attn_grad, "heads", scatter_dimension=2, tiled=True)
+    phi_grad = lax.psum_scatter(phi_grad, ROWS, scatter_dimension=0, tiled=True)
+    phi_grad = lax.psum_scatter(phi_grad, "heads", scatter_dimension=1, tiled=True)
     norms = jnp.stack((scale_one_grad, scale_two_grad, bias_one_grad, bias_two_grad))
-    if sizes is not None:
-        small = jnp.concatenate((phi_grad, norms.T), axis=1)
-        small = jnp.pad(small, ((0, 0), (0, 128 - small.shape[1]))).astype(BF16)
-        attn_grad, grad_pre = lax.optimization_barrier((attn_grad.astype(BF16), grad_pre))
-        experts_grad = weight_grads(slot_in, grad_pre, grad_slot, activated)
-        attn_grad, experts_grad = lax.optimization_barrier((attn_grad, experts_grad))
-        summed = reduce_grads(sizes, attn_grad, small)
-        attn_grad = summed[:, :, :block]
-        phi_grad = summed[0, :, block : block + slot]
-        norms = summed[0, :, block + slot : block + slot + 4].T
-    else:
-        attn_grad = lax.psum_scatter(attn_grad, ROWS, scatter_dimension=1, tiled=True)
-        attn_grad = lax.psum_scatter(attn_grad, "heads", scatter_dimension=2, tiled=True)
-        phi_grad = lax.psum_scatter(phi_grad, ROWS, scatter_dimension=0, tiled=True)
-        phi_grad = lax.psum_scatter(phi_grad, "heads", scatter_dimension=1, tiled=True)
-        norms = lax.psum(lax.psum_scatter(norms, ROWS, scatter_dimension=1, tiled=True), "heads")
+    norms = lax.psum(lax.psum_scatter(norms, ROWS, scatter_dimension=1, tiled=True), "heads")
     return (
         output,
         input_grad,
@@ -1076,6 +1455,62 @@
         norms[2:],
         attn_grad,
         phi_grad,
+        experts_grad,
+        in_bias_grad,
+        out_bias_grad,
+    )
+
+
+def shards(tokens, norm_scales, norm_biases, w_attn, phi, experts, in_bias, out_bias, cotangent):
+    arrays = (tokens, norm_scales, norm_biases, w_attn, phi, experts, in_bias, out_bias, cotangent)
+    sizes = tuple(lax.axis_size(name) for name in ("shard", "heads", "tensor"))
+    group, length, width = tokens.shape
+    fits = (sizes, group, width, *experts.shape[:3]) == ((4, 4, 2), 8, 768, 192, 2, 16)
+    if not fits or length > 208 or in_bias.shape[1] != 384:
+        return general_shards(*arrays)
+    n_s, n_h, n_t = sizes
+    own = group // n_h
+    block, slot = w_attn.shape[2], phi.shape[1]
+    beside = jnp.concatenate((phi, out_bias.T), axis=1)
+    beside = jnp.pad(beside, ((0, 0), (0, 256 - block - 2 * slot)))
+    beside = jnp.concatenate((beside[None], jnp.zeros((3, *beside.shape), BF16)), axis=0)
+    packet = jnp.concatenate((w_attn, beside), axis=2)
+    hidden_bias = in_bias.reshape(16, 6, 64).transpose(1, 0, 2).reshape(96, 64)
+    extra = jnp.concatenate((hidden_bias, norm_scales.T, norm_biases.T), axis=1)
+    extra = jnp.pad(extra, ((0, 0), (128, 60)))
+    attn, small, turned = gather_weights(sizes, packet, extra, experts)
+
+    def mine(values):
+        values = lax.dynamic_slice_in_dim(values, lax.axis_index("heads") * own, own, 0)
+        return jnp.pad(values, ((0, 0), (0, 208 - length), (0, 0)))
+
+    tokens, cotangent = mine(tokens), mine(cotangent)
+    blocks, *kept, combine = tokens_ahead(sizes, length, tokens, small, attn)
+    hidden = kept[5]
+    slot_in, activated, gate, back = expert_pass(sizes, False, blocks, turned, small)
+    output, blocks, grad_logits = tokens_middle(sizes, back, small, combine, hidden, cotangent)
+    grad_slot, grad_pre, back, in_bias_grad, out_sum, output = expert_pass(
+        sizes, True, blocks, turned, gate, output, in_bias.shape[1]
+    )
+    attn_grad, small_grad, input_grad = tokens_behind(
+        sizes, length, back, small, attn, tokens, kept, grad_logits, cotangent
+    )
+    input_grad = lax.all_gather(input_grad, "heads", axis=0, tiled=True)
+    attn_grad, grad_pre = lax.optimization_barrier((attn_grad, grad_pre))
+    experts_grad = weight_grads(slot_in, grad_pre, grad_slot, activated)
+    attn_grad, experts_grad = lax.optimization_barrier((attn_grad, experts_grad))
+    summed = reduce_grads(sizes, attn_grad, small_grad)
+    norms = summed[0, :, block + slot : block + slot + 4].T
+    out_bias_grad = lax.dynamic_slice_in_dim(
+        out_sum, lax.axis_index("tensor") * out_bias.shape[1], out_bias.shape[1], 1
+    )
+    return (
+        output[:, :length],
+        input_grad[:, :length],
+        norms[:2],
+        norms[2:],
+        summed[:, :, :block],
+        summed[0, :, block : block + slot],
         experts_grad,
         in_bias_grad,
         out_bias_grad,

time: 387 us -> 340 us (0.88); the launches traced: 381 us -> 340 us
  Pallas kernels: 242 us -> 306 us
  matrix products: 52.1 us -> 0 us
  local copies, waits for them, and re-layouts: 45.4 us -> 17.5 us
  other arithmetic: 17.5 us -> 1.47 us
  waiting for transfers between devices: 9.06 us -> 0.02 us
    pallas_call x0 -> x3, Pallas kernels: none -> 45.5 us  [the longest x1 27.4 us: tokens_behind(): pl.pallas_call(partial(behind_kernel, sizes, length), out_shape=(shape((4...]
    dot_general x19 -> x0, matrix products: 44.4 us -> none  [the longest x1 4.43 us: shards(): grad_normed_one = einsum('knsc,kdc->nsd', grad_proj, attn[:3])]
    another operation x13 -> x0, local copies, waits for them, and re-layouts: 12.1 us -> none  [the longest x4 6.17 us: shards(): query, keyed, valued = projected.reshape(3, own, seq_len, n_heads, HEAD_DIM)]
    pallas_call x2, Pallas kernels: 137 us -> 148 us  [expert_pass(): pl.pallas_call(partial(expert_kernel, sizes, backward), out_shape=outs, i...]
    all_gather x1 -> x0, waiting for transfers between devices: 9.02 us -> none  [shards(): output = lax.all_gather(output, 'heads', axis=0, tiled=True)]
    pallas_call x1, Pallas kernels: 40.5 us -> 48.7 us  [reduce_grads(): pl.pallas_call(partial(reduce_kernel, sizes), out_shape=jax.ShapeDtypeStr...]
    sub x2 -> x0, matrix products: 7.72 us -> none  [the longest x1 5.28 us: shards(): exponent = jnp.exp(scores - score_peak)]
    reshape x8 -> x1, local copies, waits for them, and re-layouts: 6.15 us -> 0.09 us  [shards(): hidden_bias = in_bias.reshape(16, 6, 64).transpose(1, 0, 2).reshape(96, 64)]
  transfers between devices with their start and end apart: 2 -> 1, of which waited for: 1 -> 0; matrix products, arithmetic and copies ran while one was open for 15% -> 2% of each run, Pallas kernels for 16% -> 21%
where the time goes in v2:
time: 340 us
  Pallas kernels  306 us (90%)
  local copies, waits for them, and re-layouts  17.5 us (5%)
  between operations  14.2 us (4%)
    pallas_call x2, Pallas kernels, expert_pass(): pl.pallas_call(partial(expert_kernel, sizes, backward), out_shape=outs, i...  148 us
    pallas_call x1, Pallas kernels, reduce_grads(): pl.pallas_call(partial(reduce_kernel, sizes), out_shape=jax.ShapeDtypeStr...  48.7 us
    pallas_call x1, Pallas kernels, gather_weights(): pl.pallas_call(partial(gather_kernel, sizes), out_shape=(jax.ShapeDtypeSt...  43.5 us
    pallas_call x1, Pallas kernels, tokens_behind(): pl.pallas_call(partial(behind_kernel, sizes, length), out_shape=(shape((4...  27.4 us
    pallas_call x1, Pallas kernels, weight_grads(): pl.pallas_call(weight_grad_kernel, grid=(2, experts // group, rows // d_b...  21 us
    pallas_call x1, Pallas kernels, tokens_ahead(): pl.pallas_call(partial(ahead_kernel, length), out_shape=(shape((sizes[1],...  14 us
    unnamed x31, local copies, waits for them, and re-layouts  7.5 us
  transfers between devices with their start and end apart: 1, of which 0 were waited for; matrix products, arithmetic and copies ran while one was open for 2% of the time, Pallas kernels for 21%

profile of v2, /device:TPU:0, one launch (start us, length us, event | category | flops | bytes accessed | tf_op | source)
XLA Modules:
  0.0 339.5 jit_solution(15971130718247073977)
XLA Ops:
  7.2 0.0 copy-start.6
  7.2 0.0 copy-start.7
  7.2 0.0 copy-start.4
  7.2 0.0 copy-start.8
  7.2 0.0 copy-start.9
  7.2 0.0 all-gather.2.cloned.1.call-start
  7.3 3.7 %constant_dynamic-slice_fusion.1 = (bf16[2,197,768]{2,0,1:T(2,128)(2,1)S(1)}, bf16[2,197,768]{2,0,1:T(2,128)(2,1)S(1)}) fusion(bf16[8,197,768]{2,0,1:T(8,128)(2,1)} %param.17, s32[]{:T(128)S(6)} %select_n.7, bf16[8,197,768]{2,0,1:T(8,128)(2,1)} %param.9), kind=kLoop, calls=%fused_computation.16 | loop fusion | bytes 2420740 | tf_op jit(solution)/shard_map/dynamic_slice | solution.py:1484
  10.9 0.0 copy-start.2
  11.0 0.1 copy.53
  11.0 0.0 copy-done.6
  11.0 0.0 copy-done.7
  11.1 0.1 copy.43
  11.2 0.0 copy-done.4
  11.2 0.1 reshape.24
  11.3 0.0 copy-done.8
  11.3 0.1 copy.45
  11.4 0.0 copy-done.9
  11.4 0.1 copy.46
  11.6 0.1 copy.54
  11.6 0.9 pad.16.tokens
  12.5 0.9 pad.19.cotangent
  13.4 0.0 copy-done.2
  13.4 0.8 fusion.1.packet
  14.1 0.7 fusion.7.extra
  14.9 43.5 %gather_weights.1 = (bf16[4,768,768]{2,1,0:T(8,128)(2,1)}, bf16[768,256]{1,0:T(8,128)(2,1)}, bf16[2,16,192,1536]{3,2,1,0:T(8,128)(2,1)}) custom-call(bf16[4,96,256]{2,1,0:T(8,128)(2,1)} %fusion.1.packet, bf16[96,256]{1,0:T(8,128)(2,1)} %fusion.7.extra, bf16[192,2,16,1536]{3,2,1,0:T(8,128)(2,1)} %experts.1), custom_call_target="tpu_custom_call" | custom-call | tf_op jit(solution)/shard_map/gather_weights/pallas_call | solution.py:298
  58.3 14.0 %tokens_ahead.1 = (bf16[4,4,2,16,192]{4,3,2,1,0:T(8,128)(2,1)}, bf16[2,208,768]{2,1,0:T(8,128)(2,1)}, bf16[2,208,768]{2,1,0:T(8,128)(2,1)}, bf16[2,256,768]{2,1,...) custom-call(bf16[2,208,768]{2,1,0:T(8,128)(2,1)} %pad.16.tokens, ...), custom_call_target="tpu_custom_call" | custom-call | tf_op jit(solution)/shard_map/tokens_ahead/pallas_call | solution.py:1108
  72.3 68.2 %experts_ahead.1 = (bf16[16,64,192]{2,1,0:T(8,128)(2,1)}, bf16[16,64,1536]{2,1,0:T(8,128)(2,1)}, f32[8,64,1536]{2,1,0:T(8,128)}, bf16[2,32,16,192]{3,2,1,0:T(8,128)(2,1)}) custom-call(bf16[4,4,2,16,192]{4,3,2,1,0:T(8,128)(2,1)} %get-tuple-element.44.refs_0_, bf16[2,16,192,1536]{3,2,1,0:T(8,128)(2,1)} %get-tuple-element.45.refs_1_, ...), custom_call_target="tpu_custom_call" | custom-call | flops 2415919104 | bytes 18874368 | tf_op jit(solution)/shard_map/experts_ahead/pallas_call | solution.py:846
  140.6 4.1 %tokens_middle.1 = (bf16[2,208,768]{2,1,0:T(8,128)(2,1)}, bf16[4,4,2,16,192]{4,3,2,1,0:T(8,128)(2,1)}, f32[2,208,64]{2,1,0:T(8,128)}) custom-call(bf16[2,32,16,192]{3,2,1,0:T(8,128)(2,1)} %get-tuple-element.46.back, bf16[768,256]{1,0:T(8,128)(2,1)} %get-tuple-element.42.small.refs_2_, f32[2,208,128]{2,1,0:T(8,128)} %get-tuple-element.47.combine, ...), custom_call_target="tpu_custom_call" | custom-call | tf_op jit(solution)/shard_map/tokens_middle/pallas_call | solution.py:1158
  144.6 79.4 %experts_back.1 = (bf16[16,64,192]{2,1,0:T(8,128)(2,1)}, bf16[16,64,1536]{2,1,0:T(8,128)(2,1)}, bf16[2,32,16,192]{3,2,1,0:T(8,128)(2,1)}, f32[16,384]{1,0:T(8,12...) custom-call(bf16[4,4,2,16,192]{4,3,2,1,0:T(8,128)(2,1)} %get-tuple-element.49.refs_0_, ...), custom_call_target="tpu_custom_call" | custom-call | flops 2415919104 | bytes 18874368 | tf_op jit(solution)/shard_map/experts_back/pallas_call | solution.py:846
  224.0 27.4 %tokens_behind.1 = (bf16[4,768,768]{2,1,0:T(8,128)(2,1)}, bf16[768,128]{1,0:T(8,128)(2,1)}, bf16[2,208,768]{2,1,0:T(8,128)(2,1)}) custom-call(bf16[2,32,16,192]{3,2,1,0:T(8,128)(2,1)} %get-tuple-element.53.back, bf16[768,256]{1,0:T(8,128)(2,1)} %get-tuple-element.42.small.refs_2_, bf16[4,768,768]{2,1,0:T(8,128)(2,1)} %get-tuple-element.43.w_hbm, ...), custom_call_target="tpu_custom_call" | custom-call | tf_op jit(solution)/shard_map/tokens_behind/pallas_call | solution.py:1271
  251.5 0.0 all-gather.2.cloned.1.call-update
  251.5 21.0 %weight_grads.1 = f32[192,2,16,1536]{3,2,1,0:T(8,128)} custom-call(bf16[16,64,192]{2,1,0:T(8,128)(2,1)} %get-tuple-element.66.slots_0, bf16[16,64,1536]{2,1,0:T(8,128)(2,1)} %get-tuple-element.67.act_0, bf16[16,64,192]{2,1,0:T(8,128)(2,1)} %get-tuple-element.68.slots_1, bf16[16,64,1536]{2,1,0:T(8,128)(2,1)} %get-tuple-element.69.act_1), custom_call_target="tpu_custom_call" | custom-call | flops 1207959552 | bytes 37748736 | tf_op jit(solution)/shard_map/weight_grads/pallas_call | solution.py:915
  272.5 0.0 copy-start
  272.5 48.7 %reduce_grads.1 = f32[4,96,256]{2,1,0:T(8,128)} custom-call(bf16[4,768,768]{2,1,0:T(8,128)(2,1)} %get-tuple-element.70.grads, bf16[768,128]{1,0:T(8,128)(2,1)} %get-tuple-element.71.small), custom_call_target="tpu_custom_call" | custom-call | tf_op jit(solution)/shard_map/reduce_grads/pallas_call | solution.py:474
  321.2 0.9 slice_bitcast_fusion.1
  322.1 0.1 fusion.8
  322.2 0.6 copy.50
  322.8 0.6 copy.51
  323.5 0.9 slice_bitcast_fusion
  324.3 0.7 copy.52
  325.0 0.0 copy-done
  325.0 0.2 slice.21
  325.2 0.0 copy-start.5
  325.2 1.9 copy.48
  327.1 0.0 copy-done.5
  327.1 0.7 constant_dynamic-slice_fusion
  327.8 0.0 all-gather.2.cloned.1.call-done
  327.8 0.0 slice-start
  327.8 1.7 slice-done
  329.4 0.0 copy-start.1
  329.5 0.0 copy-start.3
  329.5 1.9 copy.49
  331.3 0.0 copy-done.1
  331.3 0.7 copy.57
  332.1 0.0 copy-done.3
  332.1 0.6 copy.58
  (3 shorter events, 0.0 us)
Async XLA Ops:
  7.2 3.9 %copy-start.6 = (bf16[16,96]{1,0:T(8,128)(2,1)S(1)}, bf16[16,96]{1,0:T(8,128)(2,1)}, u32[]{:S(2)}) copy-start(bf16[16,96]{1,0:T(8,128)(2,1)} %param.16) | copy-start | bytes 9220
  7.2 3.9 %copy-start.7 = (bf16[96,16]{0,1:T(8,128)(2,1)S(1)}, bf16[96,16]{0,1:T(8,128)(2,1)}, u32[]{:S(2)}) copy-start(bf16[96,16]{0,1:T(8,128)(2,1)} %param.13) | copy-start | bytes 9220
  7.2 4.0 %copy-start.4 = (bf16[16,384]{1,0:T(8,128)(2,1)S(1)}, bf16[16,384]{1,0:T(8,128)(2,1)}, u32[]{:S(2)}) copy-start(bf16[16,384]{1,0:T(8,128)(2,1)} %param.15) | copy-start | bytes 36868
  7.2 4.1 %copy-start.8 = (bf16[2,96]{1,0:T(2,128)(2,1)S(1)}, bf16[2,96]{1,0:T(2,128)(2,1)}, u32[]{:S(2)}) copy-start(bf16[2,96]{1,0:T(2,128)(2,1)} %param.10) | copy-start | bytes 1156
  7.2 4.2 %copy-start.9 = (bf16[2,96]{1,0:T(2,128)(2,1)S(1)}, bf16[2,96]{1,0:T(2,128)(2,1)}, u32[]{:S(2)}) copy-start(bf16[2,96]{1,0:T(2,128)(2,1)} %param.11) | copy-start | bytes 1156
  7.2 320.5 %all-gather.2.cloned.1.call-start = ((), (), s32[]{:S(2)}) async-start(), calls=%async_computation | async-start | bytes 3194880 | tf_op jit(solution)/shard_map/all_gather | solution.py:1498
  10.9 2.4 copy-start.2
  272.5 52.5 %copy-start = (bf16[8,208,768]{2,1,0:T(8,128)(2,1)S(1)}, bf16[8,208,768]{2,1,0:T(8,128)(2,1)}, u32[]{:S(2)}) copy-start(bf16[8,208,768]{2,1,0:T(8,128)(2,1)} %get-tuple-element.52) | copy-start | bytes 7667716
  325.2 1.9 copy-start.5
  327.8 1.7 slice-start
  329.4 1.9 copy-start.1
  329.5 2.6 copy-start.3
Sparse Core Ops, SparseCore 0:
  251.6 64.9 all-gather.1

commit v3 on v2

--- a/solution.py
+++ b/solution.py
@@ -91,9 +91,9 @@
 
 
 def gather_kernel(
-    sizes, packet, extra, experts, w_out, small_out, turned,
-    w, small, lined, tile_in, tile_out,
-    z_send, z_recv, x_sems, y_sems, d_sems, c_sems, t_sems, o_sems,
+    sizes, packet, extra, experts, tokens, cotangent, w_out, small_out, turned, own_tokens, own_cot,
+    w, small, lined, tile_in, tile_out, images, picked,
+    z_send, z_recv, x_sems, y_sems, d_sems, c_sems, t_sems, o_sems, i_sems,
 ):
     (s, h, t), core, chip, sibling, across_x, across_y, line = plane(sizes)
     n_k, rows, wide = packet.shape
@@ -154,8 +154,14 @@
             t_sems.at[1, i % depth],
         )
 
+    image_loads = [
+        pltpu.make_async_copy(source, images.at[j], i_sems.at[0, j])
+        for j, source in enumerate((tokens, cotangent))
+    ]
     for i in range(depth - 1):
         load(i).start()
+    for copy in image_loads:
+        copy.start()
     swap = swap_matrix(side)
     done = [0]
 
@@ -188,6 +194,31 @@
     beside = (lane >= 0) & (lane < 16) & (column == of * 16 + lane)
     beside |= (lane >= 16) & (lane < 32) & (column == n_h * 16 + of * 16 + lane - 16)
     beside = beside.astype(F32).astype(BF16)
+
+    image_stores = [
+        pltpu.make_async_copy(picked.at[j], target, i_sems.at[1, j])
+        for j, target in enumerate((own_tokens, own_cot))
+    ]
+
+    def pick_images(j):
+        own, padded = picked.shape[1:3]
+        group = own * n_h
+        lines = images.shape[1]
+        image_loads[j].wait()
+        step = 256 // group
+        for first in range(0, padded, step):
+            count = min(step, padded - first)
+            taken = min(step * group, lines - first * group)
+            shape = (own * count, taken)
+            row = lax.broadcasted_iota(jnp.int32, shape, 0)
+            column = lax.broadcasted_iota(jnp.int32, shape, 1)
+            wanted = (row % count) * group + own * h + row // count
+            chosen = (column == wanted).astype(F32).astype(BF16)
+            source = images[j, first * group : first * group + taken]
+            picked[j, :, first : first + count] = (
+                dot(chosen, source).astype(BF16).reshape(own, count, images.shape[2])
+            )
+        image_stores[j].start()
 
     def at(k, place):
         first = pl.multiple_of((place[0] * n_t + place[2]) * rows, 16)
@@ -248,6 +279,8 @@
         i = wave - n_h + 2
         if i >= 0:
             assemble(chunks[i])
+            if i in (1, 2):
+                pick_images(i - 1)
             if i >= 1:
                 relay_xy(chunks[i - 1])
             if i >= 2:
@@ -282,11 +315,13 @@
 
     for i in range(depth):
         store(2 * n_tiles - depth + i).wait()
+    for copy in image_stores:
+        copy.wait()
     for copy in stores:
         copy.wait()
 
 
-def gather_weights(sizes, packet, extra, experts):
+def gather_weights(sizes, packet, extra, experts, tokens, cotangent):
     n_k, rows, wide = packet.shape
     n_s, n_h, n_t = sizes
     width = n_s * n_t * rows
@@ -295,29 +330,34 @@
     dma = pltpu.SemaphoreType.DMA
     hidden = experts.shape[3]
     small = (width, extra.shape[1])
+    images = jax.ShapeDtypeStruct((2, 208, width), BF16)
     return pl.pallas_call(
         partial(gather_kernel, sizes),
         out_shape=(
             jax.ShapeDtypeStruct((n_k, width, width), BF16),
             jax.ShapeDtypeStruct(small, BF16),
             jax.ShapeDtypeStruct((2, experts.shape[2], experts.shape[0], hidden), BF16),
+            images, images,
         ),
-        in_specs=[vmem, vmem, hbm],
-        out_specs=(hbm, hbm, hbm),
+        in_specs=[vmem, vmem, hbm, hbm, hbm],
+        out_specs=(hbm,) * 5,
         scratch_shapes=[
             pltpu.VMEM((n_k, width, width), BF16),
             pltpu.VMEM(small, BF16),
             pltpu.VMEM((n_h, n_k, rows, wide), BF16),
             pltpu.VMEM((4, 16, 16, hidden), BF16),
             pltpu.VMEM((4, 16, 16, hidden), BF16),
+            pltpu.VMEM((2, *tokens.shape), BF16),
+            pltpu.VMEM((2, *images.shape), BF16),
             dma((n_k, n_h, 2)), dma((n_k, n_h)), dma((2, n_k + 1)), dma((2, n_k + 1)),
             dma((2, 2 * (n_k + 1))), dma((2, 4 * (n_k + 1))), dma((2, 4)), dma((n_k + 1,)),
+            dma((2, 2)),
         ],
         compiler_params=pltpu.CompilerParams(
             collective_id=3, has_side_effects=True, vmem_limit_bytes=VMEM_BYTES
         ),
         name="gather_weights",
-    )(packet, extra, experts)
+    )(packet, extra, experts, tokens, cotangent)
 
 
 def reduce_kernel(
@@ -541,7 +581,8 @@
         lax.fori_loop(start, count, lambda k, carry: (function(k), carry)[1], 0)
 
     for p in range(2):
-        each(lambda k: block_out(p, k).start())
+        for k in range(1, n_blocks):
+            block_out(p, k).start()
         land[p, me] = blocks[h, s, p]
     few = half // 2
     group = 16
@@ -577,25 +618,22 @@
                 g_send.at[i, origin, up], g_recv.at[i, origin], line[1] if up else line[n_h - 1],
             )
 
-        def relay(wave):
-            for d in range(1, n_h):
-                i = wave - d + 1
-                if 0 <= i < own_images:
-                    @pl.when(h >= d)
-                    def _():
-                        z_hop(i, h - d, 1).wait_recv()
-
-                        @pl.when(h < n_h - 1)
-                        def _():
-                            z_hop(i, h - d, 1).start()
-
-                    @pl.when(h + d < n_h)
-                    def _():
-                        z_hop(i, h + d, 0).wait_recv()
-
-                        @pl.when(h > 0)
-                        def _():
-                            z_hop(i, h + d, 0).start()
+        def relay(i, d):
+            @pl.when(h >= d)
+            def _():
+                z_hop(i, h - d, 1).wait_recv()
+
+                @pl.when((h < n_h - 1) & (d < n_h - 1))
+                def _():
+                    z_hop(i, h - d, 1).start()
+
+            @pl.when(h + d < n_h)
+            def _():
+                z_hop(i, h + d, 0).wait_recv()
+
+                @pl.when((h > 0) & (d < n_h - 1))
+                def _():
+                    z_hop(i, h + d, 0).start()
 
         def gather_output():
             for i in range(own_images):
@@ -621,6 +659,8 @@
             bias[:, m * piece : (m + 1) * piece] = dot(jnp.concatenate(lines, axis=1), place)
 
     receive(0)
+    if backward:
+        gather_output()
     loads[0].wait()
 
     def core_copy(j):
@@ -658,8 +698,6 @@
 
     each(first_sums, few, 0)
     receive(1)
-    if backward:
-        gather_output()
     each(first_sums, half, few)
     meet(half - 1)
     loads[1].wait()
@@ -690,10 +728,10 @@
             second(other + j - 1)
 
         if backward:
-            for wave in range(3):
-                @pl.when(j == 3 + 2 * wave)
+            for when, i, d in ((2, 0, 1), (3, 1, 1), (5, 0, 2), (7, 1, 2)):
+                @pl.when(j == when)
                 def _():
-                    relay(wave)
+                    relay(i, d)
 
     def back_copy(p, k):
         place = peers.step(k, 1)
@@ -720,7 +758,8 @@
             ).reshape(group * 16, leave.shape[2])
             turned = dot(again, rows).astype(BF16)
             back[p, b * group : (b + 1) * group] = turned.reshape(group, 16, leave.shape[2])
-        each(lambda k: back_copy(p, k).start())
+        for k in range(1, n_blocks):
+            back_copy(p, k).start()
         land_back[p, me] = back[p, me]
 
     each(finish, few + 1, 0)
@@ -763,7 +802,8 @@
     for store in stores:
         store.wait()
     if backward:
-        relay(3)
+        relay(0, 3)
+        relay(1, 3)
         g_own.wait()
         for origin in range(n_h):
             @pl.when((origin < h) & (h < n_h - 1))
@@ -1287,6 +1327,31 @@
     )(back, small, weights, tokens, *kept, grad_logits, cotangent)
 
 
+def unpack_kernel(block, summed, attn, phi, scales, biases):
+    attn[...] = summed[:, :, :block]
+    rest = summed[0][:, 128:]
+    phi[...] = pltpu.roll(rest, 64, 1)[:, : phi.shape[1]]
+    turned = jnp.swapaxes(rest, 0, 1)
+    scales[...] = turned[80:82]
+    biases[...] = turned[82:84]
+
+
+def unpack_grads(summed, block, slot):
+    n_k, rows, _ = summed.shape
+    vmem = pl.BlockSpec(memory_space=pltpu.VMEM)
+    shape = jax.ShapeDtypeStruct
+    return pl.pallas_call(
+        partial(unpack_kernel, block),
+        out_shape=(
+            shape((n_k, rows, block), F32), shape((rows, slot), F32),
+            shape((2, rows), F32), shape((2, rows), F32),
+        ),
+        in_specs=[vmem],
+        out_specs=(vmem,) * 4,
+        name="unpack_grads",
+    )(summed)
+
+
 def normalize(values, scale, shift):
     centered = values - jnp.mean(values, axis=-1, keepdims=True)
     variance = jnp.mean(centered * centered, axis=-1, keepdims=True)
@@ -1466,10 +1531,9 @@
     sizes = tuple(lax.axis_size(name) for name in ("shard", "heads", "tensor"))
     group, length, width = tokens.shape
     fits = (sizes, group, width, *experts.shape[:3]) == ((4, 4, 2), 8, 768, 192, 2, 16)
-    if not fits or length > 208 or in_bias.shape[1] != 384:
+    if not fits or not 192 < length <= 208 or in_bias.shape[1] != 384:
         return general_shards(*arrays)
     n_s, n_h, n_t = sizes
-    own = group // n_h
     block, slot = w_attn.shape[2], phi.shape[1]
     beside = jnp.concatenate((phi, out_bias.T), axis=1)
     beside = jnp.pad(beside, ((0, 0), (0, 256 - block - 2 * slot)))
@@ -1478,13 +1542,12 @@
     hidden_bias = in_bias.reshape(16, 6, 64).transpose(1, 0, 2).reshape(96, 64)
     extra = jnp.concatenate((hidden_bias, norm_scales.T, norm_biases.T), axis=1)
     extra = jnp.pad(extra, ((0, 0), (128, 60)))
-    attn, small, turned = gather_weights(sizes, packet, extra, experts)
-
-    def mine(values):
-        values = lax.dynamic_slice_in_dim(values, lax.axis_index("heads") * own, own, 0)
-        return jnp.pad(values, ((0, 0), (0, 208 - length), (0, 0)))
-
-    tokens, cotangent = mine(tokens), mine(cotangent)
+    tokens, cotangent = (
+        values.transpose(1, 0, 2).reshape(group * length, width) for values in (tokens, cotangent)
+    )
+    attn, small, turned, tokens, cotangent = gather_weights(
+        sizes, packet, extra, experts, tokens, cotangent
+    )
     blocks, *kept, combine = tokens_ahead(sizes, length, tokens, small, attn)
     hidden = kept[5]
     slot_in, activated, gate, back = expert_pass(sizes, False, blocks, turned, small)
@@ -1500,17 +1563,17 @@
     experts_grad = weight_grads(slot_in, grad_pre, grad_slot, activated)
     attn_grad, experts_grad = lax.optimization_barrier((attn_grad, experts_grad))
     summed = reduce_grads(sizes, attn_grad, small_grad)
-    norms = summed[0, :, block + slot : block + slot + 4].T
+    attn_grad, phi_grad, scales_grad, biases_grad = unpack_grads(summed, block, slot)
     out_bias_grad = lax.dynamic_slice_in_dim(
         out_sum, lax.axis_index("tensor") * out_bias.shape[1], out_bias.shape[1], 1
     )
     return (
         output[:, :length],
         input_grad[:, :length],
-        norms[:2],
-        norms[2:],
-        summed[:, :, :block],
-        summed[0, :, block : block + slot],
+        scales_grad,
+        biases_grad,
+        attn_grad,
+        phi_grad,
         experts_grad,
         in_bias_grad,
         out_bias_grad,

time: 340 us -> 333 us (0.979)
  local copies, waits for them, and re-layouts: 17.5 us -> 10.9 us
    pallas_call x2, Pallas kernels: 148 us -> 143 us  [expert_pass(): pl.pallas_call(partial(expert_kernel, sizes, backward), out_shape=outs, i...]
    dynamic_slice x1 -> x0, local copies, waits for them, and re-layouts: 3.67 us -> none  [mine(): lax.dynamic_slice_in_dim(values, lax.axis_index('heads') * own, own, 0)]
    unnamed x31 -> x12, local copies, waits for them, and re-layouts: 7.5 us -> 7.4 us
  transfers between devices with their start and end apart: 1 -> 1, of which waited for: 0 -> 0; matrix products, arithmetic and copies ran while one was open for 2% -> 1% of each run, Pallas kernels for 21% -> 22%
where the time goes in v3:
time: 333 us; the launch traced here: 332 us
  Pallas kernels  304 us (91%)
  between operations  14.1 us (4%)
  local copies, waits for them, and re-layouts  10.9 us (3%)
    pallas_call x2, Pallas kernels, expert_pass(): pl.pallas_call(partial(expert_kernel, sizes, backward), out_shape=outs, i...  143 us
    pallas_call x1, Pallas kernels, reduce_grads(): pl.pallas_call(partial(reduce_kernel, sizes), out_shape=jax.ShapeDtypeStr...  49 us
    pallas_call x1, Pallas kernels, gather_weights(): pl.pallas_call(partial(gather_kernel, sizes), out_shape=(jax.ShapeDtypeSt...  43.5 us
    pallas_call x1, Pallas kernels, tokens_behind(): pl.pallas_call(partial(behind_kernel, sizes, length), out_shape=(shape((4...  27.4 us
    pallas_call x1, Pallas kernels, weight_grads(): pl.pallas_call(weight_grad_kernel, grid=(2, experts // group, rows // d_b...  21 us
    pallas_call x1, Pallas kernels, tokens_ahead(): pl.pallas_call(partial(ahead_kernel, length), out_shape=(shape((sizes[1],...  14 us
    unnamed x12, local copies, waits for them, and re-layouts  7.4 us
  transfers between devices with their start and end apart: 1, of which 0 were waited for; matrix products, arithmetic and copies ran while one was open for 1% of the time, Pallas kernels for 22%

profile of v3, /device:TPU:0, one launch (start us, length us, event | category | flops | bytes accessed | tf_op | source)
XLA Modules:
  0.0 332.1 jit_solution(16040758145307739191)
XLA Ops:
  7.2 0.0 all-gather.2.cloned.1.call-start
  7.2 0.7 pad_maximum_fusion
  7.9 0.1 copy.34
  8.1 0.8 reshape.30
  8.9 0.8 copy.36
  9.7 0.8 copy.37
  10.4 1.7 fusion.1.packet
  12.1 0.7 fusion.7.extra
  12.8 43.5 %gather_weights.1 = (bf16[4,768,768]{2,1,0:T(8,128)(2,1)}, bf16[768,256]{1,0:T(8,128)(2,1)}, bf16[2,16,192,1536]{3,2,1,0:T(8,128)(2,1)}, bf16[2,208,768]{2,1,0:T(8,128)(2,1)}, bf16[2,208,768]{2,1,0:T(8,128)(2,1)}) custom-call(bf16[4,96,256]{2,1,0:T(8,128)(2,1)} %fusion.1.packet, bf16[96,256]{1,0:T(8,128)(2,1)} %fusion.7.extra, ...), custom_call_target="tpu_custom_call" | custom-call | tf_op jit(solution)/shard_map/gather_weights/pallas_call | solution.py:334
  56.3 14.0 %tokens_ahead.1 = (bf16[4,4,2,16,192]{4,3,2,1,0:T(8,128)(2,1)}, bf16[2,208,768]{2,1,0:T(8,128)(2,1)}, bf16[2,208,768]{2,1,0:T(8,128)(2,1)}, bf16[2,256,768]{2,1,...) custom-call(bf16[2,208,768]{2,1,0:T(8,128)(2,1)} %get-tuple-element., ...), custom_call_target="tpu_custom_call" | custom-call | tf_op jit(solution)/shard_map/tokens_ahead/pallas_call | solution.py:1148
  70.3 68.1 %experts_ahead.1 = (bf16[16,64,192]{2,1,0:T(8,128)(2,1)}, bf16[16,64,1536]{2,1,0:T(8,128)(2,1)}, f32[8,64,1536]{2,1,0:T(8,128)}, bf16[2,32,16,192]{3,2,1,0:T(8,128)(2,1)}) custom-call(bf16[4,4,2,16,192]{4,3,2,1,0:T(8,128)(2,1)} %get-tuple-element.51.refs_0_, bf16[2,16,192,1536]{3,2,1,0:T(8,128)(2,1)} %get-tuple-element.52.refs_1_, ...), custom_call_target="tpu_custom_call" | custom-call | flops 2415919104 | bytes 18874368 | tf_op jit(solution)/shard_map/experts_ahead/pallas_call | solution.py:886
  138.5 4.1 %tokens_middle.1 = (bf16[2,208,768]{2,1,0:T(8,128)(2,1)}, bf16[4,4,2,16,192]{4,3,2,1,0:T(8,128)(2,1)}, f32[2,208,64]{2,1,0:T(8,128)}) custom-call(bf16[2,32,16,192]{3,2,1,0:T(8,128)(2,1)} %get-tuple-element.53.back, bf16[768,256]{1,0:T(8,128)(2,1)} %get-tuple-element.49.small.refs_2_, f32[2,208,128]{2,1,0:T(8,128)} %get-tuple-element.54.combine, ...), custom_call_target="tpu_custom_call" | custom-call | tf_op jit(solution)/shard_map/tokens_middle/pallas_call | solution.py:1198
  142.5 75.2 %experts_back.1 = (bf16[16,64,192]{2,1,0:T(8,128)(2,1)}, bf16[16,64,1536]{2,1,0:T(8,128)(2,1)}, bf16[2,32,16,192]{3,2,1,0:T(8,128)(2,1)}, f32[16,384]{1,0:T(8,12...) custom-call(bf16[4,4,2,16,192]{4,3,2,1,0:T(8,128)(2,1)} %get-tuple-element.57.refs_0_, ...), custom_call_target="tpu_custom_call" | custom-call | flops 2415919104 | bytes 18874368 | tf_op jit(solution)/shard_map/experts_back/pallas_call | solution.py:886
  217.7 27.4 %tokens_behind.1 = (bf16[4,768,768]{2,1,0:T(8,128)(2,1)}, bf16[768,128]{1,0:T(8,128)(2,1)}, bf16[2,208,768]{2,1,0:T(8,128)(2,1)}) custom-call(bf16[2,32,16,192]{3,2,1,0:T(8,128)(2,1)} %get-tuple-element.61.back, bf16[768,256]{1,0:T(8,128)(2,1)} %get-tuple-element.49.small.refs_2_, bf16[4,768,768]{2,1,0:T(8,128)(2,1)} %get-tuple-element.50.w_hbm, ...), custom_call_target="tpu_custom_call" | custom-call | tf_op jit(solution)/shard_map/tokens_behind/pallas_call | solution.py:1311
  245.1 0.0 all-gather.2.cloned.1.call-update
  245.1 21.0 %weight_grads.1 = f32[192,2,16,1536]{3,2,1,0:T(8,128)} custom-call(bf16[16,64,192]{2,1,0:T(8,128)(2,1)} %get-tuple-element.74.slots_0, bf16[16,64,1536]{2,1,0:T(8,128)(2,1)} %get-tuple-element.75.act_0, bf16[16,64,192]{2,1,0:T(8,128)(2,1)} %get-tuple-element.76.slots_1, bf16[16,64,1536]{2,1,0:T(8,128)(2,1)} %get-tuple-element.77.act_1), custom_call_target="tpu_custom_call" | custom-call | flops 1207959552 | bytes 37748736 | tf_op jit(solution)/shard_map/weight_grads/pallas_call | solution.py:955
  266.1 0.0 copy-start
  266.1 49.0 %reduce_grads.1.summed = f32[4,96,256]{2,1,0:T(8,128)} custom-call(bf16[4,768,768]{2,1,0:T(8,128)(2,1)} %get-tuple-element.78.grads, bf16[768,128]{1,0:T(8,128)(2,1)} %get-tuple-element.79.small), custom_call_target="tpu_custom_call" | custom-call | tf_op jit(solution)/shard_map/reduce_grads/pallas_call | solution.py:514
  315.1 1.8 unpack_grads.1
  316.9 1.5 copy.40
  318.4 0.0 copy-done
  318.4 0.2 slice.6
  318.5 0.0 copy-start.2
  318.5 1.9 copy.38
  320.4 0.0 copy-done.2
  320.4 0.7 constant_dynamic-slice_fusion
  321.1 0.0 all-gather.2.cloned.1.call-done
  321.1 0.0 slice-start
  321.1 1.7 slice-done
  322.8 0.0 copy-start.1
  322.8 1.9 copy.39
  324.7 0.0 copy-done.1
  324.7 0.6 copy.42
  (2 shorter events, 0.0 us)
Async XLA Ops:
  7.2 313.9 %all-gather.2.cloned.1.call-start = ((), (), s32[]{:S(2)}) async-start(), calls=%async_computation | async-start | bytes 3194880 | tf_op jit(solution)/shard_map/all_gather | solution.py:1561
  266.1 52.2 %copy-start = (bf16[8,208,768]{2,1,0:T(8,128)(2,1)S(1)}, bf16[8,208,768]{2,1,0:T(8,128)(2,1)}, u32[]{:S(2)}) copy-start(bf16[8,208,768]{2,1,0:T(8,128)(2,1)} %get-tuple-element.60) | copy-start | bytes 7667716
  318.5 1.9 copy-start.2
  321.1 1.7 slice-start
  322.8 1.9 copy-start.1
Sparse Core Ops, SparseCore 0:
  245.2 65.3 all-gather.1

commit v4 on v3

--- a/solution.py
+++ b/solution.py
@@ -91,15 +91,24 @@
 
 
 def gather_kernel(
-    sizes, packet, extra, experts, tokens, cotangent, w_out, small_out, turned, own_tokens, own_cot,
-    w, small, lined, tile_in, tile_out, images, picked,
+    sizes, w_attn, phi_t, out_bias, scales, biases, in_bias, experts, tokens, cotangent, w_out, small_out, turned, own_tokens, own_cot,
+    w, small, lined, extra, stage, tile_in, tile_out, images, picked,
     z_send, z_recv, x_sems, y_sems, d_sems, c_sems, t_sems, o_sems, i_sems,
 ):
+    n_k, rows, block = w_attn.shape
+    wide = lined.shape[3]
+    slot = phi_t.shape[0]
+    own_h = lax.axis_index("heads")
+    stage[...] = jnp.zeros_like(stage)
+    stage[64 : 64 + slot] = phi_t[...].astype(F32)
+    stage[64 + slot : 64 + 2 * slot] = out_bias[...].astype(F32)
+    lined[own_h, :, :, 128:] = jnp.zeros((n_k, rows, wide - 128), BF16)
+    lined[own_h, :, :, :block] = w_attn[...]
+    first = lined[own_h, 0, :, 128:].astype(F32) + jnp.swapaxes(stage[...], 0, 1)
+    lined[own_h, 0, :, 128:] = first.astype(BF16)
     (s, h, t), core, chip, sibling, across_x, across_y, line = plane(sizes)
-    n_k, rows, wide = packet.shape
     n_h, n_t = sizes[1], sizes[2]
     width = w.shape[2]
-    block = width // n_h
     side = 16
     n_tiles = experts.shape[0] // side
     depth = tile_in.shape[0]
@@ -130,7 +139,6 @@
                 z_hop(k, h + d, 0).start()
 
     chunks = (0, 2, 1, 3)
-    lined[h] = packet[...]
     for k in chunks:
         @pl.when(h < n_h - 1)
         def _():
@@ -194,6 +202,20 @@
     beside = (lane >= 0) & (lane < 16) & (column == of * 16 + lane)
     beside |= (lane >= 16) & (lane < 32) & (column == n_h * 16 + of * 16 + lane - 16)
     beside = beside.astype(F32).astype(BF16)
+
+    stage[...] = jnp.zeros_like(stage)
+    stage[64:66] = scales[...].astype(F32)
+    stage[66:68] = biases[...].astype(F32)
+    norms = jnp.swapaxes(stage[...], 0, 1)
+    pieces = []
+    for j in range(in_bias.shape[1] // 64):
+        shape = (in_bias.shape[1], 128)
+        row = lax.broadcasted_iota(jnp.int32, shape, 0)
+        column = lax.broadcasted_iota(jnp.int32, shape, 1)
+        chosen = ((row == 64 * j + column) & (column < 64)).astype(F32).astype(BF16)
+        pieces.append(dot(in_bias[...], chosen))
+    extra[:, :128] = jnp.zeros((rows, 128), F32)
+    extra[:, 128:] = jnp.concatenate(pieces, axis=0) + norms
 
     image_stores = [
         pltpu.make_async_copy(picked.at[j], target, i_sems.at[1, j])
@@ -247,7 +269,7 @@
             at(k, me)[:, i * block : (i + 2) * block] = dot(lines, pair).astype(BF16)
         if k == 0:
             lines = jnp.concatenate([lined[i, k] for i in range(n_h)], axis=1)
-            at(n_k, me)[...] = (dot(lines, beside) + extra[...].astype(F32)).astype(BF16)
+            at(n_k, me)[...] = (dot(lines, beside) + extra[...]).astype(BF16)
         for q in members(k):
             send(hop(q, me, across_x, x_sems, q))
             send(hop(q, me, across_y, y_sems, q))
@@ -321,15 +343,18 @@
         copy.wait()
 
 
-def gather_weights(sizes, packet, extra, experts, tokens, cotangent):
-    n_k, rows, wide = packet.shape
+def gather_weights(
+    sizes, w_attn, phi_t, out_bias, scales, biases, in_bias, experts, tokens, cotangent
+):
+    n_k, rows, _ = w_attn.shape
+    wide = 256
     n_s, n_h, n_t = sizes
     width = n_s * n_t * rows
     vmem = pl.BlockSpec(memory_space=pltpu.VMEM)
     hbm = pl.BlockSpec(memory_space=pl.ANY)
     dma = pltpu.SemaphoreType.DMA
     hidden = experts.shape[3]
-    small = (width, extra.shape[1])
+    small = (width, wide)
     images = jax.ShapeDtypeStruct((2, 208, width), BF16)
     return pl.pallas_call(
         partial(gather_kernel, sizes),
@@ -339,12 +364,14 @@
             jax.ShapeDtypeStruct((2, experts.shape[2], experts.shape[0], hidden), BF16),
             images, images,
         ),
-        in_specs=[vmem, vmem, hbm, hbm, hbm],
+        in_specs=[vmem] * 6 + [hbm] * 3,
         out_specs=(hbm,) * 5,
         scratch_shapes=[
             pltpu.VMEM((n_k, width, width), BF16),
             pltpu.VMEM(small, BF16),
             pltpu.VMEM((n_h, n_k, rows, wide), BF16),
+            pltpu.VMEM((rows, wide), F32),
+            pltpu.VMEM((128, rows), F32),
             pltpu.VMEM((4, 16, 16, hidden), BF16),
             pltpu.VMEM((4, 16, 16, hidden), BF16),
             pltpu.VMEM((2, *tokens.shape), BF16),
@@ -357,13 +384,13 @@
             collective_id=3, has_side_effects=True, vmem_limit_bytes=VMEM_BYTES
         ),
         name="gather_weights",
-    )(packet, extra, experts, tokens, cotangent)
+    )(w_attn, phi_t, out_bias, scales, biases, in_bias, experts, tokens, cotangent)
 
 
 def reduce_kernel(
     sizes, grads, small, out, core_in, core_small, met, met_small,
     d_in, d_small, x_in, x_small, y_in, y_small, pieces, z_in,
-    c_sems, d_sems, x_sems, y_sems, z_sems,
+    c_sems, d_sems, x_sems, y_sems, z_send, z_recv,
 ):
     (s, h, t), core, chip, sibling, across_x, across_y, line = plane(sizes)
     n_k, width, _ = grads.shape
@@ -452,10 +479,25 @@
         total = pick(q, met, met_small)[chip, t].astype(F32) + pick(q, *to_x)[...].astype(F32)
         return (total + pick(q, *to_y)[...].astype(F32)).astype(BF16)
 
-    def z_copy(k, d):
+    def z_copy(k, target, up):
+        place = line[1] if up else line[n_h - 1]
         return remote(
-            pieces.at[line[d][1], k], z_in.at[h, k], z_sems.at[0, k, d], z_sems.at[1, k, d], line[d]
+            pieces.at[target, k], z_in.at[up, target, k],
+            z_send.at[up, target, k], z_recv.at[up, target, k], place,
         )
+
+    def pass_along(k, hops):
+        for up in range(2):
+            for target in range(n_h - 1, -1, -1) if up else range(n_h):
+                further = target > h if up else target < h
+
+                @pl.when(further & (h == (hops if up else n_h - 1 - hops)))
+                def _():
+                    if hops > 0:
+                        z_copy(k, target, up).wait_recv()
+                        total = pieces[target, k].astype(F32) + z_in[up, target, k].astype(F32)
+                        pieces[target, k] = total.astype(BF16)
+                    z_copy(k, target, up).start()
 
     def share_out(k):
         value = whole(k)
@@ -468,34 +510,40 @@
                 lanes = lanes + little[:, i * wide : (i + 2) * wide]
             pieces[i, k] = lanes[:, :wide].astype(BF16)
             pieces[i + 1, k] = lanes[:, wide:].astype(BF16)
-        for d in range(n_h - 1, 0, -1):
-            z_copy(k, d).start()
-
-    for i in range(n_k + 2):
+        pass_along(k, 0)
+
+    for i in range(n_k + 2 + n_h - 2):
         if i < n_k:
             for q in members(chunks[i]):
                 open_up(q)
         if 0 <= i - 1 < n_k:
             for q in members(chunks[i - 1]):
                 pass_on(q)
-        if i >= 2:
+        if 0 <= i - 2 < n_k:
             share_out(chunks[i - 2])
+        for hops in range(1, n_h - 1):
+            if 0 <= i - 2 - hops < n_k:
+                pass_along(chunks[i - 2 - hops], hops)
     for k in chunks:
-        total = pieces[h, k].astype(F32)
-        for d in range(1, n_h):
-            z_copy(k, d).wait_recv()
-        for d in range(1, n_h):
-            total = total + z_in[line[d][1], k].astype(F32)
-        out[k] = total
+        out[k] = pieces[h, k].astype(F32)
+        for up, there in ((1, h > 0), (0, h < n_h - 1)):
+            @pl.when(there)
+            def _():
+                z_copy(k, h, up).wait_recv()
+                out[k] = out[k] + z_in[up, h, k].astype(F32)
+
     for k in chunks:
         for q in members(k):
             for x in range(2):
                 core_copy(q, x).wait_send()
     for copy in sent:
         copy.wait_send()
-    for k in range(n_k):
-        for d in range(1, n_h):
-            z_copy(k, d).wait_send()
+    for target in range(n_h):
+        for up in range(2):
+            @pl.when(target > h if up else target < h)
+            def _():
+                for k in range(n_k):
+                    z_copy(k, target, up).wait_send()
 
 
 def reduce_grads(sizes, grads, small):
@@ -520,9 +568,9 @@
             *buffers(2, n_t * rows), *buffers(2, n_t, rows),
             *buffers(2, rows // 2), *buffers(rows), *buffers(rows),
             pltpu.VMEM((n_h, n_k, rows, wide), BF16),
-            pltpu.VMEM((n_h, n_k, rows, wide), BF16),
+            pltpu.VMEM((2, n_h, n_k, rows, wide), BF16),
             dma((2, 2 * (n_k + 1))), dma((2, 2 * (n_k + 1))), dma((2, 2 * (n_k + 1))),
-            dma((2, 2 * (n_k + 1))), dma((2, n_k, n_h)),
+            dma((2, 2 * (n_k + 1))), dma((2, n_h, n_k)), dma((2, n_h, n_k)),
         ],
         compiler_params=pltpu.CompilerParams(
             collective_id=4, has_side_effects=True, vmem_limit_bytes=VMEM_BYTES
@@ -690,11 +738,12 @@
     def first_sums(j):
         core_out[j] = dot(slots[other + j], w_a[other + j]).astype(BF16)
         core_copy(j).start()
-        sums[j] = dot(slots[own + j], w_a[own + j])
 
         @pl.when(j > 0)
         def _():
             meet(j - 1)
+
+        sums[j] = dot(slots[own + j], w_a[own + j])
 
     each(first_sums, few, 0)
     receive(1)
@@ -1099,13 +1148,14 @@
         i = step // pairs
         lanes = pl.ds(pl.multiple_of((step % pairs) * 128, 128), 128)
         q, k, v = query[i, :, lanes], keyed[i, :, lanes], valued[i, :, lanes]
+        scaled = q * jnp.bfloat16(factor)
         parts = []
         for a in range(2):
             mine = (lane < 64) if a == 0 else (lane >= 64)
-            scores = dot_t(jnp.where(mine, q, jnp.zeros_like(q)), k) * factor
+            scores = dot_t(jnp.where(mine, scaled, jnp.zeros_like(q)), k)
             scores = jnp.where(shown, scores, -1e30)
             exponent = jnp.exp(scores - jnp.max(scores, axis=-1, keepdims=True))
-            probs = exponent / jnp.sum(exponent, axis=-1, keepdims=True)
+            probs = exponent * (1.0 / jnp.sum(exponent, axis=-1, keepdims=True))
             parts.append(dot(probs.astype(BF16), v))
         context[i, :, lanes] = jnp.where(lane < 64, parts[0], parts[1]).astype(BF16)
         return carry
@@ -1259,15 +1309,16 @@
         i = step // pairs
         lanes = pl.ds(pl.multiple_of((step % pairs) * 128, 128), 128)
         q, k, v = query[i, :, lanes], keyed[i, :, lanes], valued[i, :, lanes]
+        scaled = q * jnp.bfloat16(factor)
         g = grad_context[i, :, lanes]
         to_q, to_k, to_v = [], [], []
         for a in range(2):
             mine = (lane < 64) if a == 0 else (lane >= 64)
-            scores = dot_t(jnp.where(mine, q, jnp.zeros_like(q)), k) * factor
+            scores = dot_t(jnp.where(mine, scaled, jnp.zeros_like(q)), k)
             grad_probs = dot_t(jnp.where(mine, g, jnp.zeros_like(g)), v)
             scores = jnp.where(shown, scores, -1e30)
             exponent = jnp.exp(scores - jnp.max(scores, axis=-1, keepdims=True))
-            probs = exponent / jnp.sum(exponent, axis=-1, keepdims=True)
+            probs = exponent * (1.0 / jnp.sum(exponent, axis=-1, keepdims=True))
             weighted = jnp.sum(probs * grad_probs, axis=-1, keepdims=True)
             grad_scores = (probs * (grad_probs - weighted)).astype(BF16)
             to_v.append(dot_r(probs.astype(BF16), g))
@@ -1535,18 +1586,11 @@
         return general_shards(*arrays)
     n_s, n_h, n_t = sizes
     block, slot = w_attn.shape[2], phi.shape[1]
-    beside = jnp.concatenate((phi, out_bias.T), axis=1)
-    beside = jnp.pad(beside, ((0, 0), (0, 256 - block - 2 * slot)))
-    beside = jnp.concatenate((beside[None], jnp.zeros((3, *beside.shape), BF16)), axis=0)
-    packet = jnp.concatenate((w_attn, beside), axis=2)
-    hidden_bias = in_bias.reshape(16, 6, 64).transpose(1, 0, 2).reshape(96, 64)
-    extra = jnp.concatenate((hidden_bias, norm_scales.T, norm_biases.T), axis=1)
-    extra = jnp.pad(extra, ((0, 0), (128, 60)))
     tokens, cotangent = (
         values.transpose(1, 0, 2).reshape(group * length, width) for values in (tokens, cotangent)
     )
     attn, small, turned, tokens, cotangent = gather_weights(
-        sizes, packet, extra, experts, tokens, cotangent
+        sizes, w_attn, phi.T, out_bias, norm_scales, norm_biases, in_bias, experts, tokens, cotangent
     )
     blocks, *kept, combine = tokens_ahead(sizes, length, tokens, small, attn)
     hidden = kept[5]
@@ -1561,14 +1605,17 @@
     input_grad = lax.all_gather(input_grad, "heads", axis=0, tiled=True)
     attn_grad, grad_pre = lax.optimization_barrier((attn_grad, grad_pre))
     experts_grad = weight_grads(slot_in, grad_pre, grad_slot, activated)
-    attn_grad, experts_grad = lax.optimization_barrier((attn_grad, experts_grad))
+    output = output[:, :length].transpose(1, 0, 2)
+    out_bias_grad = lax.dynamic_slice_in_dim(
+        out_sum, lax.axis_index("tensor") * out_bias.shape[1], out_bias.shape[1], 1
+    )
+    attn_grad, experts_grad, output, out_bias_grad = lax.optimization_barrier(
+        (attn_grad, experts_grad, output, out_bias_grad)
+    )
     summed = reduce_grads(sizes, attn_grad, small_grad)
     attn_grad, phi_grad, scales_grad, biases_grad = unpack_grads(summed, block, slot)
-    out_bias_grad = lax.dynamic_slice_in_dim(
-        out_sum, lax.axis_index("tensor") * out_bias.shape[1], out_bias.shape[1], 1
-    )
     return (
-        output[:, :length],
+        output.transpose(1, 0, 2),
         input_grad[:, :length],
         scales_grad,
         biases_grad,

time: 333 us -> 338 us (1.015); the launches traced: 332 us -> 333 us
  Pallas kernels: 304 us -> 310 us
    pallas_call x1, Pallas kernels: 27.4 us -> 36.7 us  [tokens_behind(): pl.pallas_call(partial(behind_kernel, sizes, length), out_shape=(shape((4...]
    unnamed x12 -> x10, local copies, waits for them, and re-layouts: 7.4 us -> 5.85 us
  transfers between devices with their start and end apart: 1 -> 1, of which waited for: 0 -> 0; matrix products, arithmetic and copies ran while one was open for 1% -> 1% of each run, Pallas kernels for 22% -> 21%
where the time goes in v4:
time: 338 us; the launch traced here: 333 us
  Pallas kernels  310 us (92%)
  between operations  14.3 us (4%)
  local copies, waits for them, and re-layouts  8.38 us (2%)
    pallas_call x2, Pallas kernels, expert_pass(): pl.pallas_call(partial(expert_kernel, sizes, backward), out_shape=outs, i...  143 us
    pallas_call x1, Pallas kernels, reduce_grads(): pl.pallas_call(partial(reduce_kernel, sizes), out_shape=jax.ShapeDtypeStr...  46.1 us
    pallas_call x1, Pallas kernels, gather_weights(): pl.pallas_call(partial(gather_kernel, sizes), out_shape=(jax.ShapeDtypeSt...  43.6 us
    pallas_call x1, Pallas kernels, tokens_behind(): pl.pallas_call(partial(behind_kernel, sizes, length), out_shape=(shape((4...  36.7 us
    pallas_call x1, Pallas kernels, weight_grads(): pl.pallas_call(weight_grad_kernel, grid=(2, experts // group, rows // d_b...  21.1 us
    pallas_call x1, Pallas kernels, tokens_ahead(): pl.pallas_call(partial(ahead_kernel, length), out_shape=(shape((sizes[1],...  14 us
  transfers between devices with their start and end apart: 1, of which 0 were waited for; matrix products, arithmetic and copies ran while one was open for 1% of the time, Pallas kernels for 21%

profile of v4, /device:TPU:0, one launch (start us, length us, event | category | flops | bytes accessed | tf_op | source)
XLA Modules:
  0.0 333.1 jit_solution(12010974288939745435)
XLA Ops:
  7.2 0.0 all-gather.2.cloned.1.call-start
  7.2 43.6 %gather_weights.1 = (bf16[4,768,768]{2,1,0:T(8,128)(2,1)}, bf16[768,256]{1,0:T(8,128)(2,1)}, bf16[2,16,192,1536]{3,2,1,0:T(8,128)(2,1)}, bf16[2,208,768]{2,1,0:T(8,128)(2,1)}, bf16[2,208,768]{2,1,0:T(8,128)(2,1)}) custom-call(bf16[4,96,192]{2,1,0:T(8,128)(2,1)} %w_attn.1, bf16[16,96]{1,0:T(8,128)(2,1)} %bitcast.13, bf16[16,96]{1,0:T(8,128)(2,1)} %out_bias.1, ...), custom_call_target="tpu_custom_call" | custom-call | tf_op jit(solution)/shard_map/gather_weights/pallas_call | solution.py:359
  50.9 14.0 %tokens_ahead.1 = (bf16[4,4,2,16,192]{4,3,2,1,0:T(8,128)(2,1)}, bf16[2,208,768]{2,1,0:T(8,128)(2,1)}, bf16[2,208,768]{2,1,0:T(8,128)(2,1)}, bf16[2,256,768]{2,1,...) custom-call(bf16[2,208,768]{2,1,0:T(8,128)(2,1)} %get-tuple-element., ...), custom_call_target="tpu_custom_call" | custom-call | tf_op jit(solution)/shard_map/tokens_ahead/pallas_call | solution.py:1198
  64.9 67.8 %experts_ahead.1 = (bf16[16,64,192]{2,1,0:T(8,128)(2,1)}, bf16[16,64,1536]{2,1,0:T(8,128)(2,1)}, f32[8,64,1536]{2,1,0:T(8,128)}, bf16[2,32,16,192]{3,2,1,0:T(8,128)(2,1)}) custom-call(bf16[4,4,2,16,192]{4,3,2,1,0:T(8,128)(2,1)} %get-tuple-element.53.refs_0_, bf16[2,16,192,1536]{3,2,1,0:T(8,128)(2,1)} %get-tuple-element.54.refs_1_, ...), custom_call_target="tpu_custom_call" | custom-call | flops 2415919104 | bytes 18874368 | tf_op jit(solution)/shard_map/experts_ahead/pallas_call | solution.py:935
  132.7 4.1 %tokens_middle.1 = (bf16[2,208,768]{2,1,0:T(8,128)(2,1)}, bf16[4,4,2,16,192]{4,3,2,1,0:T(8,128)(2,1)}, f32[2,208,64]{2,1,0:T(8,128)}) custom-call(bf16[2,32,16,192]{3,2,1,0:T(8,128)(2,1)} %get-tuple-element.55.back, bf16[768,256]{1,0:T(8,128)(2,1)} %get-tuple-element.51.small.refs_2_, f32[2,208,128]{2,1,0:T(8,128)} %get-tuple-element.56.combine, ...), custom_call_target="tpu_custom_call" | custom-call | tf_op jit(solution)/shard_map/tokens_middle/pallas_call | solution.py:1248
  136.8 75.2 %experts_back.1 = (bf16[16,64,192]{2,1,0:T(8,128)(2,1)}, bf16[16,64,1536]{2,1,0:T(8,128)(2,1)}, bf16[2,32,16,192]{3,2,1,0:T(8,128)(2,1)}, f32[16,384]{1,0:T(8,12...) custom-call(bf16[4,4,2,16,192]{4,3,2,1,0:T(8,128)(2,1)} %get-tuple-element.59.refs_0_, ...), custom_call_target="tpu_custom_call" | custom-call | flops 2415919104 | bytes 18874368 | tf_op jit(solution)/shard_map/experts_back/pallas_call | solution.py:935
  212.0 0.0 copy-start.2
  212.0 36.7 %tokens_behind.1 = (bf16[4,768,768]{2,1,0:T(8,128)(2,1)}, bf16[768,128]{1,0:T(8,128)(2,1)}, bf16[2,208,768]{2,1,0:T(8,128)(2,1)}) custom-call(bf16[2,32,16,192]{3,2,1,0:T(8,128)(2,1)} %get-tuple-element.62.back, bf16[768,256]{1,0:T(8,128)(2,1)} %get-tuple-element.51.small.refs_2_, bf16[4,768,768]{2,1,0:T(8,128)(2,1)} %get-tuple-element.52.w_hbm, ...), custom_call_target="tpu_custom_call" | custom-call | tf_op jit(solution)/shard_map/tokens_behind/pallas_call | solution.py:1362
  248.7 0.0 all-gather.2.cloned.1.call-update
  248.7 0.0 copy-done.2
  248.7 0.7 constant_dynamic-slice_fusion
  249.4 0.0 copy-start
  249.4 21.1 %weight_grads.1 = f32[192,2,16,1536]{3,2,1,0:T(8,128)} custom-call(bf16[16,64,192]{2,1,0:T(8,128)(2,1)} %get-tuple-element.74.slots_0, bf16[16,64,1536]{2,1,0:T(8,128)(2,1)} %get-tuple-element.75.act_0, bf16[16,64,192]{2,1,0:T(8,128)(2,1)} %get-tuple-element.76.slots_1, bf16[16,64,1536]{2,1,0:T(8,128)(2,1)} %get-tuple-element.77.act_1), custom_call_target="tpu_custom_call" | custom-call | flops 1207959552 | bytes 37748736 | tf_op jit(solution)/shard_map/weight_grads/pallas_call | solution.py:1004
  270.5 0.0 copy-done
  270.5 0.2 slice_bitcast_fusion
  270.7 1.9 copy.21
  272.6 46.1 %reduce_grads.1.summed = f32[4,96,256]{2,1,0:T(8,128)} custom-call(bf16[4,768,768]{2,1,0:T(8,128)(2,1)} %get-tuple-element.82.grads, bf16[768,128]{1,0:T(8,128)(2,1)} %get-tuple-element.83.small), custom_call_target="tpu_custom_call" | custom-call | tf_op jit(solution)/shard_map/reduce_grads/pallas_call | solution.py:562
  318.6 1.8 unpack_grads.1
  320.4 1.5 copy.23
  321.9 0.0 all-gather.2.cloned.1.call-done
  321.9 0.0 slice-start
  321.9 1.7 slice-done
  323.6 0.0 copy-start.1
  323.6 1.9 copy.22
  325.5 0.0 copy-done.1
  325.5 0.6 copy.25
Async XLA Ops:
  7.2 314.7 %all-gather.2.cloned.1.call-start = ((), (), s32[]{:S(2)}) async-start(), calls=%async_computation | async-start | bytes 3194880 | tf_op jit(solution)/shard_map/all_gather | solution.py:1605
  212.0 36.7 %copy-start.2 = (f32[16,192]{1,0:T(8,128)S(1)}, f32[16,192]{1,0:T(8,128)}, u32[]{:S(2)}) copy-start(f32[16,192]{1,0:T(8,128)} %get-tuple-element.79) | copy-start | bytes 36868
  249.4 21.1 %copy-start = (bf16[8,208,768]{2,1,0:T(8,128)(2,1)S(1)}, bf16[8,208,768]{2,1,0:T(8,128)(2,1)}, u32[]{:S(2)}) copy-start(bf16[8,208,768]{2,1,0:T(8,128)(2,1)} %get-tuple-element.78) | copy-start | bytes 7667716
  321.9 1.7 slice-start
  323.6 1.9 copy-start.1
Sparse Core Ops, SparseCore 0:
  248.8 53.8 all-gather.1

commit v5 on v4

--- a/solution.py
+++ b/solution.py
@@ -833,8 +833,10 @@
         each(bias_row, 2 * half, 0)
 
         def slot_row(e):
-            sum_out[pl.ds(e, 1), :] = jnp.sum(slots[e].astype(F32), axis=0, keepdims=True)
-
+            total = jnp.sum(slots[e].astype(F32), axis=0, keepdims=True)
+            sum_out[pl.ds(e, 1), : slots.shape[2]] = total
+
+        sum_out[...] = jnp.zeros_like(sum_out)
         each(slot_row, 2 * half, 0)
 
         def piece(for_t):
@@ -898,7 +900,7 @@
         outs = (
             slots, act, returned,
             jax.ShapeDtypeStruct((experts, bias_width), F32),
-            jax.ShapeDtypeStruct((experts, rows), F32),
+            jax.ShapeDtypeStruct((experts, 256), F32),
             jax.ShapeDtypeStruct((sizes[1] * output.shape[0], *output.shape[1:]), BF16),
         )
         out_specs = (vmem, hbm, vmem, vmem, vmem, hbm)
@@ -1378,29 +1380,70 @@
     )(back, small, weights, tokens, *kept, grad_logits, cotangent)
 
 
-def unpack_kernel(block, summed, attn, phi, scales, biases):
-    attn[...] = summed[:, :, :block]
-    rest = summed[0][:, 128:]
-    phi[...] = pltpu.roll(rest, 64, 1)[:, : phi.shape[1]]
-    turned = jnp.swapaxes(rest, 0, 1)
+def unpack_kernel(summed, in_bias_sum, out_sum, attn, phi_t, scales, biases, in_bias, out_bias):
+    attn[...] = summed[:, :, : attn.shape[2]]
+    turned = jnp.swapaxes(summed[0][:, 128:], 0, 1)
+    phi_t[...] = turned[64:80]
     scales[...] = turned[80:82]
     biases[...] = turned[82:84]
-
-
-def unpack_grads(summed, block, slot):
+    in_bias[...] = in_bias_sum[...]
+    width = out_bias.shape[1]
+    value = out_sum[...]
+    later = pltpu.roll(value, value.shape[1] - width, 1)
+    out_bias[...] = jnp.where(lax.axis_index("tensor") == 0, value[:, :width], later[:, :width])
+
+
+def unpack_grads(summed, in_bias_sum, out_sum, block, slot):
     n_k, rows, _ = summed.shape
     vmem = pl.BlockSpec(memory_space=pltpu.VMEM)
     shape = jax.ShapeDtypeStruct
     return pl.pallas_call(
-        partial(unpack_kernel, block),
+        unpack_kernel,
         out_shape=(
-            shape((n_k, rows, block), F32), shape((rows, slot), F32),
+            shape((n_k, rows, block), F32), shape((slot, rows), F32),
             shape((2, rows), F32), shape((2, rows), F32),
+            shape(in_bias_sum.shape, F32), shape((out_sum.shape[0], rows), F32),
         ),
-        in_specs=[vmem],
-        out_specs=(vmem,) * 4,
+        in_specs=[vmem] * 3,
+        out_specs=(vmem,) * 6,
         name="unpack_grads",
-    )(summed)
+    )(summed, in_bias_sum, out_sum)
+
+
+def order_kernel(*refs):
+    *parts, out = refs
+    h, n_h = lax.axis_index("heads"), len(parts)
+    own = parts[0].shape[0]
+    group = own * n_h
+    step = 256 // group
+    length = out.shape[0]
+    for first in range(0, length, step):
+        count = min(step, length - first)
+        taken = min(step, parts[0].shape[1] - first)
+        shape = (count * group, group * taken)
+        row = lax.broadcasted_iota(jnp.int32, shape, 0)
+        column = lax.broadcasted_iota(jnp.int32, shape, 1)
+        block = column // taken
+        image = lax.rem(h + n_h - block // own, n_h) * own + block % own
+        chosen = ((row // group == column % taken) & (row % group == image)).astype(F32)
+        lines = jnp.concatenate(
+            [part[i, first : first + taken] for part in parts for i in range(own)], axis=0
+        )
+        value = dot(chosen.astype(BF16), lines).astype(BF16)
+        out[first : first + count] = value.reshape(count, group, value.shape[1])
+
+
+def order_images(parts, length):
+    own, _, width = parts[0].shape
+    vmem = pl.BlockSpec(memory_space=pltpu.VMEM)
+    return pl.pallas_call(
+        order_kernel,
+        out_shape=jax.ShapeDtypeStruct((length, own * len(parts), width), BF16),
+        in_specs=[vmem] * len(parts),
+        out_specs=vmem,
+        compiler_params=pltpu.CompilerParams(vmem_limit_bytes=24 * 1024 * 1024),
+        name="order_images",
+    )(*parts)
 
 
 def normalize(values, scale, shift):
@@ -1602,25 +1645,26 @@
     attn_grad, small_grad, input_grad = tokens_behind(
         sizes, length, back, small, attn, tokens, kept, grad_logits, cotangent
     )
-    input_grad = lax.all_gather(input_grad, "heads", axis=0, tiled=True)
+    parts = [input_grad] + [
+        lax.ppermute(input_grad, "heads", [(i, (i + d) % n_h) for i in range(n_h)])
+        for d in range(1, n_h)
+    ]
     attn_grad, grad_pre = lax.optimization_barrier((attn_grad, grad_pre))
     experts_grad = weight_grads(slot_in, grad_pre, grad_slot, activated)
     output = output[:, :length].transpose(1, 0, 2)
-    out_bias_grad = lax.dynamic_slice_in_dim(
-        out_sum, lax.axis_index("tensor") * out_bias.shape[1], out_bias.shape[1], 1
-    )
-    attn_grad, experts_grad, output, out_bias_grad = lax.optimization_barrier(
-        (attn_grad, experts_grad, output, out_bias_grad)
-    )
+    attn_grad, experts_grad, output = lax.optimization_barrier((attn_grad, experts_grad, output))
     summed = reduce_grads(sizes, attn_grad, small_grad)
-    attn_grad, phi_grad, scales_grad, biases_grad = unpack_grads(summed, block, slot)
+    attn_grad, phi_grad, scales_grad, biases_grad, in_bias_grad, out_bias_grad = unpack_grads(
+        summed, in_bias_grad, out_sum, block, slot
+    )
+    input_grad = order_images(parts, length)
     return (
         output.transpose(1, 0, 2),
-        input_grad[:, :length],
+        input_grad.transpose(1, 0, 2),
         scales_grad,
         biases_grad,
         attn_grad,
-        phi_grad,
+        phi_grad.T,
         experts_grad,
         in_bias_grad,
         out_bias_grad,

time: 338 us -> 323 us (0.956)
  between operations: 14.3 us -> 0.92 us
  local copies, waits for them, and re-layouts: 8.38 us -> 2.05 us
  starting transfers between devices: 0.04 us -> 3.87 us
    unnamed x10 -> x5, local copies, waits for them, and re-layouts: 5.85 us -> 1.89 us
    ppermute x0 -> x3, starting transfers between devices: none -> 3.87 us  [shards(): lax.ppermute(input_grad, 'heads', [(i, (i + d) % n_h) for i in range(n_h)])]
  transfers between devices with their start and end apart: 1 -> 3, of which waited for: 0 -> 0; matrix products, arithmetic and copies ran while one was open for 1% -> 1% of each run, Pallas kernels for 21% -> 21%
where the time goes in v5:
time: 323 us; the launch traced here: 318 us
  Pallas kernels  311 us (96%)
  starting transfers between devices  3.87 us (1%)
    pallas_call x2, Pallas kernels, expert_pass(): pl.pallas_call(partial(expert_kernel, sizes, backward), out_shape=outs, i...  143 us
    pallas_call x1, Pallas kernels, reduce_grads(): pl.pallas_call(partial(reduce_kernel, sizes), out_shape=jax.ShapeDtypeStr...  44.5 us
    pallas_call x1, Pallas kernels, gather_weights(): pl.pallas_call(partial(gather_kernel, sizes), out_shape=(jax.ShapeDtypeSt...  43.6 us
    pallas_call x1, Pallas kernels, tokens_behind(): pl.pallas_call(partial(behind_kernel, sizes, length), out_shape=(shape((4...  37 us
    pallas_call x1, Pallas kernels, weight_grads(): pl.pallas_call(weight_grad_kernel, grid=(2, experts // group, rows // d_b...  21 us
    pallas_call x1, Pallas kernels, tokens_ahead(): pl.pallas_call(partial(ahead_kernel, length), out_shape=(shape((sizes[1],...  14 us
  transfers between devices with their start and end apart: 3, of which 0 were waited for; matrix products, arithmetic and copies ran while one was open for 1% of the time, Pallas kernels for 21%

profile of v5, /device:TPU:0, one launch (start us, length us, event | category | flops | bytes accessed | tf_op | source)
XLA Modules:
  0.0 318.3 jit_solution(2037379169165539488)
XLA Ops:
  0.6 43.6 %gather_weights.1 = (bf16[4,768,768]{2,1,0:T(8,128)(2,1)}, bf16[768,256]{1,0:T(8,128)(2,1)}, bf16[2,16,192,1536]{3,2,1,0:T(8,128)(2,1)}, bf16[2,208,768]{2,1,0:T(8,128)(2,1)}, bf16[2,208,768]{2,1,0:T(8,128)(2,1)}) custom-call(bf16[4,96,192]{2,1,0:T(8,128)(2,1)} %w_attn.1, bf16[16,96]{1,0:T(8,128)(2,1)} %bitcast.16, bf16[16,96]{1,0:T(8,128)(2,1)} %out_bias.1, ...), custom_call_target="tpu_custom_call" | custom-call | tf_op jit(solution)/shard_map/gather_weights/pallas_call | solution.py:359
  44.3 14.0 %tokens_ahead.1 = (bf16[4,4,2,16,192]{4,3,2,1,0:T(8,128)(2,1)}, bf16[2,208,768]{2,1,0:T(8,128)(2,1)}, bf16[2,208,768]{2,1,0:T(8,128)(2,1)}, bf16[2,256,768]{2,1,...) custom-call(bf16[2,208,768]{2,1,0:T(8,128)(2,1)} %get-tuple-element., ...), custom_call_target="tpu_custom_call" | custom-call | tf_op jit(solution)/shard_map/tokens_ahead/pallas_call | solution.py:1200
  58.3 67.8 %experts_ahead.1 = (bf16[16,64,192]{2,1,0:T(8,128)(2,1)}, bf16[16,64,1536]{2,1,0:T(8,128)(2,1)}, f32[8,64,1536]{2,1,0:T(8,128)}, bf16[2,32,16,192]{3,2,1,0:T(8,128)(2,1)}) custom-call(bf16[4,4,2,16,192]{4,3,2,1,0:T(8,128)(2,1)} %get-tuple-element.54.refs_0_, bf16[2,16,192,1536]{3,2,1,0:T(8,128)(2,1)} %get-tuple-element.55.refs_1_, ...), custom_call_target="tpu_custom_call" | custom-call | flops 2415919104 | bytes 18874368 | tf_op jit(solution)/shard_map/experts_ahead/pallas_call | solution.py:937
  126.1 4.1 %tokens_middle.1 = (bf16[2,208,768]{2,1,0:T(8,128)(2,1)}, bf16[4,4,2,16,192]{4,3,2,1,0:T(8,128)(2,1)}, f32[2,208,64]{2,1,0:T(8,128)}) custom-call(bf16[2,32,16,192]{3,2,1,0:T(8,128)(2,1)} %get-tuple-element.56.back, bf16[768,256]{1,0:T(8,128)(2,1)} %get-tuple-element.52.small.refs_2_, f32[2,208,128]{2,1,0:T(8,128)} %get-tuple-element.57.combine, ...), custom_call_target="tpu_custom_call" | custom-call | tf_op jit(solution)/shard_map/tokens_middle/pallas_call | solution.py:1250
  130.1 75.4 %experts_back.1 = (bf16[16,64,192]{2,1,0:T(8,128)(2,1)}, bf16[16,64,1536]{2,1,0:T(8,128)(2,1)}, bf16[2,32,16,192]{3,2,1,0:T(8,128)(2,1)}, f32[16,384]{1,0:T(8,12...) custom-call(bf16[4,4,2,16,192]{4,3,2,1,0:T(8,128)(2,1)} %get-tuple-element.60.refs_0_, ...), custom_call_target="tpu_custom_call" | custom-call | flops 2415919104 | bytes 18874368 | tf_op jit(solution)/shard_map/experts_back/pallas_call | solution.py:937
  205.6 37.0 %tokens_behind.1 = (bf16[4,768,768]{2,1,0:T(8,128)(2,1)}, bf16[768,128]{1,0:T(8,128)(2,1)}, bf16[2,208,768]{2,1,0:T(8,128)(2,1)}) custom-call(bf16[2,32,16,192]{3,2,1,0:T(8,128)(2,1)} %get-tuple-element.63.back, bf16[768,256]{1,0:T(8,128)(2,1)} %get-tuple-element.52.small.refs_2_, bf16[4,768,768]{2,1,0:T(8,128)(2,1)} %get-tuple-element.53.w_hbm, ...), custom_call_target="tpu_custom_call" | custom-call | tf_op jit(solution)/shard_map/tokens_behind/pallas_call | solution.py:1364
  242.6 0.1 collective-permute-start
  242.6 1.1 collective-permute-start.1
  243.7 2.7 collective-permute-start.2
  246.5 0.0 copy-start.1
  246.5 21.0 %weight_grads.1 = f32[192,2,16,1536]{3,2,1,0:T(8,128)} custom-call(bf16[16,64,192]{2,1,0:T(8,128)(2,1)} %get-tuple-element.75.slots_0, bf16[16,64,1536]{2,1,0:T(8,128)(2,1)} %get-tuple-element.76.act_0, bf16[16,64,192]{2,1,0:T(8,128)(2,1)} %get-tuple-element.77.slots_1, bf16[16,64,1536]{2,1,0:T(8,128)(2,1)} %get-tuple-element.78.act_1), custom_call_target="tpu_custom_call" | custom-call | flops 1207959552 | bytes 37748736 | tf_op jit(solution)/shard_map/weight_grads/pallas_call | solution.py:1006
  267.5 0.0 copy-done.1
  267.5 0.2 slice_bitcast_fusion
  267.6 1.9 copy.18
  269.5 0.0 copy-start
  269.5 44.5 %reduce_grads.1.summed = f32[4,96,256]{2,1,0:T(8,128)} custom-call(bf16[4,768,768]{2,1,0:T(8,128)(2,1)} %get-tuple-element.82.grads, bf16[768,128]{1,0:T(8,128)(2,1)} %get-tuple-element.83.small), custom_call_target="tpu_custom_call" | custom-call | tf_op jit(solution)/shard_map/reduce_grads/pallas_call | solution.py:562
  314.0 1.8 unpack_grads.1
  315.9 0.0 collective-permute-done.refs_1_
  315.9 0.0 collective-permute-done.1.refs_2_
  315.9 0.0 collective-permute-done.2.refs_3_
  315.9 0.0 copy-done
  315.9 2.2 order_images.1
Async XLA Ops:
  242.6 73.3 %collective-permute-start = (bf16[2,208,768]{2,1,0:T(8,128)(2,1)}, bf16[2,208,768]{2,1,0:T(8,128)(2,1)S(1)}, u32[]{:S(2)}, u32[]{:S(2)}) collective-permute-start(bf16[2,208,768]{2,1,0:T(8,128)(2,1)} %get-tuple-element.81.refs_0_), channel_id=1, source_target_pairs={{0,2},{2,4},{4,6},{6,0},{1,3},{3,5},{5,7},{7,1},{8,10},{10,12},{12... | collective-permute-start | bytes 1916936 | tf_op jit(solution)/shard_map/ppermute | solution.py:1649
  242.6 73.2 %collective-permute-start.1 = (bf16[2,208,768]{2,1,0:T(8,128)(2,1)}, bf16[2,208,768]{2,1,0:T(8,128)(2,1)S(1)}, u32[]{:S(2)}, u32[]{:S(2)}) collective-permute-start(bf16[2,208,768]{2,1,0:T(8,128)(2,1)} %get-tuple-element.81.refs_0_), channel_id=1, source_target_pairs={{0,4},{2,6},{4,0},{6,2},{1,5},{3,7},{5,1},{7,3},{8,12},{10,14},{12... | collective-permute-start | bytes 1916936 | tf_op jit(solution)/shard_map/ppermute | solution.py:1649
  243.7 72.1 %collective-permute-start.2 = (bf16[2,208,768]{2,1,0:T(8,128)(2,1)}, bf16[2,208,768]{2,1,0:T(8,128)(2,1)S(1)}, u32[]{:S(2)}, u32[]{:S(2)}) collective-permute-start(bf16[2,208,768]{2,1,0:T(8,128)(2,1)} %get-tuple-element.81.refs_0_), channel_id=1, source_target_pairs={{0,6},{2,0},{4,2},{6,4},{1,7},{3,1},{5,3},{7,5},{8,14},{10,8},{12,... | collective-permute-start | bytes 1916936 | tf_op jit(solution)/shard_map/ppermute | solution.py:1649
  246.5 21.0 %copy-start.1 = (bf16[8,208,768]{2,1,0:T(8,128)(2,1)S(1)}, bf16[8,208,768]{2,1,0:T(8,128)(2,1)}, u32[]{:S(2)}) copy-start(bf16[8,208,768]{2,1,0:T(8,128)(2,1)} %get-tuple-element.79) | copy-start | bytes 7667716
  269.5 46.4 %copy-start = (bf16[2,208,768]{2,1,0:T(8,128)(2,1)S(1)}, bf16[2,208,768]{2,1,0:T(8,128)(2,1)}, u32[]{:S(2)}) copy-start(bf16[2,208,768]{2,1,0:T(8,128)(2,1)} %get-tuple-element.81.refs_0_) | copy-start | bytes 1916932
